TPU v7x, 32 devices: a whole 2x2x4 slice. The times are simulated.
32 devices in a mesh: ens: 2 (over x), tile: 16 (over z, y, core).
Axes of the slice: x: 2, y: 2, z: 4, core: 2. Of those that a mesh axis runs over, the one named last changes fastest.
Arguments:
- adjoint_in: float32 [16, 72, 256, 128], P('ens', None, 'tile'), parts along dimension 0, may hold values from -6 to 6
- east_courant: float32 [144, 256, 128], P('ens', 'tile'), parts along dimension 0, may hold values from -0.25 to 0.25
- north_courant: float32 [144, 256, 128], P('ens', 'tile'), parts along dimension 0, may hold values from -0.25 to 0.25
- level_mix: bfloat16 [72, 72], replicated, may hold values from -0.05 to 1, as said below
- avg_kernel: bfloat16 [144, 16384], P('ens', 'tile'), parts along dimension 0, may hold values from 0.19921875 to 1.796875
- pixel_weight: bfloat16 [16, 16384], P('ens', 'tile'), parts along dimension 0, may hold values from -6 to 6
- pixel_owner: int32 [16384, 2], P('tile', 'ens'), parts along dimension 1, may hold values from 0 to 15; in each aligned block of 1024 rows (0 to 1023, 1024 to 2047, ...) at most 256 rows name the same one
- pixel_column: int32 [2, 16384], P('ens', 'tile'), parts along dimension 0, may hold values from 0 to 2047
Outputs:
- adjoint_out: float32 [16, 72, 256, 128], P('ens', None, 'tile'), parts along dimension 0
There are 2 independent parts, one for each index of `ens`. A program takes and returns all parts, laid end to end along the dimension named above; an argument that names none is the same for every part. Nothing has to cross between parts.
Inputs may be any that keep to these rules, and one draw needn't show every extreme that they name: `pixel_owner`: of the 1024 pixels of one device, at most 256 name the same tile; in every draw some device sends exactly 256 to some tile. `level_mix`: diagonally dominant: each row's off-diagonal magnitudes sum to less than its diagonal entry, which lies in 0.6 to 1.
All inputs are finite; a program needn't handle non-finite values.
Results may differ from a plain program's by a relative error of at most 0.0052.
Values may be sent and summed in bfloat16 or wider, within the bound.
No kernel may reach another device: no remote copies, remote signals or barrier semaphores. Data moves between devices by JAX's collectives and lax.ppermute only.
A program may use at most 128 MiB of HBM per device.

v0:
```python
import math

import jax
import jax.numpy as jnp
from jax import lax
from jax.sharding import PartitionSpec as P

STEPS = 4


def shifted(value, axis, steps):
    count = lax.axis_size(axis)
    pairs = [(source, (source + steps) % count) for source in range(count)]
    return lax.ppermute(value, axis, pairs)


def with_halo(cells, sides, width):
    for axis, dim in sides:
        count = lax.axis_size(axis)
        head = lax.slice_in_dim(cells, 0, width, axis=dim)
        tail = lax.slice_in_dim(cells, cells.shape[dim] - width, cells.shape[dim], axis=dim)
        cells = jnp.concatenate(
            [
                lax.ppermute(tail, axis, [(i, (i + 1) % count) for i in range(count)]),
                cells,
                lax.ppermute(head, axis, [((i + 1) % count, i) for i in range(count)]),
            ],
            axis=dim,
        )
    return cells


def mix_levels(field, level_mix):
    return jnp.einsum(
        "lm,tlxy->tmxy", level_mix, field.astype(jnp.bfloat16), preferred_element_type=jnp.float32
    )


def transport(extended, east_face, west_face, north_face):
    centre = extended[:, :, 1:-1]
    east_value = extended[:, :, 2:]
    west_value = extended[:, :, :-2]
    zeros_row = jnp.zeros_like(centre[..., :1])
    north_value = jnp.concatenate([centre[..., 1:], zeros_row], axis=-1)
    south_value = jnp.concatenate([zeros_row, centre[..., :-1]], axis=-1)
    south_face = jnp.concatenate(
        [jnp.zeros_like(north_face[..., :1]), north_face[..., :-1]], axis=-1
    )
    result = centre + jnp.maximum(east_face, 0.0) * (east_value - centre)
    result = result + jnp.minimum(west_face, 0.0) * (centre - west_value)
    result = result + jnp.maximum(north_face, 0.0) * (north_value - centre)
    return result + jnp.minimum(south_face, 0.0) * (centre - south_value)


def per_device(
    adjoint_in,
    east_courant,
    north_courant,
    level_mix,
    avg_kernel,
    pixel_weight,
    pixel_owner,
    pixel_column,
):
    tracers, levels, lon_cells, lat_cells = adjoint_in.shape
    cols_dev = lon_cells * lat_cells
    pix_dev = avg_kernel.shape[1]
    tile_count = lax.axis_size("tile")
    capacity = 4 * pix_dev // tile_count
    slot_total = tile_count * capacity
    half_steps = STEPS // 2
    owner_tile = pixel_owner[:, 0]
    member = (owner_tile[:, None] == jnp.arange(tile_count, dtype=jnp.int32)[None, :]).astype(
        jnp.int32
    )
    position = jnp.sum((jnp.cumsum(member, axis=0) - 1) * member, axis=1)
    slot_index = owner_tile * capacity + position
    kernel_sent = (
        jnp.zeros((levels, slot_total), avg_kernel.dtype).at[:, slot_index].set(avg_kernel)
    )
    weight_sent = (
        jnp.zeros((tracers, slot_total), pixel_weight.dtype).at[:, slot_index].set(pixel_weight)
    )
    column_sent = jnp.full((slot_total,), -1, jnp.int32).at[slot_index].set(pixel_column[0])
    kernel_got, weight_got = (
        lax.all_to_all(kernel_sent, "tile", split_axis=1, concat_axis=1, tiled=True),
        lax.all_to_all(weight_sent, "tile", split_axis=1, concat_axis=1, tiled=True),
    )
    column_got = lax.all_to_all(column_sent, "tile", split_axis=0, concat_axis=0, tiled=True)
    latitude = jnp.arange(lat_cells, dtype=jnp.int32)
    north_face = north_courant * (latitude < lat_cells - 1).astype(jnp.float32)
    weighted = (
        weight_got.astype(jnp.float32)[:, None, :] * kernel_got.astype(jnp.float32)[None, :, :]
    ).astype(jnp.bfloat16)
    weighted = weighted.reshape(tracers * levels, slot_total)
    block_size = math.gcd(slot_total, 512)
    column_ids = jnp.arange(cols_dev, dtype=jnp.int32)

    def add_block(block_index, running):
        offset = block_index * block_size
        block_rows = lax.dynamic_slice_in_dim(weighted, offset, block_size, 1)
        block_cols = lax.dynamic_slice_in_dim(column_got, offset, block_size, 0)
        one_hot = (block_cols[:, None] == column_ids[None, :]).astype(jnp.bfloat16)
        return running + jnp.dot(block_rows, one_hot, preferred_element_type=jnp.float32)

    forcing = lax.fori_loop(
        0, slot_total // block_size, add_block, jnp.zeros((tracers * levels, cols_dev), jnp.float32)
    )
    forcing = forcing.reshape(tracers, levels, lon_cells, lat_cells)
    west_row = shifted(east_courant[:, -1:, :], "tile", 1)
    west_face = jnp.concatenate([west_row, east_courant[:, :-1, :]], axis=1)

    def half_window(field):
        for turn_index in range(half_steps):
            mixed_field = mix_levels(field, level_mix)
            extended = with_halo(mixed_field, (("tile", 2),), 1)
            field = transport(extended, east_courant, west_face, north_face)
        return field

    field = half_window(adjoint_in)
    field = field + forcing
    return half_window(field)


def solution(mesh):
    in_specs = (
        P("ens", None, "tile", None),
        P("ens", "tile", None),
        P("ens", "tile", None),
        P(),
        P("ens", "tile"),
        P("ens", "tile"),
        P("tile", "ens"),
        P("ens", "tile"),
    )
    out_specs = P("ens", None, "tile", None)
    return jax.shard_map(
        per_device, mesh=mesh, in_specs=in_specs, out_specs=out_specs, check_vma=False
    )
```

profile of v0, /device:TPU:0, one launch (start us, length us, event | category | flops | bytes accessed | tf_op | source)
XLA Modules:
  0.0 185.2 jit_solution(11118787736411997952)
XLA Ops:
  0.0 1.0 slice.100
  1.0 0.5 collective-permute-start.1
  1.5 0.7 fusion.68
  2.2 4.5 %reduce-window.6 = s32[16,8,128]{2,1,0:T(8,128)S(1)} reduce-window(s32[16,8,128]{2,1,0:T(8,128)S(1)} %fusion.68, s32[]{:T(128)} %constant.48.clone.1), window={size=1x1x128 pad=0_0x0_0x127_0}, to_apply=%region_0.0 | reduce-window | flops 2080768 | bytes 131076 | tf_op jit(solution)/shard_map/reduce-window
  6.7 0.1 slice.136
  6.8 0.1 copy.67
  7.0 0.1 add_add_fusion
  7.1 0.7 fusion.67
  7.8 0.7 compare_select_fusion
  8.5 0.9 copy.69
  9.4 3.5 %scatter_custom_fusion = bf16[8,4096]{0,1:T(8,128)(2,1)S(1)} fusion(s32[1024]{0:T(1024)S(1)} %bitcast.76, bf16[1024,8]{1,0:T(8,128)(2,1)S(1)} %copy.69, bf16[]{:T(256)} %constant.49.clone.1), kind=kCustom, calls=%fused_computation.69 | custom fusion | bytes 65538 | tf_op jit(solution)/shard_map/scatter | solution.py:82
  13.0 1.0 copy.70
  13.9 7.2 %all-to-all-start = ((bf16[8,16,256]{2,0,1:T(8,128)(2,1)}), bf16[8,16,256]{2,0,1:T(8,128)(2,1)S(1)}, u32[]{:S(2)}, u32[]{:S(2)}) async-start(bf16[8,16,256]{2,0,1:T(8,128)(2,1)} %copy.70), calls=%async_computation | async-start | bytes 131072 | tf_op jit(solution)/shard_map/all_to_all | solution.py:87
  21.2 2.7 %convert_element_type.54 = bf16[8,72,16,128]{3,2,1,0:T(8,128)(2,1)S(1)} convert(f32[8,72,16,128]{3,2,1,0:T(8,128)} %param.10) | non-fusion elementwise | flops 1179648 | bytes 7077888 | tf_op jit(solution)/shard_map/convert_element_type | solution.py:35
  23.9 0.8 fusion.59
  24.7 0.8 fusion.88
  25.5 4.4 %collective-permute-start = (f32[8,72,1,128]{3,1,2,0:T(8,128)}, f32[8,72,1,128]{3,1,2,0:T(8,128)}, u32[]{:S(2)}, u32[]{:S(2)}) collective-permute-start(f32[8,72,1,128]{3,1,2,0:T(8,128)} %get-tuple-element.141), channel_id=1, source_target_pairs={{1,0},{2,1},{3,2},{4,3},{5,4},{6,5},{7,6},{8,7},{9,8},{10,9},{11,1... | collective-permute-start | bytes 884744 | tf_op jit(solution)/shard_map/ppermute | solution.py:26
  29.9 5.2 %fusion.87 = (f32[8,72,16,127]{3,1,2,0:T(8,128)}, f32[8,72,16,127]{3,1,2,0:T(8,128)}) fusion(f32[8,72,16,128]{3,1,2,0:T(8,128)S(1)} %fusion.59), kind=kLoop, calls=%fused_computation.101 | loop fusion | bytes 18726912 | tf_op jit(solution)/shard_map/slice | solution.py:44
  35.2 0.9 broadcast_maximum_fusion
  36.1 0.2 pad_minimum_fusion
  36.4 0.8 copy.71
  37.2 0.2 copy.62
  37.4 4.0 %scatter_custom_fusion.1 = bf16[72,4096]{0,1:T(8,128)(2,1)S(1)} fusion(s32[1024]{0:T(1024)S(1)} %bitcast.77, bf16[1024,72]{1,0:T(8,128)(2,1)} %copy.71, bf16[]{:T(256)} %constant.49.clone.1), kind=kCustom, calls=%fused_computation.67 | custom fusion | bytes 590336 | tf_op jit(solution)/shard_map/scatter | solution.py:79
  41.4 1.2 copy.72
  42.6 1.3 copy.64
  43.9 0.2 copy.65
  44.1 5.0 %scatter_custom_fusion.2 = s32[4096]{0:T(1024)} fusion(s32[1024]{0:T(1024)S(1)} %bitcast.78, s32[1024]{0:T(1024)} %bitcast.79, s32[]{:T(128)} %constant.51.clone.1), kind=kCustom, calls=%fused_computation.86 | custom fusion | bytes 16896 | tf_op jit(solution)/shard_map/scatter | solution.py:84
  49.1 0.1 maximum_minimum_fusion
  49.2 0.2 copy.63
  49.4 5.8 %all-to-all-start.1 = ((bf16[72,16,256]{2,0,1:T(8,128)(2,1)}), bf16[72,16,256]{2,0,1:T(8,128)(2,1)S(1)}, u32[]{:S(2)}, u32[]{:S(2)}) async-start(bf16[72,16,256]{2,0,1:T(8,128)(2,1)} %copy.72), calls=%async_computation.1 | async-start | bytes 1179648 | tf_op jit(solution)/shard_map/all_to_all | solution.py:86
  55.3 9.8 %fusion.56 = f32[8,72,16,128]{3,1,2,0:T(8,128)S(1)} fusion(f32[8,72,16,128]{3,1,2,0:T(8,128)} %copy-done.2, f32[8,72,1,128]{3,1,2,0:T(8,128)} %collective-permute-done.2, f32[8,72,1,128]{3,1,2,0:T(8,128)} %collective-permute-done, f32[8,72,16,127]{3,1,2,0:T(8,128)} %get-tuple-element.140, f32[8,72,16,127]{3,1,2,0:T(8,128)} %get-tuple-element.139, ...), kind=kOutput, calls=%fused_computation.62 | convolution fusion | flops 187564032 | bytes 21760128 | tf_op jit(solution)/shard_map/lm,tlxy->tmxy/dot_general | solution.py:34
  65.2 0.8 fusion.86
  66.0 4.4 %collective-permute-start.3 = (f32[8,72,1,128]{3,1,2,0:T(8,128)}, f32[8,72,1,128]{3,1,2,0:T(8,128)}, u32[]{:S(2)}, u32[]{:S(2)}) collective-permute-start(f32[8,72,1,128]{3,1,2,0:T(8,128)} %get-tuple-element.137), channel_id=1, source_target_pairs={{1,0},{2,1},{3,2},{4,3},{5,4},{6,5},{7,6},{8,7},{9,8},{10,9},{11,1... | collective-permute-start | bytes 884744 | tf_op jit(solution)/shard_map/ppermute | solution.py:26
  70.4 5.2 %fusion.85 = (f32[8,72,16,127]{3,1,2,0:T(8,128)}, f32[8,72,16,127]{3,1,2,0:T(8,128)}) fusion(f32[8,72,16,128]{3,1,2,0:T(8,128)S(1)} %fusion.56), kind=kLoop, calls=%fused_computation.99 | loop fusion | bytes 18726912 | tf_op jit(solution)/shard_map/slice | solution.py:44
  75.6 5.8 %all-to-all-start.2 = ((s32[16,256,1]{1,2,0:T(1,128)}), s32[16,256,1]{1,2,0:T(1,128)S(1)}, u32[]{:S(2)}, u32[]{:S(2)}) async-start(s32[16,256,1]{1,2,0:T(1,128)} %bitcast.17), calls=%async_computation.2 | async-start | bytes 32768 | tf_op jit(solution)/shard_map/all_to_all | solution.py:89
  81.5 0.1 convert_bitcast_fusion
  81.5 0.1 copy.87
  81.7 3.0 %multiply_convert_fusion = bf16[8,72,4096]{2,1,0:T(8,128)(2,1)} fusion(f32[72,4096]{1,0:T(8,128)S(1)} %bitcast.62, f32[8,4096]{1,0:T(8,128)S(1)} %convert.2), kind=kLoop, calls=%fused_computation.10 | loop fusion | flops 4718592 | bytes 6029312 | tf_op jit(solution)/shard_map/convert_element_type | solution.py:94
  84.6 3.3 %all-to-all-done.2 = s32[16,256,1]{1,2,0:T(1,128)S(1)} async-done(((s32[16,256,1]{1,2,0:T(1,128)}), s32[16,256,1]{1,2,0:T(1,128)S(1)}, u32[]{:S(2)}, u32[]{:S(2)}) %all-to-all-start.2) | async-done | bytes 16416 | tf_op jit(solution)/shard_map/all_to_all | solution.py:89
  88.0 50.0 %while.14 = (s32[]{:T(128)}, f32[576,2048]{1,0:T(8,128)}, bf16[576,4096]{1,0:T(8,128)(2,1)}, s32[4096]{0:T(1024)S(1)}, s32[]{:T(128)}, /*index=5*/s32[]{:T(128)}, s32[]{:T(128)}, s32[]{:T(128)}) while((s32[]{:T(128)}, f32[576,2048]{1,0:T(8,128)}, bf16[576,4096]{1,0:T(8,128)(2,1)}, s32[4096]{0:T(1024)S(1)}, s32[]{:T(128)}, ...), condition=%wide.region_7.8_spmd.clone, body=%wide.region_6.7_spmd.clone.sunk | while | flops 1211367424 | bytes 10033309 | solution.py:106
  88.0 0.1 dynamic_slice.21
  88.0 4.9 %select_add_fusion.2 = f32[576,2048]{1,0:T(8,128)} fusion(f32[576,2048]{1,0:T(8,128)} %get-tuple-element.177, pred[]{:T(512)S(6)} %compare.12, s32[512]{0:T(512)S(1)} %dynamic_slice.21, bf16[576,4096]{1,0:T(8,128)(2,1)} %get-tuple-element.186, s32[]{:T(128)S(6)} %select_n.18), kind=kOutput, calls=%fused_computation.4.clone.1 | convolution fusion | flops 1211367424 | bytes 10029061 | tf_op jit(solution)/shard_map/while/body/eval_jaxpr/dot_general | solution.py:104
  93.0 6.4 %select_add_fusion.2 = f32[576,2048]{1,0:T(8,128)} fusion(f32[576,2048]{1,0:T(8,128)} %get-tuple-element.177, pred[]{:T(512)S(6)} %compare.12, s32[512]{0:T(512)S(1)} %dynamic_slice.21, bf16[576,4096]{1,0:T(8,128)(2,1)} %get-tuple-element.186, s32[]{:T(128)S(6)} %select_n.18), kind=kOutput, calls=%fused_computation.4.clone.1 | convolution fusion | flops 1211367424 | bytes 10029061 | tf_op jit(solution)/shard_map/while/body/eval_jaxpr/dot_general | solution.py:104
  99.4 6.4 %select_add_fusion.2 = f32[576,2048]{1,0:T(8,128)} fusion(f32[576,2048]{1,0:T(8,128)} %get-tuple-element.177, pred[]{:T(512)S(6)} %compare.12, s32[512]{0:T(512)S(1)} %dynamic_slice.21, bf16[576,4096]{1,0:T(8,128)(2,1)} %get-tuple-element.186, s32[]{:T(128)S(6)} %select_n.18), kind=kOutput, calls=%fused_computation.4.clone.1 | convolution fusion | flops 1211367424 | bytes 10029061 | tf_op jit(solution)/shard_map/while/body/eval_jaxpr/dot_general | solution.py:104
  105.8 6.4 %select_add_fusion.2 = f32[576,2048]{1,0:T(8,128)} fusion(f32[576,2048]{1,0:T(8,128)} %get-tuple-element.177, pred[]{:T(512)S(6)} %compare.12, s32[512]{0:T(512)S(1)} %dynamic_slice.21, bf16[576,4096]{1,0:T(8,128)(2,1)} %get-tuple-element.186, s32[]{:T(128)S(6)} %select_n.18), kind=kOutput, calls=%fused_computation.4.clone.1 | convolution fusion | flops 1211367424 | bytes 10029061 | tf_op jit(solution)/shard_map/while/body/eval_jaxpr/dot_general | solution.py:104
  112.3 6.3 %select_add_fusion.2 = f32[576,2048]{1,0:T(8,128)} fusion(f32[576,2048]{1,0:T(8,128)} %get-tuple-element.177, pred[]{:T(512)S(6)} %compare.12, s32[512]{0:T(512)S(1)} %dynamic_slice.21, bf16[576,4096]{1,0:T(8,128)(2,1)} %get-tuple-element.186, s32[]{:T(128)S(6)} %select_n.18), kind=kOutput, calls=%fused_computation.4.clone.1 | convolution fusion | flops 1211367424 | bytes 10029061 | tf_op jit(solution)/shard_map/while/body/eval_jaxpr/dot_general | solution.py:104
  118.7 6.4 %select_add_fusion.2 = f32[576,2048]{1,0:T(8,128)} fusion(f32[576,2048]{1,0:T(8,128)} %get-tuple-element.177, pred[]{:T(512)S(6)} %compare.12, s32[512]{0:T(512)S(1)} %dynamic_slice.21, bf16[576,4096]{1,0:T(8,128)(2,1)} %get-tuple-element.186, s32[]{:T(128)S(6)} %select_n.18), kind=kOutput, calls=%fused_computation.4.clone.1 | convolution fusion | flops 1211367424 | bytes 10029061 | tf_op jit(solution)/shard_map/while/body/eval_jaxpr/dot_general | solution.py:104
  125.1 6.3 %select_add_fusion.2 = f32[576,2048]{1,0:T(8,128)} fusion(f32[576,2048]{1,0:T(8,128)} %get-tuple-element.177, pred[]{:T(512)S(6)} %compare.12, s32[512]{0:T(512)S(1)} %dynamic_slice.21, bf16[576,4096]{1,0:T(8,128)(2,1)} %get-tuple-element.186, s32[]{:T(128)S(6)} %select_n.18), kind=kOutput, calls=%fused_computation.4.clone.1 | convolution fusion | flops 1211367424 | bytes 10029061 | tf_op jit(solution)/shard_map/while/body/eval_jaxpr/dot_general | solution.py:104
  131.6 6.4 %select_add_fusion.2 = f32[576,2048]{1,0:T(8,128)} fusion(f32[576,2048]{1,0:T(8,128)} %get-tuple-element.177, pred[]{:T(512)S(6)} %compare.12, s32[512]{0:T(512)S(1)} %dynamic_slice.21, bf16[576,4096]{1,0:T(8,128)(2,1)} %get-tuple-element.186, s32[]{:T(128)S(6)} %select_n.18), kind=kOutput, calls=%fused_computation.4.clone.1 | convolution fusion | flops 1211367424 | bytes 10029061 | tf_op jit(solution)/shard_map/while/body/eval_jaxpr/dot_general | solution.py:104
  137.9 3.4 %copy.89 = f32[72,8,16,128]{3,2,1,0:T(8,128)S(1)} copy(f32[72,8,16,128]{3,1,2,0:T(8,128)} %bitcast.59) | data formatting | bytes 9437184
  141.3 10.6 %fusion.50 = f32[8,72,16,128]{3,1,2,0:T(8,128)S(1)} fusion(f32[8,72,16,128]{3,1,2,0:T(8,128)} %copy-done.1, f32[8,72,1,128]{3,1,2,0:T(8,128)} %collective-permute-done.4, f32[8,72,1,128]{3,1,2,0:T(8,128)} %collective-permute-done.3, f32[8,72,16,128]{3,2,1,0:T(8,128)S(1)} %bitcast.60, f32[8,72,16,127]{3,1,2,0:T(8,128)} %get-tuple-element.136, ...), kind=kOutput, calls=%fused_computation.60 | convolution fusion | flops 188743680 | bytes 26478720 | tf_op jit(solution)/shard_map/lm,tlxy->tmxy/dot_general | solution.py:34
  152.0 1.1 collective-permute-start.5
  153.1 3.8 %fusion.83 = (f32[8,72,16,127]{3,1,2,0:T(8,128)S(1)}, f32[8,72,16,127]{3,1,2,0:T(8,128)}) fusion(f32[8,72,16,128]{3,1,2,0:T(8,128)S(1)} %fusion.50), kind=kLoop, calls=%fused_computation.97 | loop fusion | bytes 18726912 | tf_op jit(solution)/shard_map/slice | solution.py:44
  156.9 0.5 collective-permute-done.5
  157.4 4.6 %collective-permute-done.6 = f32[8,72,1,128]{3,1,2,0:T(8,128)S(1)} collective-permute-done((f32[8,72,1,128]{3,1,2,0:T(8,128)S(1)}, f32[8,72,1,128]{3,1,2,0:T(8,128)S(1)}, u32[]{:S(2)}, u32[]{:S(2)}) %collective-permute-start.6) | collective-permute-done | bytes 294944 | tf_op jit(solution)/shard_map/ppermute | solution.py:24
  162.0 5.9 %fusion.53 = f32[8,72,16,128]{3,1,2,0:T(8,128)S(1)} fusion(f32[8,72,16,128]{3,1,2,0:T(8,128)S(1)} %fusion.50, f32[8,72,1,128]{3,1,2,0:T(8,128)S(1)} %collective-permute-done.6, f32[8,72,1,128]{3,1,2,0:T(8,128)S(1)} %collective-permute-done.5, f32[8,72,16,127]{3,1,2,0:T(8,128)} %get-tuple-element.132, f32[8,72,16,127]{3,1,2,0:T(8,128)S(1)} %get-tuple-element.131, ...), kind=kOutput, calls=%fused_computation.61 | convolution fusion | flops 187564032 | bytes 21760128 | tf_op jit(solution)/shard_map/lm,tlxy->tmxy/dot_general | solution.py:34
  168.0 0.2 collective-permute-start.7
  168.1 0.4 collective-permute-start.8
  168.5 1.6 fusion.81
  170.1 2.3 %collective-permute-done.7 = f32[8,72,1,128]{3,1,2,0:T(8,128)S(1)} collective-permute-done((f32[8,72,1,128]{3,1,2,0:T(8,128)S(1)}, f32[8,72,1,128]{3,1,2,0:T(8,128)S(1)}, u32[]{:S(2)}, u32[]{:S(2)}) %collective-permute-start.7) | collective-permute-done | bytes 294944 | tf_op jit(solution)/shard_map/ppermute | solution.py:26
  172.4 4.8 %collective-permute-done.8 = f32[8,72,1,128]{3,1,2,0:T(8,128)S(1)} collective-permute-done((f32[8,72,1,128]{3,1,2,0:T(8,128)S(1)}, f32[8,72,1,128]{3,1,2,0:T(8,128)S(1)}, u32[]{:S(2)}, u32[]{:S(2)}) %collective-permute-start.8) | collective-permute-done | bytes 294944 | tf_op jit(solution)/shard_map/ppermute | solution.py:24
  177.1 0.7 copy-done.9
  177.9 4.3 %fusion.10 = f32[8,72,16,128]{3,1,2,0:T(8,128)S(1)} fusion(f32[8,72,16,128]{3,1,2,0:T(8,128)S(1)} %fusion.53, f32[8,72,1,128]{3,1,2,0:T(8,128)} %copy-done.9, f32[8,72,1,128]{3,1,2,0:T(8,128)S(1)} %collective-permute-done.7, f32[8,72,16,127]{3,1,2,0:T(8,128)S(1)} %get-tuple-element.128, f32[8,72,16,127]{3,1,2,0:T(8,128)S(1)} %get-tuple-element.127, ...), kind=kLoop, calls=%fused_computation.16 | loop fusion | flops 16515072 | bytes 21749760 | tf_op jit(solution)/shard_map/add | solution.py:52
  182.2 3.0 %copy.78 = f32[8,72,16,128]{3,2,1,0:T(8,128)} copy(f32[8,72,16,128]{3,1,2,0:T(8,128)S(1)} %fusion.10) | data formatting | bytes 9437184 | tf_op jit(solution)/shard_map/add | solution.py:52
  (47 shorter events, 0.8 us)
Async XLA Ops:
  0.0 23.9 %copy-start = (bf16[72,72]{1,0:T(8,128)(2,1)S(1)}, bf16[72,72]{1,0:T(8,128)(2,1)}, u32[]{:S(2)}) copy-start(bf16[72,72]{1,0:T(8,128)(2,1)} %param.13) | copy-start | bytes 31108
  1.0 48.1 %collective-permute-start.1 = (f32[72,1,128]{2,1,0:T(1,128)S(1)}, f32[72,1,128]{2,1,0:T(1,128)S(1)}, u32[]{:S(2)}, u32[]{:S(2)}) collective-permute-start(f32[72,1,128]{2,1,0:T(1,128)S(1)} %slice.100), channel_id=1, source_target_pairs={{0,1},{1,2},{2,3},{3,4},{4,5},{5,6},{6,7},{7,8},{8,9},{9,10},{10,1... | collective-permute-start | bytes 110600 | tf_op jit(solution)/shard_map/ppermute | solution.py:14
  13.9 35.5 %all-to-all-start = ((bf16[8,16,256]{2,0,1:T(8,128)(2,1)}), bf16[8,16,256]{2,0,1:T(8,128)(2,1)S(1)}, u32[]{:S(2)}, u32[]{:S(2)}) async-start(bf16[8,16,256]{2,0,1:T(8,128)(2,1)} %copy.70), calls=%async_computation | async-start | bytes 131072 | tf_op jit(solution)/shard_map/all_to_all | solution.py:87
  24.7 10.5 %copy-start.2 = (f32[8,72,16,128]{3,1,2,0:T(8,128)}, f32[8,72,16,128]{3,1,2,0:T(8,128)S(1)}, u32[]{:S(2)}) copy-start(f32[8,72,16,128]{3,1,2,0:T(8,128)S(1)} %fusion.59) | copy-start | bytes 14155780
  25.5 29.8 %collective-permute-start = (f32[8,72,1,128]{3,1,2,0:T(8,128)}, f32[8,72,1,128]{3,1,2,0:T(8,128)}, u32[]{:S(2)}, u32[]{:S(2)}) collective-permute-start(f32[8,72,1,128]{3,1,2,0:T(8,128)} %get-tuple-element.141), channel_id=1, source_target_pairs={{1,0},{2,1},{3,2},{4,3},{5,4},{6,5},{7,6},{8,7},{9,8},{10,9},{11,1... | collective-permute-start | bytes 884744 | tf_op jit(solution)/shard_map/ppermute | solution.py:26
  29.9 25.4 %collective-permute-start.2 = (f32[8,72,1,128]{3,1,2,0:T(8,128)S(1)}, f32[8,72,1,128]{3,1,2,0:T(8,128)}, u32[]{:S(2)}, u32[]{:S(2)}) collective-permute-start(f32[8,72,1,128]{3,1,2,0:T(8,128)S(1)} %get-tuple-element.142), channel_id=1, source_target_pairs={{0,1},{1,2},{2,3},{3,4},{4,5},{5,6},{6,7},{7,8},{8,9},{9,10},{10,1... | collective-permute-start | bytes 884744 | tf_op jit(solution)/shard_map/ppermute | solution.py:24
  29.9 5.3 %copy-start.8 = (f32[72,16,128]{2,1,0:T(8,128)S(1)}, f32[72,16,128]{2,1,0:T(8,128)}, u32[]{:S(2)}) copy-start(f32[72,16,128]{2,1,0:T(8,128)} %param.12) | copy-start | bytes 1769476
  29.9 6.2 %copy-start.7 = (f32[72,16,128]{2,1,0:T(8,128)S(1)}, f32[72,16,128]{2,1,0:T(8,128)}, u32[]{:S(2)}) copy-start(f32[72,16,128]{2,1,0:T(8,128)} %param.11) | copy-start | bytes 1769476
  29.9 6.4 %copy-start.10 = (bf16[72,1024]{1,0:T(8,128)(2,1)S(1)}, bf16[72,1024]{1,0:T(8,128)(2,1)}, u32[]{:S(2)}) copy-start(bf16[72,1024]{1,0:T(8,128)(2,1)} %param.14) | copy-start | bytes 442372
  37.4 124.6 %copy-start.3 = (f32[72,16,128]{2,0,1:T(8,128)}, f32[72,16,128]{2,0,1:T(8,128)S(1)}, u32[]{:S(2)}) copy-start(f32[72,16,128]{2,0,1:T(8,128)S(1)} %copy.62) | copy-start | bytes 1769476
  43.8 118.1 %copy-start.4 = (f32[72,16,128]{2,0,1:T(8,128)}, f32[72,16,128]{2,0,1:T(8,128)S(1)}, u32[]{:S(2)}) copy-start(f32[72,16,128]{2,0,1:T(8,128)S(1)} %copy.64) | copy-start | bytes 1769476
  44.1 117.9 %copy-start.5 = (f32[72,16,128]{2,0,1:T(8,128)}, f32[72,16,128]{2,0,1:T(8,128)S(1)}, u32[]{:S(2)}) copy-start(f32[72,16,128]{2,0,1:T(8,128)S(1)} %copy.65) | copy-start | bytes 1769476
  49.4 112.6 %copy-start.6 = (f32[72,16,128]{2,0,1:T(8,128)}, f32[72,16,128]{2,0,1:T(8,128)S(1)}, u32[]{:S(2)}) copy-start(f32[72,16,128]{2,0,1:T(8,128)S(1)} %copy.63) | copy-start | bytes 1769476
  49.4 26.2 %all-to-all-start.1 = ((bf16[72,16,256]{2,0,1:T(8,128)(2,1)}), bf16[72,16,256]{2,0,1:T(8,128)(2,1)S(1)}, u32[]{:S(2)}, u32[]{:S(2)}) async-start(bf16[72,16,256]{2,0,1:T(8,128)(2,1)} %copy.72), calls=%async_computation.1 | async-start | bytes 1179648 | tf_op jit(solution)/shard_map/all_to_all | solution.py:86
  65.2 5.2 %copy-start.1 = (f32[8,72,16,128]{3,1,2,0:T(8,128)}, f32[8,72,16,128]{3,1,2,0:T(8,128)S(1)}, u32[]{:S(2)}) copy-start(f32[8,72,16,128]{3,1,2,0:T(8,128)S(1)} %fusion.56) | copy-start | bytes 14155780
  66.0 75.3 %collective-permute-start.3 = (f32[8,72,1,128]{3,1,2,0:T(8,128)}, f32[8,72,1,128]{3,1,2,0:T(8,128)}, u32[]{:S(2)}, u32[]{:S(2)}) collective-permute-start(f32[8,72,1,128]{3,1,2,0:T(8,128)} %get-tuple-element.137), channel_id=1, source_target_pairs={{1,0},{2,1},{3,2},{4,3},{5,4},{6,5},{7,6},{8,7},{9,8},{10,9},{11,1... | collective-permute-start | bytes 884744 | tf_op jit(solution)/shard_map/ppermute | solution.py:26
  70.4 70.9 %collective-permute-start.4 = (f32[8,72,1,128]{3,1,2,0:T(8,128)S(1)}, f32[8,72,1,128]{3,1,2,0:T(8,128)}, u32[]{:S(2)}, u32[]{:S(2)}) collective-permute-start(f32[8,72,1,128]{3,1,2,0:T(8,128)S(1)} %get-tuple-element.138), channel_id=1, source_target_pairs={{0,1},{1,2},{2,3},{3,4},{4,5},{5,6},{6,7},{7,8},{8,9},{9,10},{10,1... | collective-permute-start | bytes 884744 | tf_op jit(solution)/shard_map/ppermute | solution.py:24
  75.6 12.3 %all-to-all-start.2 = ((s32[16,256,1]{1,2,0:T(1,128)}), s32[16,256,1]{1,2,0:T(1,128)S(1)}, u32[]{:S(2)}, u32[]{:S(2)}) async-start(s32[16,256,1]{1,2,0:T(1,128)} %bitcast.17), calls=%async_computation.2 | async-start | bytes 32768 | tf_op jit(solution)/shard_map/all_to_all | solution.py:89
  152.0 5.4 %collective-permute-start.5 = (f32[8,72,1,128]{3,1,2,0:T(8,128)S(1)}, f32[8,72,1,128]{3,1,2,0:T(8,128)S(1)}, u32[]{:S(2)}, u32[]{:S(2)}) collective-permute-start(f32[8,72,1,128]{3,1,2,0:T(8,128)S(1)} %get-tuple-element.133), channel_id=1, source_target_pairs={{1,0},{2,1},{3,2},{4,3},{5,4},{6,5},{7,6},{8,7},{9,8},{10,9},{11,1... | collective-permute-start | bytes 884744 | tf_op jit(solution)/shard_map/ppermute | solution.py:26
  153.1 8.8 %collective-permute-start.6 = (f32[8,72,1,128]{3,1,2,0:T(8,128)S(1)}, f32[8,72,1,128]{3,1,2,0:T(8,128)S(1)}, u32[]{:S(2)}, u32[]{:S(2)}) collective-permute-start(f32[8,72,1,128]{3,1,2,0:T(8,128)S(1)} %get-tuple-element.134), channel_id=1, source_target_pairs={{0,1},{1,2},{2,3},{3,4},{4,5},{5,6},{6,7},{7,8},{8,9},{9,10},{10,1... | collective-permute-start | bytes 884744 | tf_op jit(solution)/shard_map/ppermute | solution.py:24
  168.0 4.4 %collective-permute-start.7 = (f32[8,72,1,128]{3,1,2,0:T(8,128)S(1)}, f32[8,72,1,128]{3,1,2,0:T(8,128)S(1)}, u32[]{:S(2)}, u32[]{:S(2)}) collective-permute-start(f32[8,72,1,128]{3,1,2,0:T(8,128)S(1)} %get-tuple-element.129), channel_id=1, source_target_pairs={{1,0},{2,1},{3,2},{4,3},{5,4},{6,5},{7,6},{8,7},{9,8},{10,9},{11,1... | collective-permute-start | bytes 884744 | tf_op jit(solution)/shard_map/ppermute | solution.py:26
  168.1 9.0 %collective-permute-start.8 = (f32[8,72,1,128]{3,1,2,0:T(8,128)S(1)}, f32[8,72,1,128]{3,1,2,0:T(8,128)S(1)}, u32[]{:S(2)}, u32[]{:S(2)}) collective-permute-start(f32[8,72,1,128]{3,1,2,0:T(8,128)S(1)} %get-tuple-element.130), channel_id=1, source_target_pairs={{0,1},{1,2},{2,3},{3,4},{4,5},{5,6},{6,7},{7,8},{8,9},{9,10},{10,1... | collective-permute-start | bytes 884744 | tf_op jit(solution)/shard_map/ppermute | solution.py:24
  177.1 0.7 copy-start.9
where the time goes:
time: 186 us; the launch traced here: 185 us
  matrix products  76.5 us (41%)
  local copies, waits for them, and re-layouts  45 us (24%)
  starting transfers between devices  29.8 us (16%)
  other arithmetic  18.1 us (10%)
  waiting for transfers between devices  15.5 us (8%)
    dot_general x8, matrix products, add_block(): jnp.dot(block_rows, one_hot, preferred_element_type=jnp.float32)  49.3 us
    dot_general x4, matrix products, mix_levels(): jnp.einsum('lm,tlxy->tmxy', level_mix, field.astype(jnp.bfloat16), prefer...  27.2 us
    slice x4, local copies, waits for them, and re-layouts, transport(): north_value = jnp.concatenate([centre[..., 1:], zeros_row], axis=-1)  15.8 us
    ppermute x4, starting transfers between devices, with_halo(): lax.ppermute(head, axis, [((i + 1) % count, i) for i in range(count)])  10 us
    ppermute x4, waiting for transfers between devices, with_halo(): lax.ppermute(tail, axis, [(i, (i + 1) % count) for i in range(count)])  9.38 us
    all_to_all x1, starting transfers between devices, per_device(): lax.all_to_all(weight_sent, 'tile', split_axis=1, concat_axis=1, tiled=True)  7.22 us
    unnamed x25, local copies, waits for them, and re-layouts  5.87 us
    all_to_all x1, starting transfers between devices, per_device(): lax.all_to_all(kernel_sent, 'tile', split_axis=1, concat_axis=1, tiled=True)  5.82 us
  transfers between devices with their start and end apart: 12, of which 5 were waited for; matrix products, arithmetic and copies ran while one was open for 61% of the time, Pallas kernels for 0%

commit v1 on v0

v1 whole, which is shorter than its diff:
```python
import functools

import jax
import jax.numpy as jnp
from jax import lax
from jax.experimental import pallas as pl
from jax.experimental.pallas import tpu as pltpu
from jax.sharding import PartitionSpec as P

F32 = jnp.float32
BF16 = jnp.bfloat16
GROUP = 2
HALO = 2
VMEM = 56 * 1024 * 1024


def params(**more):
    return pltpu.CompilerParams(vmem_limit_bytes=VMEM, **more)


def nt_dot(a, b):
    return lax.dot_general(a, b, (((1,), (1,)), ((), ())), preferred_element_type=F32)


def rows16(row):
    return jnp.broadcast_to(row, (16, row.shape[1])).astype(BF16)


def stacked(block, count):
    return jnp.concatenate([block] * count, axis=0)


def pack_kernel(kernel_ref, weight_ref, owner_ref, column_ref, out_ref, *, tiles, capacity, lat):
    levels, pixels = kernel_ref.shape
    column = column_ref[...]
    lon_row = (column // lat).astype(F32)
    lat_row = (column % lat).astype(F32)
    line = lax.broadcasted_iota(jnp.int32, (8, pixels), 0)
    place = jnp.where(line == 0, lon_row, jnp.where(line == 1, lat_row, 0.0))
    payload = jnp.concatenate(
        [kernel_ref[...].astype(F32), weight_ref[...].astype(F32), place], axis=0
    ).astype(BF16)
    owner = owner_ref[...]
    block = min(256, pixels)
    upto = (
        lax.broadcasted_iota(jnp.int32, (block, block), 0)
        <= lax.broadcasted_iota(jnp.int32, (block, block), 1)
    ).astype(F32).astype(BF16)
    carry = jnp.zeros((tiles, 1), F32)
    ranks = []
    for start in range(0, pixels, block):
        named = owner[:, start : start + block] == lax.broadcasted_iota(
            jnp.int32, (tiles, block), 0
        )
        counts = (
            jnp.dot(named.astype(F32).astype(BF16), upto, preferred_element_type=F32) + carry
        )
        carry = counts[:, block - 1 : block]
        ranks.append(jnp.where(named, counts - 1.0, -1.0))
    ranks = jnp.concatenate(ranks, axis=1)
    slot = lax.broadcasted_iota(jnp.int32, (capacity, pixels), 0).astype(F32).astype(BF16)
    for tile in range(tiles):
        rank = stacked(rows16(ranks[tile : tile + 1, :]), capacity // 16)
        chosen = jnp.where(slot == rank, jnp.ones_like(slot), jnp.zeros_like(slot))
        out_ref[tile] = nt_dot(payload, chosen).astype(BF16)


def edge_kernel(field_ref, east_ref, north_ref, fwd_ref, bwd_ref, *, lon, levels):
    step = pl.program_id(0)
    rows = field_ref.shape[0] // lon
    total = rows * pl.num_programs(0)

    def column(ref, x, count):
        return ref[pl.ds(x, count, stride=lon), :].astype(BF16)

    for c in range(HALO):
        at = pl.ds(pl.multiple_of(c * total + step * rows, 16), rows)
        fwd_ref[at, :] = column(field_ref, lon - HALO + c, rows)
        bwd_ref[at, :] = column(field_ref, c, rows)

    @pl.when(step == 0)
    def _():
        def put(out, place, ref, x):
            spot = HALO * total + place * (levels + 8)
            value = ref[pl.ds(x, levels, stride=lon), :]
            value = jnp.concatenate([value, jnp.zeros((8, value.shape[1]), F32)], axis=0)
            out[spot : spot + levels + 8, :] = value.astype(BF16)

        put(fwd_ref, 0, east_ref, lon - 2)
        put(fwd_ref, 1, east_ref, lon - 1)
        put(fwd_ref, 2, north_ref, lon - 1)
        put(bwd_ref, 0, east_ref, 0)
        put(bwd_ref, 1, north_ref, 0)


def fill_coefs(east_ref, north_ref, fwd_ref, bwd_ref, coef_ref, lon, levels, total):
    lat = east_ref.shape[1]
    base = HALO * total

    def far(ref, place):
        spot = base + place * (levels + 8)
        return ref[spot : spot + levels + 8, :].astype(F32)[:levels]

    def own(ref, x):
        return ref[pl.ds(x, levels, stride=lon), :]

    def east(e):
        if e < HALO:
            return far(fwd_ref, e)
        return own(east_ref, e - HALO) if e < lon + HALO else far(bwd_ref, 0)

    def north(e):
        if e < HALO:
            return far(fwd_ref, 2)
        return own(north_ref, e - HALO) if e < lon + HALO else far(bwd_ref, 1)

    lane = lax.broadcasted_iota(jnp.int32, (levels, lat), 1)
    for e in range(1, lon + 2 * HALO - 1):
        at = slice(e * lat, (e + 1) * lat)
        face = jnp.where(lane < lat - 1, north(e), 0.0)
        to_east = jnp.maximum(east(e), 0.0)
        to_west = jnp.minimum(east(e - 1), 0.0)
        to_north = jnp.maximum(face, 0.0)
        to_south = pltpu.roll(jnp.minimum(face, 0.0), 1, 1)
        coef_ref[0, :, at] = (1.0 - to_east) + to_west + (to_south - to_north)
        coef_ref[1, :, at] = to_east
        coef_ref[2, :, at] = -to_west
        coef_ref[3, :, at] = to_north
        coef_ref[4, :, at] = -to_south


def stencil(mixed_ref, coef_ref, e, lat, levels, emit):
    rows = mixed_ref.shape[0]
    here = pl.ds(pl.multiple_of(e * lat, lat), lat)
    right = pl.ds(pl.multiple_of(e * lat + lat, lat), lat)
    left = pl.ds(pl.multiple_of(e * lat - lat, lat), lat)
    for k in range(0, rows, levels):
        part = slice(k, k + levels)
        centre = mixed_ref[part, here]
        value = coef_ref[0, :, here] * centre
        value = value + coef_ref[1, :, here] * mixed_ref[part, right]
        value = value + coef_ref[2, :, here] * mixed_ref[part, left]
        value = value + coef_ref[3, :, here] * pltpu.roll(centre, lat - 1, 1)
        value = value + coef_ref[4, :, here] * pltpu.roll(centre, 1, 1)
        emit(k, value)


def two_steps(mix_ref, field_ref, mixed_ref, hold_ref, coef_ref, lon, lat, levels, put):
    whole = lon + 2 * HALO
    mixed_ref[...] = jnp.dot(mix_ref[...], field_ref[...], preferred_element_type=F32)

    def first(e, carry):
        here = pl.ds(pl.multiple_of(e * lat, lat), lat)

        def emit(k, value):
            hold_ref[k : k + levels, :] = value

        stencil(mixed_ref, coef_ref, e, lat, levels, emit)
        field_ref[:, here] = hold_ref[...].astype(BF16)
        return carry

    lax.fori_loop(1, whole - 1, first, 0)
    inner = slice(lat, (whole - 1) * lat)
    mixed_ref[:, inner] = jnp.dot(mix_ref[...], field_ref[:, inner], preferred_element_type=F32)

    def second(e, carry):
        stencil(mixed_ref, coef_ref, e, lat, levels, functools.partial(put, e))
        return carry

    lax.fori_loop(HALO, whole - HALO, second, 0)


def first_half_kernel(
    mix_ref, east_ref, north_ref, fwd_ref, bwd_ref, in_ref, out_ref,
    coef_ref, field_ref, mixed_ref, hold_ref, *, lon, levels, total,
):
    step = pl.program_id(0)
    lat = in_ref.shape[1]
    rows = in_ref.shape[0] // lon

    @pl.when(step == 0)
    def _():
        fill_coefs(east_ref, north_ref, fwd_ref, bwd_ref, coef_ref, lon, levels, total)

    for c in range(HALO):
        at = pl.ds(pl.multiple_of(c * total + step * rows, 16), rows)
        field_ref[:, c * lat : (c + 1) * lat] = fwd_ref[at, :]
        e = lon + HALO + c
        field_ref[:, e * lat : (e + 1) * lat] = bwd_ref[at, :]
    for x in range(lon):
        value = in_ref[pl.ds(x, rows, stride=lon), :]
        field_ref[:, (x + HALO) * lat : (x + HALO + 1) * lat] = value.astype(BF16)

    def put(e, k, value):
        out_ref[k : k + levels, pl.ds(pl.multiple_of((e - HALO) * lat, lat), lat)] = value

    two_steps(mix_ref, field_ref, mixed_ref, hold_ref, coef_ref, lon, lat, levels, put)


def second_half_kernel(
    mix_ref, east_ref, north_ref, fwd_ref, bwd_ref, far_w_ref, own_w_ref, inner_ref, own_e_ref,
    far_e_ref, out_ref, coef_ref, field_ref, mixed_ref, hold_ref, *, lon, levels, total,
):
    lat = out_ref.shape[1]
    rows = out_ref.shape[0] // lon

    @pl.when(pl.program_id(0) == 0)
    def _():
        fill_coefs(east_ref, north_ref, fwd_ref, bwd_ref, coef_ref, lon, levels, total)

    spot = 0
    for ref in (far_w_ref, own_w_ref, inner_ref, own_e_ref, far_e_ref):
        width = ref.shape[-1]
        field_ref[:, spot : spot + width] = ref[...]
        spot = spot + width

    def put(e, k, value):
        out_ref[pl.ds(k * lon + e - HALO, levels, stride=lon), :] = value

    two_steps(mix_ref, field_ref, mixed_ref, hold_ref, coef_ref, lon, lat, levels, put)


def forcing_kernel(got_ref, field_ref, out_ref, weighted_ref, place_ref, *, lat, levels, tracers, pair):
    tiles, _, capacity = got_ref.shape
    step = pl.program_id(0)

    @pl.when(step == 0)
    def _():
        for tile in range(tiles):
            at = slice(tile * capacity, (tile + 1) * capacity)
            got = got_ref[tile].astype(F32)
            kernel = got[:levels]
            for t in range(0, tracers, GROUP):
                parts = [
                    kernel * got[levels + j : levels + j + 1, :] for j in range(t, t + GROUP)
                ]
                weighted_ref[t * levels : (t + GROUP) * levels, at] = jnp.concatenate(
                    parts, axis=0
                ).astype(BF16)
            spot = levels + tracers
            column = got[spot : spot + 1, :] * lat + got[spot + 1 : spot + 2, :]
            place_ref[:, at] = jnp.broadcast_to(column, (8, capacity))

    cells = field_ref.shape[1]
    slots = tiles * capacity
    offset = (pair(step) * cells).astype(F32)
    key = rows16(place_ref[0:1, :] - offset)
    cell = lax.broadcasted_iota(jnp.int32, (cells, slots), 0).astype(F32).astype(BF16)
    hit = cell == stacked(key, cells // 16)
    one_hot = jnp.where(hit, jnp.ones_like(cell), jnp.zeros_like(cell))
    total = nt_dot(weighted_ref[...], one_hot)
    out_ref[...] = (field_ref[...] + total).astype(BF16)


def per_device(
    adjoint_in,
    east_courant,
    north_courant,
    level_mix,
    avg_kernel,
    pixel_weight,
    pixel_owner,
    pixel_column,
):
    tracers, levels, lon, lat = adjoint_in.shape
    pixels = avg_kernel.shape[1]
    tiles = lax.axis_size("tile")
    capacity = 4 * pixels // tiles
    slots = tiles * capacity
    total = tracers * levels
    steps = tracers // GROUP
    rows = GROUP * levels
    ring = [(i, (i + 1) % tiles) for i in range(tiles)]
    back = [((i + 1) % tiles, i) for i in range(tiles)]

    field = adjoint_in.reshape(total * lon, lat)
    east = east_courant.reshape(levels * lon, lat)
    north = north_courant.reshape(levels * lon, lat)
    mix = jnp.kron(jnp.eye(GROUP, dtype=BF16), level_mix.T)

    height = levels + tracers + 8
    payload = pl.pallas_call(
        functools.partial(pack_kernel, tiles=tiles, capacity=capacity, lat=lat),
        out_shape=jax.ShapeDtypeStruct((tiles, height, capacity), BF16),
        compiler_params=params(),
        name="pack",
    )(avg_kernel, pixel_weight, pixel_owner.reshape(1, pixels), pixel_column)
    got = lax.all_to_all(payload, "tile", split_axis=0, concat_axis=0, tiled=True)

    fwd_rows = HALO * total + 3 * (levels + 8)
    bwd_rows = HALO * total + 2 * (levels + 8)
    whole = lambda *shape: pl.BlockSpec(shape, lambda i: (0,) * len(shape))
    fwd, bwd = pl.pallas_call(
        functools.partial(edge_kernel, lon=lon, levels=levels),
        grid=(steps,),
        in_specs=[
            pl.BlockSpec((rows * lon, lat), lambda i: (i, 0)),
            whole(levels * lon, lat),
            whole(levels * lon, lat),
        ],
        out_specs=[whole(fwd_rows, lat), whole(bwd_rows, lat)],
        out_shape=[
            jax.ShapeDtypeStruct((fwd_rows, lat), BF16),
            jax.ShapeDtypeStruct((bwd_rows, lat), BF16),
        ],
        compiler_params=params(),
        name="edges",
    )(field, east, north)
    fwd = lax.ppermute(fwd, "tile", ring)
    bwd = lax.ppermute(bwd, "tile", back)

    span = (lon + 2 * HALO) * lat
    scratch = [
        pltpu.VMEM((5, levels, span), F32),
        pltpu.VMEM((rows, span), BF16),
        pltpu.VMEM((rows, span), F32),
        pltpu.VMEM((rows, lat), F32),
    ]
    common_specs = [
        whole(rows, rows),
        whole(levels * lon, lat),
        whole(levels * lon, lat),
        whole(fwd_rows, lat),
        whole(bwd_rows, lat),
    ]
    middle = pl.pallas_call(
        functools.partial(first_half_kernel, lon=lon, levels=levels, total=total),
        grid=(steps,),
        in_specs=common_specs + [pl.BlockSpec((rows * lon, lat), lambda i: (i, 0))],
        out_specs=pl.BlockSpec((rows, lon * lat), lambda i: (i, 0)),
        out_shape=jax.ShapeDtypeStruct((total, lon * lat), F32),
        scratch_shapes=scratch,
        compiler_params=params(),
        name="first_half",
    )(mix, east, north, fwd, bwd, field)

    cells = HALO * lat
    pairs = lon // HALO

    def forced(name, count, pair):
        return pl.pallas_call(
            functools.partial(
                forcing_kernel, lat=lat, levels=levels, tracers=tracers, pair=pair
            ),
            grid=(count,),
            in_specs=[
                whole(tiles, height, capacity),
                pl.BlockSpec((total, cells), lambda i: (0, pair(i))),
            ],
            out_specs=pl.BlockSpec((total, cells), lambda i: (0, i)),
            out_shape=jax.ShapeDtypeStruct((total, count * cells), BF16),
            scratch_shapes=[pltpu.VMEM((total, slots), BF16), pltpu.VMEM((8, slots), F32)],
            compiler_params=params(),
            name=name,
        )(got, middle)

    rim = forced("forcing_rim", 2, lambda i: i * (pairs - 1))
    own_w, own_e = rim[:, :cells], rim[:, cells:]
    far_w = lax.ppermute(own_e, "tile", ring)
    far_e = lax.ppermute(own_w, "tile", back)
    inner = forced("forcing_inner", pairs - 2, lambda i: i + 1)

    strip = lambda width: pl.BlockSpec((rows, width), lambda i: (i, 0))
    out = pl.pallas_call(
        functools.partial(second_half_kernel, lon=lon, levels=levels, total=total),
        grid=(steps,),
        in_specs=common_specs
        + [strip(cells), strip(cells), strip((pairs - 2) * cells), strip(cells), strip(cells)],
        out_specs=pl.BlockSpec((rows * lon, lat), lambda i: (i, 0)),
        out_shape=jax.ShapeDtypeStruct((total * lon, lat), F32),
        scratch_shapes=scratch,
        compiler_params=params(),
        name="second_half",
    )(mix, east, north, fwd, bwd, far_w, own_w, inner, own_e, far_e)
    return out.reshape(tracers, levels, lon, lat)


def solution(mesh):
    in_specs = (
        P("ens", None, "tile", None),
        P("ens", "tile", None),
        P("ens", "tile", None),
        P(),
        P("ens", "tile"),
        P("ens", "tile"),
        P("tile", "ens"),
        P("ens", "tile"),
    )
    out_specs = P("ens", None, "tile", None)
    return jax.shard_map(
        per_device, mesh=mesh, in_specs=in_specs, out_specs=out_specs, check_vma=False
    )
```

time: 186 us -> 105 us (0.56)
  the two profiles are of different devices: /device:TPU:0 before, /device:TPU:13 now
where the time goes in v1:
time: 105 us
  Pallas kernels  73.7 us (70%)
  waiting for transfers between devices  14.6 us (14%)
  starting transfers between devices  10.7 us (10%)
  local copies, waits for them, and re-layouts  5.69 us (5%)
    pallas_call x1, Pallas kernels, per_device(): pl.pallas_call(functools.partial(first_half_kernel, lon=lon, levels=level...  24 us
    pallas_call x1, Pallas kernels, per_device(): pl.pallas_call(functools.partial(second_half_kernel, lon=lon, levels=leve...  23.5 us
    pallas_call x2, Pallas kernels, forced(): pl.pallas_call(functools.partial(forcing_kernel, lat=lat, levels=levels,...  17.1 us
    ppermute x1, waiting for transfers between devices, per_device(): bwd = lax.ppermute(bwd, 'tile', back)  14.6 us
    all_to_all x1, starting transfers between devices, per_device(): lax.all_to_all(payload, 'tile', split_axis=0, concat_axis=0, tiled=True)  6.56 us
    pallas_call x1, Pallas kernels, per_device(): pl.pallas_call(functools.partial(pack_kernel, tiles=tiles, capacity=capac...  4.63 us
    pallas_call x1, Pallas kernels, per_device(): pl.pallas_call(functools.partial(edge_kernel, lon=lon, levels=levels), gr...  4.46 us
    unnamed x16, local copies, waits for them, and re-layouts  3.77 us
  transfers between devices with their start and end apart: 5, of which 1 were waited for; matrix products, arithmetic and copies ran while one was open for 1% of the time, Pallas kernels for 38%

profile of v1, /device:TPU:13, one launch (start us, length us, event | category | flops | bytes accessed | tf_op | source)
XLA Modules:
  0.0 104.9 jit_solution(8079729630020805520)
XLA Ops:
  0.0 0.0 copy-start.7
  0.0 4.6 %pack.1 = bf16[16,88,256]{2,1,0:T(8,128)(2,1)} custom-call(bf16[72,1024]{1,0:T(8,128)(2,1)} %kernel_ref.1, bf16[8,1024]{1,0:T(8,128)(2,1)} %weight_ref.1, s32[1,1024]{1,0:T(1,128)} %bitcast.15, s32[1,1024]{1,0:T(1,128)} %column_ref.1), custom_call_target="tpu_custom_call" | custom-call | tf_op jit(solution)/shard_map/pack/pallas_call | solution.py:282
  4.6 6.6 %all-to-all-start = ((bf16[16,88,256]{2,1,0:T(8,128)(2,1)}), bf16[16,88,256]{2,1,0:T(8,128)(2,1)S(1)}, u32[]{:S(2)}, u32[]{:S(2)}) async-start(bf16[16,88,256]{2,1,0:T(8,128)(2,1)} %pack.1), calls=%async_computation | async-start | bytes 1441792 | tf_op jit(solution)/shard_map/all_to_all | solution.py:288
  11.2 4.5 %edges.1 = (bf16[1392,128]{1,0:T(8,128)(2,1)}, bf16[1312,128]{1,0:T(8,128)(2,1)}) custom-call(f32[9216,128]{1,0:T(8,128)} %bitcast.6, f32[1152,128]{1,0:T(8,128)} %bitcast.8, f32[1152,128]{1,0:T(8,128)} %bitcast.11), custom_call_target="tpu_custom_call" | custom-call | tf_op jit(solution)/shard_map/edges/pallas_call | solution.py:293
  15.6 1.4 %collective-permute-start = (bf16[1392,128]{1,0:T(8,128)(2,1)}, bf16[1392,128]{1,0:T(8,128)(2,1)S(1)}, u32[]{:S(2)}, u32[]{:S(2)}) collective-permute-start(bf16[1392,128]{1,0:T(8,128)(2,1)} %get-tuple-element.7), channel_id=1, source_target_pairs={{0,1},{1,2},{2,3},{3,4},{4,5},{5,6},{6,7},{7,8},{8,9},{9,10},{10,1... | collective-permute-start | bytes 1069064 | tf_op jit(solution)/shard_map/ppermute | solution.py:309
  17.1 0.0 collective-permute-start.1
  17.1 0.0 copy-done.7
  17.1 0.1 copy.9
  17.2 0.1 broadcast_multiply_fusion
  17.3 0.7 mul.27.mix_ref
  18.1 14.6 %collective-permute-done.1.bwd_ref = bf16[1312,128]{1,0:T(8,128)(2,1)S(1)} collective-permute-done((bf16[1312,128]{1,0:T(8,128)(2,1)}, bf16[1312,128]{1,0:T(8,128)(2,1)S(1)}, u32[]{:S(2)}, u32[]{:S(2)}) %collective-permute-start.1) | collective-permute-done | bytes 335904 | tf_op jit(solution)/shard_map/ppermute | solution.py:310
  32.7 0.0 copy-start.2
  32.7 0.0 collective-permute-done.fwd_ref
  32.7 0.7 copy-done.2
  33.4 0.0 copy-start.1
  33.4 0.7 copy-done.1
  34.1 24.0 %first_half.1.field_ref = f32[576,2048]{1,0:T(8,128)} custom-call(bf16[144,144]{1,0:T(8,128)(2,1)} %mul.27.mix_ref, f32[1152,128]{1,0:T(8,128)} %bitcast.9, f32[1152,128]{1,0:T(8,128)} %bitcast.12, bf16[1392,128]{1,0:T(8,128)(2,1)} %copy-done.1, bf16[1312,128]{1,0:T(8,128)(2,1)} %copy-done.2, f32[9216,128]{1,0:T(8,128)} %bitcast.7), custom_call_target="tpu_custom_call" | custom-call | tf_op jit(solution)/shard_map/first_half/pallas_call | solution.py:326
  58.2 0.0 all-to-all-done.got_ref
  58.2 0.0 copy-start
  58.2 0.9 copy-done
  59.0 5.6 %forcing_rim.1 = bf16[576,512]{1,0:T(8,128)(2,1)} custom-call(bf16[16,88,256]{2,1,0:T(8,128)(2,1)} %copy-done, f32[576,2048]{1,0:T(8,128)} %first_half.1.field_ref), custom_call_target="tpu_custom_call" | custom-call | tf_op jit(solution)/shard_map/forcing_rim/pallas_call | solution.py:341
  64.7 1.1 %fusion = (bf16[576,256]{1,0:T(8,128)(2,1)S(1)}, bf16[576,256]{1,0:T(8,128)(2,1)S(1)}) fusion(bf16[576,512]{1,0:T(8,128)(2,1)} %forcing_rim.1), kind=kLoop, calls=%fused_computation.2 | loop fusion | bytes 1179648 | tf_op jit(solution)/shard_map/slice | solution.py:358
  65.7 0.0 copy-start.3
  65.8 0.0 copy-start.4
  65.8 0.1 collective-permute-start.3
  65.8 2.6 %collective-permute-start.2 = (bf16[576,256]{1,0:T(8,128)(2,1)S(1)}, bf16[576,256]{1,0:T(8,128)(2,1)S(1)}, u32[]{:S(2)}, u32[]{:S(2)}) collective-permute-start(bf16[576,256]{1,0:T(8,128)(2,1)S(1)} %get-tuple-element.10.own_e_ref), channel_id=1, source_target_pairs={{0,1},{1,2},{2,3},{3,4},{4,5},{5,6},{6,7},{7,8},{8,9},{9,10},{10,1... | collective-permute-start | bytes 884744 | tf_op jit(solution)/shard_map/ppermute | solution.py:359
  68.5 11.5 %forcing_inner.1.inner_ref = bf16[576,1536]{1,0:T(8,128)(2,1)} custom-call(bf16[16,88,256]{2,1,0:T(8,128)(2,1)} %copy-done, f32[576,2048]{1,0:T(8,128)} %first_half.1.field_ref), custom_call_target="tpu_custom_call" | custom-call | tf_op jit(solution)/shard_map/forcing_inner/pallas_call | solution.py:341
  79.9 0.0 collective-permute-done.3.far_e_ref
  79.9 0.0 copy-start.5
  80.0 0.0 collective-permute-done.2.far_w_ref
  80.0 0.0 copy-done.3
  80.0 0.0 copy-done.4
  80.0 0.7 copy-done.5
  80.7 0.0 copy-start.6
  80.7 0.7 copy-done.6
  81.4 23.5 %second_half.1 = f32[9216,128]{1,0:T(8,128)} custom-call(bf16[144,144]{1,0:T(8,128)(2,1)} %mul.27.mix_ref, f32[1152,128]{1,0:T(8,128)} %bitcast.10, f32[1152,128]{1,0:T(8,128)} %bitcast.13, bf16[1392,128]{1,0:T(8,128)(2,1)} %copy-done.1, bf16[1312,128]{1,0:T(8,128)(2,1)} %copy-done.2, bf16[576,256]{1,0:T(8,128)(2,1)} %copy-done.6, ...), custom_call_target="tpu_custom_call" | custom-call | tf_op jit(solution)/shard_map/second_half/pallas_call | solution.py:364
  (1 shorter events, 0.0 us)
Async XLA Ops:
  0.0 17.1 %copy-start.7 = (bf16[72,72]{1,0:T(8,128)(2,1)S(1)}, bf16[72,72]{1,0:T(8,128)(2,1)}, u32[]{:S(2)}) copy-start(bf16[72,72]{1,0:T(8,128)(2,1)} %param.11) | copy-start | bytes 31108
  4.6 53.5 %all-to-all-start = ((bf16[16,88,256]{2,1,0:T(8,128)(2,1)}), bf16[16,88,256]{2,1,0:T(8,128)(2,1)S(1)}, u32[]{:S(2)}, u32[]{:S(2)}) async-start(bf16[16,88,256]{2,1,0:T(8,128)(2,1)} %pack.1), calls=%async_computation | async-start | bytes 1441792 | tf_op jit(solution)/shard_map/all_to_all | solution.py:288
  15.6 17.0 %collective-permute-start = (bf16[1392,128]{1,0:T(8,128)(2,1)}, bf16[1392,128]{1,0:T(8,128)(2,1)S(1)}, u32[]{:S(2)}, u32[]{:S(2)}) collective-permute-start(bf16[1392,128]{1,0:T(8,128)(2,1)} %get-tuple-element.7), channel_id=1, source_target_pairs={{0,1},{1,2},{2,3},{3,4},{4,5},{5,6},{6,7},{7,8},{8,9},{9,10},{10,1... | collective-permute-start | bytes 1069064 | tf_op jit(solution)/shard_map/ppermute | solution.py:309
  17.1 15.6 %collective-permute-start.1 = (bf16[1312,128]{1,0:T(8,128)(2,1)}, bf16[1312,128]{1,0:T(8,128)(2,1)S(1)}, u32[]{:S(2)}, u32[]{:S(2)}) collective-permute-start(bf16[1312,128]{1,0:T(8,128)(2,1)} %get-tuple-element.8), channel_id=1, source_target_pairs={{1,0},{2,1},{3,2},{4,3},{5,4},{6,5},{7,6},{8,7},{9,8},{10,9},{11,1... | collective-permute-start | bytes 1007624 | tf_op jit(solution)/shard_map/ppermute | solution.py:310
  32.7 0.7 copy-start.2
  33.4 0.7 copy-start.1
  58.2 0.9 copy-start
  65.7 14.2 %copy-start.3 = (bf16[576,256]{1,0:T(8,128)(2,1)}, bf16[576,256]{1,0:T(8,128)(2,1)S(1)}, u32[]{:S(2)}) copy-start(bf16[576,256]{1,0:T(8,128)(2,1)S(1)} %get-tuple-element.9.own_w_ref) | copy-start | bytes 884740
  65.8 14.2 %copy-start.4 = (bf16[576,256]{1,0:T(8,128)(2,1)}, bf16[576,256]{1,0:T(8,128)(2,1)S(1)}, u32[]{:S(2)}) copy-start(bf16[576,256]{1,0:T(8,128)(2,1)S(1)} %get-tuple-element.10.own_e_ref) | copy-start | bytes 884740
  65.8 14.2 %collective-permute-start.3 = (bf16[576,256]{1,0:T(8,128)(2,1)S(1)}, bf16[576,256]{1,0:T(8,128)(2,1)S(1)}, u32[]{:S(2)}, u32[]{:S(2)}) collective-permute-start(bf16[576,256]{1,0:T(8,128)(2,1)S(1)} %get-tuple-element.9.own_w_ref), channel_id=1, source_target_pairs={{1,0},{2,1},{3,2},{4,3},{5,4},{6,5},{7,6},{8,7},{9,8},{10,9},{11,1... | collective-permute-start | bytes 884744 | tf_op jit(solution)/shard_map/ppermute | solution.py:360
  65.8 14.1 %collective-permute-start.2 = (bf16[576,256]{1,0:T(8,128)(2,1)S(1)}, bf16[576,256]{1,0:T(8,128)(2,1)S(1)}, u32[]{:S(2)}, u32[]{:S(2)}) collective-permute-start(bf16[576,256]{1,0:T(8,128)(2,1)S(1)} %get-tuple-element.10.own_e_ref), channel_id=1, source_target_pairs={{0,1},{1,2},{2,3},{3,4},{4,5},{5,6},{6,7},{7,8},{8,9},{9,10},{10,1... | collective-permute-start | bytes 884744 | tf_op jit(solution)/shard_map/ppermute | solution.py:359
  79.9 0.7 copy-start.5
  80.7 0.7 copy-start.6

commit v2 on v1

v2 whole, which is shorter than its diff:
```python
import functools

import jax
import jax.numpy as jnp
from jax import lax
from jax.experimental import pallas as pl
from jax.experimental.pallas import tpu as pltpu
from jax.sharding import PartitionSpec as P

F32 = jnp.float32
BF16 = jnp.bfloat16
GROUP = 2
HALO = 2
VMEM = 56 * 1024 * 1024


def params(**more):
    return pltpu.CompilerParams(vmem_limit_bytes=VMEM, **more)


def nt_dot(a, b):
    return lax.dot_general(a, b, (((1,), (1,)), ((), ())), preferred_element_type=F32)


def rows16(row):
    return jnp.broadcast_to(row, (16, row.shape[1])).astype(BF16)


def stacked(block, count):
    return jnp.concatenate([block] * count, axis=0)


def pack_kernel(kernel_ref, weight_ref, owner_ref, column_ref, out_ref, *, tiles, capacity, lat):
    levels, pixels = kernel_ref.shape
    column = column_ref[...]
    lon_row = (column // lat).astype(F32)
    lat_row = (column % lat).astype(F32)
    line = lax.broadcasted_iota(jnp.int32, (8, pixels), 0)
    place = jnp.where(line == 0, lon_row, jnp.where(line == 1, lat_row, 0.0))
    payload = jnp.concatenate(
        [kernel_ref[...].astype(F32), weight_ref[...].astype(F32), place], axis=0
    ).astype(BF16)
    owner = owner_ref[...]
    block = min(256, pixels)
    upto = (
        lax.broadcasted_iota(jnp.int32, (block, block), 0)
        <= lax.broadcasted_iota(jnp.int32, (block, block), 1)
    ).astype(F32).astype(BF16)
    carry = jnp.zeros((tiles, 1), F32)
    ranks = []
    for start in range(0, pixels, block):
        named = owner[:, start : start + block] == lax.broadcasted_iota(
            jnp.int32, (tiles, block), 0
        )
        counts = (
            jnp.dot(named.astype(F32).astype(BF16), upto, preferred_element_type=F32) + carry
        )
        carry = counts[:, block - 1 : block]
        ranks.append(jnp.where(named, counts - 1.0, -1.0))
    ranks = jnp.concatenate(ranks, axis=1)
    slot = lax.broadcasted_iota(jnp.int32, (capacity, pixels), 0).astype(F32).astype(BF16)
    for tile in range(tiles):
        rank = stacked(rows16(ranks[tile : tile + 1, :]), capacity // 16)
        chosen = jnp.where(slot == rank, jnp.ones_like(slot), jnp.zeros_like(slot))
        out_ref[tile] = nt_dot(payload, chosen).astype(BF16)


def both(ref, block, x, lon, levels):
    parts = [
        ref[pl.ds((t * levels + block * 8) * lon + x, 8, stride=lon), :] for t in range(GROUP)
    ]
    return jnp.concatenate(parts, axis=0).astype(BF16)


def edge_kernel(field_ref, east_ref, north_ref, fwd_ref, bwd_ref, *, lon, levels):
    step = pl.program_id(0)
    rows = field_ref.shape[0] // lon
    total = rows * pl.num_programs(0)
    for c in range(HALO):
        for block in range(levels // 8):
            spot = c * total + step * rows + block * 8 * GROUP
            at = pl.ds(pl.multiple_of(spot, 16), 8 * GROUP)
            fwd_ref[at, :] = both(field_ref, block, lon - HALO + c, lon, levels)
            bwd_ref[at, :] = both(field_ref, block, c, lon, levels)

    @pl.when(step == 0)
    def _():
        def put(out, place, ref, x):
            spot = HALO * total + place * (levels + 8)
            value = ref[pl.ds(x, levels, stride=lon), :]
            value = jnp.concatenate([value, jnp.zeros((8, value.shape[1]), F32)], axis=0)
            out[spot : spot + levels + 8, :] = value.astype(BF16)

        put(fwd_ref, 0, east_ref, lon - 2)
        put(fwd_ref, 1, east_ref, lon - 1)
        put(fwd_ref, 2, north_ref, lon - 1)
        put(bwd_ref, 0, east_ref, 0)
        put(bwd_ref, 1, north_ref, 0)


def fill_coefs(east_ref, north_ref, edges, coef_ref, columns, lon, levels, total):
    lat = east_ref.shape[1]
    base = HALO * total

    def far(ref, place):
        spot = base + place * (levels + 8)
        return ref[spot : spot + levels + 8, :].astype(F32)[:levels]

    def own(ref, x):
        return ref[pl.ds(x, levels, stride=lon), :]

    def east(x):
        if x < 0:
            return far(edges[0], x + HALO)
        return own(east_ref, x) if x < lon else far(edges[1], 0)

    def north(x):
        if x < 0:
            return far(edges[0], 2)
        return own(north_ref, x) if x < lon else far(edges[1], 1)

    lane = lax.broadcasted_iota(jnp.int32, (levels, lat), 1)
    for i, x in enumerate(columns):
        at = slice(i * lat, (i + 1) * lat)
        face = jnp.where(lane < lat - 1, north(x), 0.0)
        to_east = jnp.maximum(east(x), 0.0)
        to_west = jnp.minimum(east(x - 1), 0.0)
        to_north = jnp.maximum(face, 0.0)
        to_south = pltpu.roll(jnp.minimum(face, 0.0), 1, 1)
        coef_ref[0, :, at] = (1.0 - to_east) + to_west + (to_south - to_north)
        coef_ref[1, :, at] = to_east
        coef_ref[2, :, at] = -to_west
        coef_ref[3, :, at] = to_north
        coef_ref[4, :, at] = -to_south


def stencil(mixed_ref, coef_ref, start, count, coef_start, lat, levels, emit):
    def column(e):
        return slice(e * lat, (e + 1) * lat)

    for block in range(levels // 8):
        lines = slice(block * 8, block * 8 + 8)
        tracer_rows = [
            slice(block * 8 * GROUP + 8 * t, block * 8 * GROUP + 8 * t + 8) for t in range(GROUP)
        ]
        left = [mixed_ref[r, column(start - 1)] for r in tracer_rows]
        centre = [mixed_ref[r, column(start)] for r in tracer_rows]
        for e in range(start, start + count):
            at = column(coef_start + e - start)
            factor = [coef_ref[j, lines, at] for j in range(5)]
            values = []
            for t, r in enumerate(tracer_rows):
                right = mixed_ref[r, column(e + 1)]
                value = (factor[0] * centre[t] + factor[1] * right) + (
                    factor[2] * left[t] + factor[3] * pltpu.roll(centre[t], lat - 1, 1)
                )
                values.append(value + factor[4] * pltpu.roll(centre[t], 1, 1))
                left[t], centre[t] = centre[t], right
            emit(block, e, values)


def two_steps(mix_ref, field_ref, mixed_ref, coef_ref, start, count, coef_start, lat, levels, put):
    def mix(lo, hi):
        for e in range(lo, hi, 2):
            at = slice(e * lat, (e + 2) * lat)
            mixed_ref[:, at] = jnp.dot(mix_ref[...], field_ref[:, at], preferred_element_type=F32)

    def keep(block, e, values):
        at = slice(block * 8 * GROUP, (block + 1) * 8 * GROUP)
        field_ref[at, e * lat : (e + 1) * lat] = jnp.concatenate(values, axis=0).astype(BF16)

    mix(start, start + count)
    stencil(mixed_ref, coef_ref, start + 1, count - 2, coef_start, lat, levels, keep)
    mix(start + 1, start + count - 1)
    stencil(mixed_ref, coef_ref, start + 2, count - 4, coef_start + 1, lat, levels, put)


def inner_kernel(
    mix_ref, east_ref, north_ref, in_ref, out_ref, near_ref, coef_ref, field_ref, mixed_ref,
    *, lon, levels,
):
    lat = in_ref.shape[1]

    @pl.when(pl.program_id(0) == 0)
    def _():
        fill_coefs(east_ref, north_ref, None, coef_ref, range(1, lon - 1), lon, levels, 0)

    for x in range(lon):
        for block in range(levels // 8):
            at = slice(block * 8 * GROUP, (block + 1) * 8 * GROUP)
            field_ref[at, x * lat : (x + 1) * lat] = both(in_ref, block, x, lon, levels)
    side = 2 * HALO * lat
    near_ref[:, :side] = field_ref[:, :side]
    near_ref[:, side:] = field_ref[:, lon * lat - side :]

    def put(block, e, values):
        for t, value in enumerate(values):
            row = block * 8 * GROUP + 8 * t
            out_ref[row : row + 8, (e - HALO) * lat : (e - HALO + 1) * lat] = value

    two_steps(mix_ref, field_ref, mixed_ref, coef_ref, 0, lon, 0, lat, levels, put)


def rim_kernel(
    mix_ref, east_ref, north_ref, fwd_ref, bwd_ref, near_ref, out_ref, coef_ref, field_ref,
    mixed_ref, *, lon, levels, total,
):
    step = pl.program_id(0)
    lat = fwd_ref.shape[1]
    rows = near_ref.shape[0]
    wide = 3 * HALO

    @pl.when(step == 0)
    def _():
        columns = list(range(1 - HALO, HALO + 1)) + list(range(lon - HALO - 1, lon + HALO - 1))
        fill_coefs(
            east_ref, north_ref, (fwd_ref, bwd_ref), coef_ref, columns, lon, levels, total
        )

    for c in range(HALO):
        at = pl.ds(pl.multiple_of(c * total + step * rows, 16), rows)
        field_ref[:, c * lat : (c + 1) * lat] = fwd_ref[at, :]
        e = wide + 2 * HALO + c
        field_ref[:, e * lat : (e + 1) * lat] = bwd_ref[at, :]
    side = 2 * HALO * lat
    field_ref[:, HALO * lat : HALO * lat + side] = near_ref[:, :side]
    field_ref[:, wide * lat : wide * lat + side] = near_ref[:, side:]
    for half in range(2):
        start = half * wide

        def put(block, e, values):
            spot = (e - start - HALO + half * HALO) * lat
            for t, value in enumerate(values):
                row = block * 8 * GROUP + 8 * t
                out_ref[row : row + 8, spot : spot + lat] = value

        two_steps(
            mix_ref, field_ref, mixed_ref, coef_ref, start, wide, half * 2 * HALO, lat, levels, put
        )


def second_half_kernel(
    mix_ref, east_ref, north_ref, fwd_ref, bwd_ref, far_w_ref, own_w_ref, inner_ref, own_e_ref,
    far_e_ref, out_ref, coef_ref, field_ref, mixed_ref, *, lon, levels, total,
):
    lat = out_ref.shape[1]

    @pl.when(pl.program_id(0) == 0)
    def _():
        columns = range(1 - HALO, lon + HALO - 1)
        fill_coefs(
            east_ref, north_ref, (fwd_ref, bwd_ref), coef_ref, columns, lon, levels, total
        )

    spot = 0
    for ref in (far_w_ref, own_w_ref, inner_ref, own_e_ref, far_e_ref):
        width = ref.shape[-1]
        field_ref[:, spot : spot + width] = ref[...]
        spot = spot + width

    def put(block, e, values):
        for t, value in enumerate(values):
            first = (t * levels + block * 8) * lon + e - HALO
            out_ref[pl.ds(first, 8, stride=lon), :] = value

    two_steps(
        mix_ref, field_ref, mixed_ref, coef_ref, 0, lon + 2 * HALO, 0, lat, levels, put
    )


def forcing(got_ref, field, weighted_ref, place_ref, step, pair, *, lat, levels, tracers):
    tiles, _, capacity = got_ref.shape

    @pl.when(step == 0)
    def _():
        for tile in range(tiles):
            at = slice(tile * capacity, (tile + 1) * capacity)
            got = got_ref[tile].astype(F32)
            row = 0
            for t in range(0, tracers, GROUP):
                for block in range(0, levels, 8):
                    kernel = got[block : block + 8]
                    parts = [
                        kernel * got[levels + j : levels + j + 1, :] for j in range(t, t + GROUP)
                    ]
                    value = jnp.concatenate(parts, axis=0).astype(BF16)
                    weighted_ref[row : row + 8 * GROUP, at] = value
                    row = row + 8 * GROUP
            spot = levels + tracers
            column = got[spot : spot + 1, :] * lat + got[spot + 1 : spot + 2, :]
            place_ref[:, at] = jnp.broadcast_to(column, (8, capacity))

    cells = HALO * lat
    slots = tiles * capacity
    key = rows16(place_ref[0:1, :] - (pair * cells).astype(F32))
    cell = lax.broadcasted_iota(jnp.int32, (cells, slots), 0).astype(F32).astype(BF16)
    hit = cell == stacked(key, cells // 16)
    one_hot = jnp.where(hit, jnp.ones_like(cell), jnp.zeros_like(cell))
    return (field + nt_dot(weighted_ref[...], one_hot)).astype(BF16)


def forcing_inner_kernel(got_ref, field_ref, out_ref, weighted_ref, place_ref, **sizes):
    step = pl.program_id(0)
    out_ref[...] = forcing(got_ref, field_ref[...], weighted_ref, place_ref, step, step + 1, **sizes)


def forcing_rim_kernel(
    got_ref, field_ref, west_ref, east_ref, weighted_ref, place_ref, *, pairs, **sizes
):
    step = pl.program_id(0)
    value = forcing(
        got_ref, field_ref[...], weighted_ref, place_ref, step, step * (pairs - 1), **sizes
    )

    @pl.when(step == 0)
    def _():
        west_ref[...] = value

    @pl.when(step == 1)
    def _():
        east_ref[...] = value


def per_device(
    adjoint_in,
    east_courant,
    north_courant,
    level_mix,
    avg_kernel,
    pixel_weight,
    pixel_owner,
    pixel_column,
):
    tracers, levels, lon, lat = adjoint_in.shape
    pixels = avg_kernel.shape[1]
    tiles = lax.axis_size("tile")
    capacity = 4 * pixels // tiles
    slots = tiles * capacity
    total = tracers * levels
    steps = tracers // GROUP
    rows = GROUP * levels
    ring = [(i, (i + 1) % tiles) for i in range(tiles)]
    back = [((i + 1) % tiles, i) for i in range(tiles)]

    field = adjoint_in.reshape(total * lon, lat)
    east = east_courant.reshape(levels * lon, lat)
    north = north_courant.reshape(levels * lon, lat)
    blocks = level_mix.T.reshape(levels // 8, 1, 8, levels // 8, 1, 8)
    same = jnp.eye(GROUP, dtype=BF16).reshape(1, GROUP, 1, 1, GROUP, 1)
    mix = (blocks * same).reshape(rows, rows)

    height = levels + tracers + 8
    payload = pl.pallas_call(
        functools.partial(pack_kernel, tiles=tiles, capacity=capacity, lat=lat),
        out_shape=jax.ShapeDtypeStruct((tiles, height, capacity), BF16),
        compiler_params=params(),
        name="pack",
    )(avg_kernel, pixel_weight, pixel_owner.reshape(1, pixels), pixel_column)
    got = lax.all_to_all(payload, "tile", split_axis=0, concat_axis=0, tiled=True)

    fwd_rows = HALO * total + 3 * (levels + 8)
    bwd_rows = HALO * total + 2 * (levels + 8)
    whole = lambda *shape: pl.BlockSpec(shape, lambda i: (0,) * len(shape))
    fwd, bwd = pl.pallas_call(
        functools.partial(edge_kernel, lon=lon, levels=levels),
        grid=(steps,),
        in_specs=[
            pl.BlockSpec((rows * lon, lat), lambda i: (i, 0)),
            whole(levels * lon, lat),
            whole(levels * lon, lat),
        ],
        out_specs=[whole(fwd_rows, lat), whole(bwd_rows, lat)],
        out_shape=[
            jax.ShapeDtypeStruct((fwd_rows, lat), BF16),
            jax.ShapeDtypeStruct((bwd_rows, lat), BF16),
        ],
        compiler_params=params(),
        name="edges",
    )(field, east, north)
    fwd = lax.ppermute(fwd, "tile", ring)
    bwd = lax.ppermute(bwd, "tile", back)

    def scratch(columns, coefs):
        return [
            pltpu.VMEM((5, levels, coefs * lat), F32),
            pltpu.VMEM((rows, columns * lat), BF16),
            pltpu.VMEM((rows, columns * lat), F32),
        ]

    strip = lambda width: pl.BlockSpec((rows, width), lambda i: (i, 0))
    cells = HALO * lat
    pairs = lon // HALO
    fixed_specs = [whole(rows, rows), whole(levels * lon, lat), whole(levels * lon, lat)]
    edge_specs = [whole(fwd_rows, lat), whole(bwd_rows, lat)]
    inner_width = (lon - 2 * HALO) * lat
    middle, near = pl.pallas_call(
        functools.partial(inner_kernel, lon=lon, levels=levels),
        grid=(steps,),
        in_specs=fixed_specs + [pl.BlockSpec((rows * lon, lat), lambda i: (i, 0))],
        out_specs=[strip(inner_width), strip(4 * cells)],
        out_shape=[
            jax.ShapeDtypeStruct((total, inner_width), F32),
            jax.ShapeDtypeStruct((total, 4 * cells), BF16),
        ],
        scratch_shapes=scratch(lon, lon - 2),
        compiler_params=params(),
        name="first_half_inner",
    )(mix, east, north, field)
    rim = pl.pallas_call(
        functools.partial(rim_kernel, lon=lon, levels=levels, total=total),
        grid=(steps,),
        in_specs=fixed_specs + edge_specs + [strip(4 * cells)],
        out_specs=strip(2 * cells),
        out_shape=jax.ShapeDtypeStruct((total, 2 * cells), F32),
        scratch_shapes=scratch(6 * HALO, 4 * HALO),
        compiler_params=params(),
        name="first_half_rim",
    )(mix, east, north, fwd, bwd, near)

    sizes = dict(lat=lat, levels=levels, tracers=tracers)
    forcing_specs = [
        whole(tiles, height, capacity),
        pl.BlockSpec((total, cells), lambda i: (0, i)),
    ]
    forcing_scratch = [pltpu.VMEM((total, slots), BF16), pltpu.VMEM((8, slots), F32)]
    own_w, own_e = pl.pallas_call(
        functools.partial(forcing_rim_kernel, pairs=pairs, **sizes),
        grid=(2,),
        in_specs=forcing_specs,
        out_specs=[whole(total, cells), whole(total, cells)],
        out_shape=[jax.ShapeDtypeStruct((total, cells), BF16)] * 2,
        scratch_shapes=forcing_scratch,
        compiler_params=params(),
        name="forcing_rim",
    )(got, rim)
    far_w = lax.ppermute(own_e, "tile", ring)
    far_e = lax.ppermute(own_w, "tile", back)
    inner = pl.pallas_call(
        functools.partial(forcing_inner_kernel, **sizes),
        grid=(pairs - 2,),
        in_specs=forcing_specs,
        out_specs=pl.BlockSpec((total, cells), lambda i: (0, i)),
        out_shape=jax.ShapeDtypeStruct((total, inner_width), BF16),
        scratch_shapes=forcing_scratch,
        compiler_params=params(),
        name="forcing_inner",
    )(got, middle)

    out = pl.pallas_call(
        functools.partial(second_half_kernel, lon=lon, levels=levels, total=total),
        grid=(steps,),
        in_specs=fixed_specs
        + edge_specs
        + [strip(cells), strip(cells), strip(inner_width), strip(cells), strip(cells)],
        out_specs=pl.BlockSpec((rows * lon, lat), lambda i: (i, 0)),
        out_shape=jax.ShapeDtypeStruct((total * lon, lat), F32),
        scratch_shapes=scratch(lon + 2 * HALO, lon + 2 * HALO - 2),
        compiler_params=params(),
        name="second_half",
    )(mix, east, north, fwd, bwd, far_w, own_w, inner, own_e, far_e)
    return out.reshape(tracers, levels, lon, lat)


def solution(mesh):
    in_specs = (
        P("ens", None, "tile", None),
        P("ens", "tile", None),
        P("ens", "tile", None),
        P(),
        P("ens", "tile"),
        P("ens", "tile"),
        P("tile", "ens"),
        P("ens", "tile"),
    )
    out_specs = P("ens", None, "tile", None)
    return jax.shard_map(
        per_device, mesh=mesh, in_specs=in_specs, out_specs=out_specs, check_vma=False
    )
```

time: 105 us -> 76.9 us (0.73)
  the two profiles are of different devices: /device:TPU:13 before, /device:TPU:0 now
where the time goes in v2:
time: 76.9 us; the launch traced here: 76.5 us
  Pallas kernels  54.7 us (71%)
  starting transfers between devices  16.3 us (21%)
  local copies, waits for them, and re-layouts  4.38 us (6%)
    pallas_call x1, Pallas kernels, per_device(): pl.pallas_call(functools.partial(forcing_inner_kernel, **sizes), grid=(pa...  11.7 us
    pallas_call x1, Pallas kernels, per_device(): pl.pallas_call(functools.partial(second_half_kernel, lon=lon, levels=leve...  11 us
    pallas_call x1, Pallas kernels, per_device(): pl.pallas_call(functools.partial(inner_kernel, lon=lon, levels=levels), g...  10.2 us
    all_to_all x1, starting transfers between devices, per_device(): lax.all_to_all(payload, 'tile', split_axis=0, concat_axis=0, tiled=True)  7.52 us
    pallas_call x1, Pallas kernels, per_device(): pl.pallas_call(functools.partial(rim_kernel, lon=lon, levels=levels, tota...  6.93 us
    pallas_call x1, Pallas kernels, per_device(): pl.pallas_call(functools.partial(forcing_rim_kernel, pairs=pairs, **sizes...  5.82 us
    pallas_call x1, Pallas kernels, per_device(): pl.pallas_call(functools.partial(pack_kernel, tiles=tiles, capacity=capac...  4.62 us
    pallas_call x1, Pallas kernels, per_device(): pl.pallas_call(functools.partial(edge_kernel, lon=lon, levels=levels), gr...  4.44 us
  transfers between devices with their start and end apart: 5, of which 1 were waited for; matrix products, arithmetic and copies ran while one was open for 3% of the time, Pallas kernels for 43%

profile of v2, /device:TPU:0, one launch (start us, length us, event | category | flops | bytes accessed | tf_op | source)
XLA Modules:
  0.0 76.5 jit_solution(15627712442273695876)
XLA Ops:
  0.0 4.6 %pack.1 = bf16[16,88,256]{2,1,0:T(8,128)(2,1)} custom-call(bf16[72,1024]{1,0:T(8,128)(2,1)} %kernel_ref.1, bf16[8,1024]{1,0:T(8,128)(2,1)} %weight_ref.1, s32[1,1024]{1,0:T(1,128)} %bitcast.17, s32[1,1024]{1,0:T(1,128)} %column_ref.1), custom_call_target="tpu_custom_call" | custom-call | tf_op jit(solution)/shard_map/pack/pallas_call | solution.py:353
  4.6 0.0 copy-start.5
  4.6 7.5 %all-to-all-start = ((bf16[16,88,256]{2,1,0:T(8,128)(2,1)}), bf16[16,88,256]{2,1,0:T(8,128)(2,1)S(1)}, u32[]{:S(2)}, u32[]{:S(2)}) async-start(bf16[16,88,256]{2,1,0:T(8,128)(2,1)} %pack.1), calls=%async_computation | async-start | bytes 1441792 | tf_op jit(solution)/shard_map/all_to_all | solution.py:359
  12.1 4.4 %edges.1 = (bf16[1392,128]{1,0:T(8,128)(2,1)}, bf16[1312,128]{1,0:T(8,128)(2,1)}) custom-call(f32[9216,128]{1,0:T(8,128)} %bitcast.6, f32[1152,128]{1,0:T(8,128)} %bitcast.8, f32[1152,128]{1,0:T(8,128)} %bitcast.12), custom_call_target="tpu_custom_call" | custom-call | tf_op jit(solution)/shard_map/edges/pallas_call | solution.py:364
  16.6 4.4 %collective-permute-start.1 = (bf16[1312,128]{1,0:T(8,128)(2,1)}, bf16[1312,128]{1,0:T(8,128)(2,1)S(1)}, u32[]{:S(2)}, u32[]{:S(2)}) collective-permute-start(bf16[1312,128]{1,0:T(8,128)(2,1)} %get-tuple-element.12), channel_id=1, source_target_pairs={{1,0},{2,1},{3,2},{4,3},{5,4},{6,5},{7,6},{8,7},{9,8},{10,9},{11,1... | collective-permute-start | bytes 1007624 | tf_op jit(solution)/shard_map/ppermute | solution.py:381
  21.0 0.0 collective-permute-start
  21.0 0.0 copy-done.5
  21.0 0.1 copy.10
  21.1 0.2 mul.19
  21.3 0.6 broadcast_multiply_fusion
  22.0 1.0 %mul.23.mix_ref = bf16[144,144]{1,0:T(8,128)(2,1)} reshape(bf16[9,2,8,9,2,8]{5,4,3,2,1,0:T(2,128)(2,1)S(1)} %broadcast_multiply_fusion) | data formatting | bytes 82944 | tf_op jit(solution)/shard_map/mul | solution.py:350
  22.9 10.2 %first_half_inner.1 = (f32[576,1536]{1,0:T(8,128)}, bf16[576,1024]{1,0:T(8,128)(2,1)}) custom-call(bf16[144,144]{1,0:T(8,128)(2,1)} %mul.23.mix_ref, f32[1152,128]{1,0:T(8,128)} %bitcast.9, f32[1152,128]{1,0:T(8,128)} %bitcast.13, f32[9216,128]{1,0:T(8,128)} %bitcast.7), custom_call_target="tpu_custom_call" | custom-call | tf_op jit(solution)/shard_map/first_half_inner/pallas_call | solution.py:396
  33.2 0.0 collective-permute-done.1.bwd_ref
  33.2 0.0 copy-start.2
  33.2 0.4 collective-permute-done.fwd_ref
  33.6 0.0 copy-start.1
  33.6 0.3 copy-done.2
  33.9 0.4 copy-done.1
  34.4 6.9 %first_half_rim.1.field_ref = f32[576,512]{1,0:T(8,128)} custom-call(bf16[144,144]{1,0:T(8,128)(2,1)} %mul.23.mix_ref, f32[1152,128]{1,0:T(8,128)} %bitcast.10, f32[1152,128]{1,0:T(8,128)} %bitcast.14, bf16[1392,128]{1,0:T(8,128)(2,1)} %copy-done.1, bf16[1312,128]{1,0:T(8,128)(2,1)} %copy-done.2, bf16[576,1024]{1,0:T(8,128)(2,1)} %get-tuple-element.13.near_ref), custom_call_target="tpu_custom_call" | custom-call | tf_op jit(solution)/shard_map/first_half_rim/pallas_call | solution.py:409
  41.3 0.0 all-to-all-done.got_ref
  41.3 0.0 copy-start
  41.3 0.9 %copy-done = bf16[16,88,256]{2,1,0:T(8,128)(2,1)} copy-done((bf16[16,88,256]{2,1,0:T(8,128)(2,1)}, bf16[16,88,256]{2,1,0:T(8,128)(2,1)S(1)}, u32[]{:S(2)}) %copy-start) | copy-done | bytes 720920
  42.2 5.8 %forcing_rim.1 = (bf16[576,256]{1,0:T(8,128)(2,1)}, bf16[576,256]{1,0:T(8,128)(2,1)}) custom-call(bf16[16,88,256]{2,1,0:T(8,128)(2,1)} %copy-done, f32[576,512]{1,0:T(8,128)} %first_half_rim.1.field_ref), custom_call_target="tpu_custom_call" | custom-call | tf_op jit(solution)/shard_map/forcing_rim/pallas_call | solution.py:426
  48.0 0.0 collective-permute-start.2
  48.0 4.4 %collective-permute-start.3 = (bf16[576,256]{1,0:T(8,128)(2,1)}, bf16[576,256]{1,0:T(8,128)(2,1)S(1)}, u32[]{:S(2)}, u32[]{:S(2)}) collective-permute-start(bf16[576,256]{1,0:T(8,128)(2,1)} %get-tuple-element.15.own_w_ref), channel_id=1, source_target_pairs={{1,0},{2,1},{3,2},{4,3},{5,4},{6,5},{7,6},{8,7},{9,8},{10,9},{11,1... | collective-permute-start | bytes 884744 | tf_op jit(solution)/shard_map/ppermute | solution.py:437
  52.4 11.7 %forcing_inner.1.inner_ref = bf16[576,1536]{1,0:T(8,128)(2,1)} custom-call(bf16[16,88,256]{2,1,0:T(8,128)(2,1)} %copy-done, f32[576,1536]{1,0:T(8,128)} %get-tuple-element.16.field_ref), custom_call_target="tpu_custom_call" | custom-call | tf_op jit(solution)/shard_map/forcing_inner/pallas_call | solution.py:438
  64.1 0.0 collective-permute-done.2.far_w_ref
  64.1 0.0 copy-start.3
  64.1 0.0 collective-permute-done.3.far_e_ref
  64.1 0.7 copy-done.3
  64.8 0.0 copy-start.4
  64.8 0.7 copy-done.4
  65.5 11.0 %second_half.1 = f32[9216,128]{1,0:T(8,128)} custom-call(bf16[144,144]{1,0:T(8,128)(2,1)} %mul.23.mix_ref, f32[1152,128]{1,0:T(8,128)} %bitcast.11, f32[1152,128]{1,0:T(8,128)} %bitcast.15, bf16[1392,128]{1,0:T(8,128)(2,1)} %copy-done.1, bf16[1312,128]{1,0:T(8,128)(2,1)} %copy-done.2, bf16[576,256]{1,0:T(8,128)(2,1)} %copy-done.3, ...), custom_call_target="tpu_custom_call" | custom-call | tf_op jit(solution)/shard_map/second_half/pallas_call | solution.py:449
  (1 shorter events, 0.0 us)
Async XLA Ops:
  4.6 16.4 %copy-start.5 = (bf16[72,72]{1,0:T(8,128)(2,1)S(1)}, bf16[72,72]{1,0:T(8,128)(2,1)}, u32[]{:S(2)}) copy-start(bf16[72,72]{1,0:T(8,128)(2,1)} %param.11) | copy-start | bytes 31108
  4.6 36.7 %all-to-all-start = ((bf16[16,88,256]{2,1,0:T(8,128)(2,1)}), bf16[16,88,256]{2,1,0:T(8,128)(2,1)S(1)}, u32[]{:S(2)}, u32[]{:S(2)}) async-start(bf16[16,88,256]{2,1,0:T(8,128)(2,1)} %pack.1), calls=%async_computation | async-start | bytes 1441792 | tf_op jit(solution)/shard_map/all_to_all | solution.py:359
  16.6 16.6 %collective-permute-start.1 = (bf16[1312,128]{1,0:T(8,128)(2,1)}, bf16[1312,128]{1,0:T(8,128)(2,1)S(1)}, u32[]{:S(2)}, u32[]{:S(2)}) collective-permute-start(bf16[1312,128]{1,0:T(8,128)(2,1)} %get-tuple-element.12), channel_id=1, source_target_pairs={{1,0},{2,1},{3,2},{4,3},{5,4},{6,5},{7,6},{8,7},{9,8},{10,9},{11,1... | collective-permute-start | bytes 1007624 | tf_op jit(solution)/shard_map/ppermute | solution.py:381
  21.0 12.7 %collective-permute-start = (bf16[1392,128]{1,0:T(8,128)(2,1)}, bf16[1392,128]{1,0:T(8,128)(2,1)S(1)}, u32[]{:S(2)}, u32[]{:S(2)}) collective-permute-start(bf16[1392,128]{1,0:T(8,128)(2,1)} %get-tuple-element.11), channel_id=1, source_target_pairs={{0,1},{1,2},{2,3},{3,4},{4,5},{5,6},{6,7},{7,8},{8,9},{9,10},{10,1... | collective-permute-start | bytes 1069064 | tf_op jit(solution)/shard_map/ppermute | solution.py:380
  33.2 0.7 copy-start.2
  33.6 0.7 copy-start.1
  41.3 0.9 %copy-start = (bf16[16,88,256]{2,1,0:T(8,128)(2,1)}, bf16[16,88,256]{2,1,0:T(8,128)(2,1)S(1)}, u32[]{:S(2)}) copy-start(bf16[16,88,256]{2,1,0:T(8,128)(2,1)S(1)} %all-to-all-done.got_ref) | copy-start | bytes 2162692
  48.0 16.1 %collective-permute-start.2 = (bf16[576,256]{1,0:T(8,128)(2,1)}, bf16[576,256]{1,0:T(8,128)(2,1)S(1)}, u32[]{:S(2)}, u32[]{:S(2)}) collective-permute-start(bf16[576,256]{1,0:T(8,128)(2,1)} %get-tuple-element.14.own_e_ref), channel_id=1, source_target_pairs={{0,1},{1,2},{2,3},{3,4},{4,5},{5,6},{6,7},{7,8},{8,9},{9,10},{10,1... | collective-permute-start | bytes 884744 | tf_op jit(solution)/shard_map/ppermute | solution.py:436
  48.0 16.1 %collective-permute-start.3 = (bf16[576,256]{1,0:T(8,128)(2,1)}, bf16[576,256]{1,0:T(8,128)(2,1)S(1)}, u32[]{:S(2)}, u32[]{:S(2)}) collective-permute-start(bf16[576,256]{1,0:T(8,128)(2,1)} %get-tuple-element.15.own_w_ref), channel_id=1, source_target_pairs={{1,0},{2,1},{3,2},{4,3},{5,4},{6,5},{7,6},{8,7},{9,8},{10,9},{11,1... | collective-permute-start | bytes 884744 | tf_op jit(solution)/shard_map/ppermute | solution.py:437
  64.1 0.7 copy-start.3
  64.8 0.7 copy-start.4

commit v3 on v2

--- a/solution.py
+++ b/solution.py
@@ -30,35 +30,65 @@
     return jnp.concatenate([block] * count, axis=0)
 
 
-def pack_kernel(kernel_ref, weight_ref, owner_ref, column_ref, out_ref, *, tiles, capacity, lat):
+def pack_kernel(
+    kernel_ref, weight_ref, owner_ref, column_ref, out_ref, *, tiles, capacity, lat, pairs
+):
     levels, pixels = kernel_ref.shape
     column = column_ref[...]
-    lon_row = (column // lat).astype(F32)
-    lat_row = (column % lat).astype(F32)
+    longitude = column // lat
     line = lax.broadcasted_iota(jnp.int32, (8, pixels), 0)
-    place = jnp.where(line == 0, lon_row, jnp.where(line == 1, lat_row, 0.0))
+    place = jnp.where(
+        line == 0,
+        (longitude + 1).astype(F32),
+        jnp.where(line == 1, (column % lat).astype(F32), 0.0),
+    )
     payload = jnp.concatenate(
         [kernel_ref[...].astype(F32), weight_ref[...].astype(F32), place], axis=0
     ).astype(BF16)
-    owner = owner_ref[...]
+    classes = tiles * pairs
+    named = owner_ref[...] * pairs + longitude // HALO
     block = min(256, pixels)
-    upto = (
-        lax.broadcasted_iota(jnp.int32, (block, block), 0)
-        <= lax.broadcasted_iota(jnp.int32, (block, block), 1)
-    ).astype(F32).astype(BF16)
-    carry = jnp.zeros((tiles, 1), F32)
-    ranks = []
+
+    def iota(shape, dim):
+        return lax.broadcasted_iota(jnp.int32, shape, dim)
+
+    def flags(mask):
+        return mask.astype(F32).astype(BF16)
+
+    upto = flags(iota((block, block), 0) <= iota((block, block), 1))
+    carry = jnp.zeros((classes, 1), F32)
+    members, counted = [], []
     for start in range(0, pixels, block):
-        named = owner[:, start : start + block] == lax.broadcasted_iota(
-            jnp.int32, (tiles, block), 0
+        member = named[:, start : start + block] == iota((classes, block), 0)
+        counts = jnp.dot(flags(member), upto, preferred_element_type=F32) + carry
+        carry = counts[:, block - 1 : block]
+        members.append(member)
+        counted.append(counts)
+    size = jnp.broadcast_to(carry, (classes, 128))
+    row, other = iota((classes, classes), 0), iota((classes, classes), 1)
+    same = row // pairs == other // pairs
+    sizes = size.astype(BF16)
+    before = jnp.dot(flags(same & (other < row)), sizes, preferred_element_type=F32)
+    after = jnp.dot(flags(same & (other >= row)), sizes, preferred_element_type=F32)
+    pair = iota((classes, 128), 0) % pairs
+    slack = pair.astype(F32) * (capacity // pairs) - before
+    shift = 1
+    while shift < pairs:
+        slack = jnp.where(pair >= shift, jnp.maximum(slack, pltpu.roll(slack, shift, 0)), slack)
+        shift = 2 * shift
+    begin = jnp.minimum(before + slack, capacity - after)[:, :1]
+    gather = flags(iota((tiles, classes), 0) == iota((tiles, classes), 1) // pairs)
+    ranks = [
+        jnp.dot(
+            gather,
+            jnp.where(member, begin + counts, 0.0).astype(BF16),
+            preferred_element_type=F32,
         )
-        counts = (
-            jnp.dot(named.astype(F32).astype(BF16), upto, preferred_element_type=F32) + carry
-        )
-        carry = counts[:, block - 1 : block]
-        ranks.append(jnp.where(named, counts - 1.0, -1.0))
+        - 1.0
+        for member, counts in zip(members, counted)
+    ]
     ranks = jnp.concatenate(ranks, axis=1)
-    slot = lax.broadcasted_iota(jnp.int32, (capacity, pixels), 0).astype(F32).astype(BF16)
+    slot = iota((capacity, pixels), 0).astype(F32).astype(BF16)
     for tile in range(tiles):
         rank = stacked(rows16(ranks[tile : tile + 1, :]), capacity // 16)
         chosen = jnp.where(slot == rank, jnp.ones_like(slot), jnp.zeros_like(slot))
@@ -72,7 +102,9 @@
     return jnp.concatenate(parts, axis=0).astype(BF16)
 
 
-def edge_kernel(field_ref, east_ref, north_ref, fwd_ref, bwd_ref, *, lon, levels):
+def edge_kernel(
+    field_ref, east_ref, north_ref, level_mix_ref, fwd_ref, bwd_ref, mix_ref, *, lon, levels
+):
     step = pl.program_id(0)
     rows = field_ref.shape[0] // lon
     total = rows * pl.num_programs(0)
@@ -96,6 +128,15 @@
         put(fwd_ref, 2, north_ref, lon - 1)
         put(bwd_ref, 0, east_ref, 0)
         put(bwd_ref, 1, north_ref, 0)
+        rows = GROUP * levels
+        row = lax.broadcasted_iota(jnp.int32, (rows, levels), 0)
+        level = row // (8 * GROUP) * 8 + row % 8
+        mine = level == lax.broadcasted_iota(jnp.int32, (rows, levels), 1)
+        mix = jnp.zeros((rows, rows), F32)
+        for t in range(GROUP):
+            pick = (mine & (row // 8 % GROUP == t)).astype(F32).astype(BF16)
+            mix = mix + nt_dot(nt_dot(pick, level_mix_ref[...]).astype(BF16), pick)
+        mix_ref[...] = mix.astype(BF16)
 
 
 def fill_coefs(east_ref, north_ref, edges, coef_ref, columns, lon, levels, total):
@@ -268,49 +309,85 @@
     )
 
 
-def forcing(got_ref, field, weighted_ref, place_ref, step, pair, *, lat, levels, tracers):
+def regions_of(capacity):
+    return capacity // 64 if capacity % 128 == 0 else 1
+
+
+def regroup(got_ref, store):
+    tiles, height, capacity = got_ref.shape
+    if regions_of(capacity) == 1:
+        for tile in range(tiles):
+            store(tile * capacity, got_ref[tile].astype(F32))
+        return
+    low = lax.broadcasted_iota(jnp.int32, (height, 128), 1) < 64
+    for tile in range(0, tiles, 2):
+        for half in range(capacity // 128):
+            at = slice(half * 128, half * 128 + 128)
+            one, two = got_ref[tile, :, at].astype(F32), got_ref[tile + 1, :, at].astype(F32)
+            spot = 2 * half * tiles * 64 + tile * 64
+            store(spot, jnp.where(low, one, pltpu.roll(two, 64, 1)))
+            store(spot + tiles * 64, jnp.where(low, pltpu.roll(one, 64, 1), two))
+
+
+def forcing(
+    got_ref, field_ref, weighted_ref, place_ref, range_ref, total_ref, step, pair,
+    *, lat, levels, tracers,
+):
     tiles, _, capacity = got_ref.shape
+    cells = HALO * lat
+    parts = regions_of(capacity)
+    wide = tiles * capacity // parts
 
     @pl.when(step == 0)
     def _():
-        for tile in range(tiles):
-            at = slice(tile * capacity, (tile + 1) * capacity)
-            got = got_ref[tile].astype(F32)
+        def store(spot, got):
+            at = slice(spot, spot + got.shape[1])
             row = 0
             for t in range(0, tracers, GROUP):
                 for block in range(0, levels, 8):
                     kernel = got[block : block + 8]
-                    parts = [
+                    pieces = [
                         kernel * got[levels + j : levels + j + 1, :] for j in range(t, t + GROUP)
                     ]
-                    value = jnp.concatenate(parts, axis=0).astype(BF16)
+                    value = jnp.concatenate(pieces, axis=0).astype(BF16)
                     weighted_ref[row : row + 8 * GROUP, at] = value
                     row = row + 8 * GROUP
-            spot = levels + tracers
-            column = got[spot : spot + 1, :] * lat + got[spot + 1 : spot + 2, :]
-            place_ref[:, at] = jnp.broadcast_to(column, (8, capacity))
-
-    cells = HALO * lat
-    slots = tiles * capacity
-    key = rows16(place_ref[0:1, :] - (pair * cells).astype(F32))
-    cell = lax.broadcasted_iota(jnp.int32, (cells, slots), 0).astype(F32).astype(BF16)
-    hit = cell == stacked(key, cells // 16)
-    one_hot = jnp.where(hit, jnp.ones_like(cell), jnp.zeros_like(cell))
-    return (field + nt_dot(weighted_ref[...], one_hot)).astype(BF16)
-
-
-def forcing_inner_kernel(got_ref, field_ref, out_ref, weighted_ref, place_ref, **sizes):
+            first = levels + tracers
+            column = (got[first : first + 1, :] - 1.0) * lat + got[first + 1 : first + 2, :]
+            place_ref[:, at] = jnp.broadcast_to(column, (8, got.shape[1]))
+
+        regroup(got_ref, store)
+        for part in range(parts):
+            place = place_ref[:, part * wide : (part + 1) * wide]
+            far = 1e6
+            range_ref[2 * part] = jnp.min(jnp.where(place < 0.0, far, place))
+            range_ref[2 * part + 1] = jnp.max(place)
+
+    total_ref[...] = field_ref[...]
+    offset = (pair * cells).astype(F32)
+    for part in range(parts):
+        held = (range_ref[2 * part] < offset + cells) & (range_ref[2 * part + 1] >= offset)
+
+        @pl.when(held)
+        def _():
+            at = slice(part * wide, (part + 1) * wide)
+            key = rows16(place_ref[0:1, at] - offset)
+            cell = lax.broadcasted_iota(jnp.int32, (cells, wide), 0).astype(F32).astype(BF16)
+            hit = cell == stacked(key, cells // 16)
+            one_hot = jnp.where(hit, jnp.ones_like(cell), jnp.zeros_like(cell))
+            total_ref[...] += nt_dot(weighted_ref[:, at], one_hot)
+
+    return total_ref[...].astype(BF16)
+
+
+def forcing_inner_kernel(got_ref, field_ref, out_ref, *scratch, **sizes):
     step = pl.program_id(0)
-    out_ref[...] = forcing(got_ref, field_ref[...], weighted_ref, place_ref, step, step + 1, **sizes)
-
-
-def forcing_rim_kernel(
-    got_ref, field_ref, west_ref, east_ref, weighted_ref, place_ref, *, pairs, **sizes
-):
+    out_ref[...] = forcing(got_ref, field_ref, *scratch, step, step + 1, **sizes)
+
+
+def forcing_rim_kernel(got_ref, field_ref, west_ref, east_ref, *scratch, pairs, **sizes):
     step = pl.program_id(0)
-    value = forcing(
-        got_ref, field_ref[...], weighted_ref, place_ref, step, step * (pairs - 1), **sizes
-    )
+    value = forcing(got_ref, field_ref, *scratch, step, step * (pairs - 1), **sizes)
 
     @pl.when(step == 0)
     def _():
@@ -345,13 +422,10 @@
     field = adjoint_in.reshape(total * lon, lat)
     east = east_courant.reshape(levels * lon, lat)
     north = north_courant.reshape(levels * lon, lat)
-    blocks = level_mix.T.reshape(levels // 8, 1, 8, levels // 8, 1, 8)
-    same = jnp.eye(GROUP, dtype=BF16).reshape(1, GROUP, 1, 1, GROUP, 1)
-    mix = (blocks * same).reshape(rows, rows)
-
+    pairs = lon // HALO
     height = levels + tracers + 8
     payload = pl.pallas_call(
-        functools.partial(pack_kernel, tiles=tiles, capacity=capacity, lat=lat),
+        functools.partial(pack_kernel, tiles=tiles, capacity=capacity, lat=lat, pairs=pairs),
         out_shape=jax.ShapeDtypeStruct((tiles, height, capacity), BF16),
         compiler_params=params(),
         name="pack",
@@ -361,22 +435,24 @@
     fwd_rows = HALO * total + 3 * (levels + 8)
     bwd_rows = HALO * total + 2 * (levels + 8)
     whole = lambda *shape: pl.BlockSpec(shape, lambda i: (0,) * len(shape))
-    fwd, bwd = pl.pallas_call(
+    fwd, bwd, mix = pl.pallas_call(
         functools.partial(edge_kernel, lon=lon, levels=levels),
         grid=(steps,),
         in_specs=[
             pl.BlockSpec((rows * lon, lat), lambda i: (i, 0)),
             whole(levels * lon, lat),
             whole(levels * lon, lat),
+            whole(levels, levels),
         ],
-        out_specs=[whole(fwd_rows, lat), whole(bwd_rows, lat)],
+        out_specs=[whole(fwd_rows, lat), whole(bwd_rows, lat), whole(rows, rows)],
         out_shape=[
             jax.ShapeDtypeStruct((fwd_rows, lat), BF16),
             jax.ShapeDtypeStruct((bwd_rows, lat), BF16),
+            jax.ShapeDtypeStruct((rows, rows), BF16),
         ],
         compiler_params=params(),
         name="edges",
-    )(field, east, north)
+    )(field, east, north, level_mix)
     fwd = lax.ppermute(fwd, "tile", ring)
     bwd = lax.ppermute(bwd, "tile", back)
 
@@ -389,7 +465,6 @@
 
     strip = lambda width: pl.BlockSpec((rows, width), lambda i: (i, 0))
     cells = HALO * lat
-    pairs = lon // HALO
     fixed_specs = [whole(rows, rows), whole(levels * lon, lat), whole(levels * lon, lat)]
     edge_specs = [whole(fwd_rows, lat), whole(bwd_rows, lat)]
     inner_width = (lon - 2 * HALO) * lat
@@ -422,7 +497,12 @@
         whole(tiles, height, capacity),
         pl.BlockSpec((total, cells), lambda i: (0, i)),
     ]
-    forcing_scratch = [pltpu.VMEM((total, slots), BF16), pltpu.VMEM((8, slots), F32)]
+    forcing_scratch = [
+        pltpu.VMEM((total, slots), BF16),
+        pltpu.VMEM((8, slots), F32),
+        pltpu.SMEM((2 * regions_of(capacity),), F32),
+        pltpu.VMEM((total, cells), F32),
+    ]
     own_w, own_e = pl.pallas_call(
         functools.partial(forcing_rim_kernel, pairs=pairs, **sizes),
         grid=(2,),

time: 76.9 us -> 73.4 us (0.954)
  Pallas kernels: 54.7 us -> 51.6 us
  waiting for transfers between devices: 0.43 us -> 2.02 us
  local copies, waits for them, and re-layouts: 4.38 us -> 3 us
    pallas_call x1, Pallas kernels: 11.7 us -> 8.48 us  [per_device(): pl.pallas_call(functools.partial(forcing_inner_kernel, **sizes), grid=(pa...]
    ppermute x1, waiting for transfers between devices: 0.42 us -> 2.01 us  [per_device(): fwd = lax.ppermute(fwd, 'tile', ring)]
    mul x2 -> x0, local copies, waits for them, and re-layouts: 1.23 us -> none  [per_device(): mix = (blocks * same).reshape(rows, rows)]
    pallas_call x1, Pallas kernels: 5.82 us -> 4.91 us  [per_device(): pl.pallas_call(functools.partial(forcing_rim_kernel, pairs=pairs, **sizes...]
    unnamed x12 -> x10, local copies, waits for them, and re-layouts: 3.06 us -> 3 us
  transfers between devices with their start and end apart: 5 -> 5, of which waited for: 1 -> 1; matrix products, arithmetic and copies ran while one was open for 3% -> 0% of each run, Pallas kernels for 43% -> 42%
where the time goes in v3:
time: 73.4 us; the launch traced here: 72.9 us
  Pallas kernels  51.6 us (70%)
  starting transfers between devices  16.3 us (22%)
  local copies, waits for them, and re-layouts  3 us (4%)
  waiting for transfers between devices  2.02 us (3%)
    pallas_call x1, Pallas kernels, per_device(): pl.pallas_call(functools.partial(second_half_kernel, lon=lon, levels=leve...  11 us
    pallas_call x1, Pallas kernels, per_device(): pl.pallas_call(functools.partial(inner_kernel, lon=lon, levels=levels), g...  10.2 us
    pallas_call x1, Pallas kernels, per_device(): pl.pallas_call(functools.partial(forcing_inner_kernel, **sizes), grid=(pa...  8.48 us
    all_to_all x1, starting transfers between devices, per_device(): lax.all_to_all(payload, 'tile', split_axis=0, concat_axis=0, tiled=True)  7.39 us
    pallas_call x1, Pallas kernels, per_device(): pl.pallas_call(functools.partial(rim_kernel, lon=lon, levels=levels, tota...  6.92 us
    pallas_call x1, Pallas kernels, per_device(): pl.pallas_call(functools.partial(pack_kernel, tiles=tiles, capacity=capac...  5.29 us
    pallas_call x1, Pallas kernels, per_device(): pl.pallas_call(functools.partial(forcing_rim_kernel, pairs=pairs, **sizes...  4.91 us
    pallas_call x1, Pallas kernels, per_device(): pl.pallas_call(functools.partial(edge_kernel, lon=lon, levels=levels), gr...  4.76 us
  transfers between devices with their start and end apart: 5, of which 1 were waited for; matrix products, arithmetic and copies ran while one was open for 0% of the time, Pallas kernels for 42%

profile of v3, /device:TPU:0, one launch (start us, length us, event | category | flops | bytes accessed | tf_op | source)
XLA Modules:
  0.0 72.9 jit_solution(14421555403034510116)
XLA Ops:
  0.0 5.3 %pack.1 = bf16[16,88,256]{2,1,0:T(8,128)(2,1)} custom-call(bf16[72,1024]{1,0:T(8,128)(2,1)} %kernel_ref.1, bf16[8,1024]{1,0:T(8,128)(2,1)} %weight_ref.1, s32[1,1024]{1,0:T(1,128)} %bitcast.15, s32[1,1024]{1,0:T(1,128)} %column_ref.1), custom_call_target="tpu_custom_call" | custom-call | tf_op jit(solution)/shard_map/pack/pallas_call | solution.py:427
  5.3 7.4 %all-to-all-start = ((bf16[16,88,256]{2,1,0:T(8,128)(2,1)}), bf16[16,88,256]{2,1,0:T(8,128)(2,1)S(1)}, u32[]{:S(2)}, u32[]{:S(2)}) async-start(bf16[16,88,256]{2,1,0:T(8,128)(2,1)} %pack.1), calls=%async_computation | async-start | bytes 1441792 | tf_op jit(solution)/shard_map/all_to_all | solution.py:433
  12.7 4.8 %edges.1 = (bf16[1392,128]{1,0:T(8,128)(2,1)}, bf16[1312,128]{1,0:T(8,128)(2,1)}, bf16[144,144]{1,0:T(8,128)(2,1)}) custom-call(f32[9216,128]{1,0:T(8,128)} %bitcast.5, f32[1152,128]{1,0:T(8,128)} %bitcast.7, f32[1152,128]{1,0:T(8,128)} %bitcast.11, bf16[72,72]{1,0:T(8,128)(2,1)} %level_mix_ref.1), custom_call_target="tpu_custom_call" | custom-call | tf_op jit(solution)/shard_map/edges/pallas_call | solution.py:438
  17.4 0.4 collective-permute-start
  17.9 4.0 %collective-permute-start.1 = (bf16[1312,128]{1,0:T(8,128)(2,1)}, bf16[1312,128]{1,0:T(8,128)(2,1)S(1)}, u32[]{:S(2)}, u32[]{:S(2)}) collective-permute-start(bf16[1312,128]{1,0:T(8,128)(2,1)} %get-tuple-element.14), channel_id=1, source_target_pairs={{1,0},{2,1},{3,2},{4,3},{5,4},{6,5},{7,6},{8,7},{9,8},{10,9},{11,1... | collective-permute-start | bytes 1007624 | tf_op jit(solution)/shard_map/ppermute | solution.py:457
  21.9 10.2 %first_half_inner.1 = (f32[576,1536]{1,0:T(8,128)}, bf16[576,1024]{1,0:T(8,128)(2,1)}) custom-call(bf16[144,144]{1,0:T(8,128)(2,1)} %get-tuple-element.12.mix_ref, f32[1152,128]{1,0:T(8,128)} %bitcast.8, f32[1152,128]{1,0:T(8,128)} %bitcast.12, f32[9216,128]{1,0:T(8,128)} %bitcast.6), custom_call_target="tpu_custom_call" | custom-call | tf_op jit(solution)/shard_map/first_half_inner/pallas_call | solution.py:471
  32.1 0.0 collective-permute-done.1.bwd_ref
  32.1 0.0 copy-start.2
  32.2 2.0 %collective-permute-done.fwd_ref = bf16[1392,128]{1,0:T(8,128)(2,1)S(1)} collective-permute-done((bf16[1392,128]{1,0:T(8,128)(2,1)}, bf16[1392,128]{1,0:T(8,128)(2,1)S(1)}, u32[]{:S(2)}, u32[]{:S(2)}) %collective-permute-start) | collective-permute-done | bytes 356384 | tf_op jit(solution)/shard_map/ppermute | solution.py:456
  34.2 0.0 copy-start.1
  34.2 0.0 copy-done.2
  34.2 0.7 copy-done.1
  34.9 6.9 %first_half_rim.1.field_ref = f32[576,512]{1,0:T(8,128)} custom-call(bf16[144,144]{1,0:T(8,128)(2,1)} %get-tuple-element.12.mix_ref, f32[1152,128]{1,0:T(8,128)} %bitcast.9, f32[1152,128]{1,0:T(8,128)} %bitcast.13, bf16[1392,128]{1,0:T(8,128)(2,1)} %copy-done.1, bf16[1312,128]{1,0:T(8,128)(2,1)} %copy-done.2, bf16[576,1024]{1,0:T(8,128)(2,1)} %get-tuple-element.15.near_ref), custom_call_target="tpu_custom_call" | custom-call | tf_op jit(solution)/shard_map/first_half_rim/pallas_call | solution.py:484
  41.8 0.0 all-to-all-done.got_ref
  41.8 0.0 copy-start
  41.8 0.9 %copy-done = bf16[16,88,256]{2,1,0:T(8,128)(2,1)} copy-done((bf16[16,88,256]{2,1,0:T(8,128)(2,1)}, bf16[16,88,256]{2,1,0:T(8,128)(2,1)S(1)}, u32[]{:S(2)}) %copy-start) | copy-done | bytes 720920
  42.7 4.9 %forcing_rim.1 = (bf16[576,256]{1,0:T(8,128)(2,1)}, bf16[576,256]{1,0:T(8,128)(2,1)}) custom-call(bf16[16,88,256]{2,1,0:T(8,128)(2,1)} %copy-done, f32[576,512]{1,0:T(8,128)} %first_half_rim.1.field_ref), custom_call_target="tpu_custom_call" | custom-call | tf_op jit(solution)/shard_map/forcing_rim/pallas_call | solution.py:506
  47.6 0.0 collective-permute-start.2
  47.6 4.4 %collective-permute-start.3 = (bf16[576,256]{1,0:T(8,128)(2,1)}, bf16[576,256]{1,0:T(8,128)(2,1)S(1)}, u32[]{:S(2)}, u32[]{:S(2)}) collective-permute-start(bf16[576,256]{1,0:T(8,128)(2,1)} %get-tuple-element.17.own_w_ref), channel_id=1, source_target_pairs={{1,0},{2,1},{3,2},{4,3},{5,4},{6,5},{7,6},{8,7},{9,8},{10,9},{11,1... | collective-permute-start | bytes 884744 | tf_op jit(solution)/shard_map/ppermute | solution.py:517
  52.0 8.5 %forcing_inner.1.inner_ref = bf16[576,1536]{1,0:T(8,128)(2,1)} custom-call(bf16[16,88,256]{2,1,0:T(8,128)(2,1)} %copy-done, f32[576,1536]{1,0:T(8,128)} %get-tuple-element.18.field_ref), custom_call_target="tpu_custom_call" | custom-call | tf_op jit(solution)/shard_map/forcing_inner/pallas_call | solution.py:518
  60.5 0.0 collective-permute-done.2.far_w_ref
  60.5 0.0 copy-start.3
  60.5 0.0 collective-permute-done.3.far_e_ref
  60.5 0.7 copy-done.3
  61.2 0.0 copy-start.4
  61.2 0.7 copy-done.4
  61.9 11.0 %second_half.1 = f32[9216,128]{1,0:T(8,128)} custom-call(bf16[144,144]{1,0:T(8,128)(2,1)} %get-tuple-element.12.mix_ref, f32[1152,128]{1,0:T(8,128)} %bitcast.10, f32[1152,128]{1,0:T(8,128)} %bitcast.14, bf16[1392,128]{1,0:T(8,128)(2,1)} %copy-done.1, bf16[1312,128]{1,0:T(8,128)(2,1)} %copy-done.2, bf16[576,256]{1,0:T(8,128)(2,1)} %copy-done.3, ...), custom_call_target="tpu_custom_call" | custom-call | tf_op jit(solution)/shard_map/second_half/pallas_call | solution.py:529
Async XLA Ops:
  5.3 36.5 %all-to-all-start = ((bf16[16,88,256]{2,1,0:T(8,128)(2,1)}), bf16[16,88,256]{2,1,0:T(8,128)(2,1)S(1)}, u32[]{:S(2)}, u32[]{:S(2)}) async-start(bf16[16,88,256]{2,1,0:T(8,128)(2,1)} %pack.1), calls=%async_computation | async-start | bytes 1441792 | tf_op jit(solution)/shard_map/all_to_all | solution.py:433
  17.4 16.7 %collective-permute-start = (bf16[1392,128]{1,0:T(8,128)(2,1)}, bf16[1392,128]{1,0:T(8,128)(2,1)S(1)}, u32[]{:S(2)}, u32[]{:S(2)}) collective-permute-start(bf16[1392,128]{1,0:T(8,128)(2,1)} %get-tuple-element.13), channel_id=1, source_target_pairs={{0,1},{1,2},{2,3},{3,4},{4,5},{5,6},{6,7},{7,8},{8,9},{9,10},{10,1... | collective-permute-start | bytes 1069064 | tf_op jit(solution)/shard_map/ppermute | solution.py:456
  17.9 14.3 %collective-permute-start.1 = (bf16[1312,128]{1,0:T(8,128)(2,1)}, bf16[1312,128]{1,0:T(8,128)(2,1)S(1)}, u32[]{:S(2)}, u32[]{:S(2)}) collective-permute-start(bf16[1312,128]{1,0:T(8,128)(2,1)} %get-tuple-element.14), channel_id=1, source_target_pairs={{1,0},{2,1},{3,2},{4,3},{5,4},{6,5},{7,6},{8,7},{9,8},{10,9},{11,1... | collective-permute-start | bytes 1007624 | tf_op jit(solution)/shard_map/ppermute | solution.py:457
  32.1 2.0 %copy-start.2 = (bf16[1312,128]{1,0:T(8,128)(2,1)}, bf16[1312,128]{1,0:T(8,128)(2,1)S(1)}, u32[]{:S(2)}) copy-start(bf16[1312,128]{1,0:T(8,128)(2,1)S(1)} %collective-permute-done.1.bwd_ref) | copy-start | bytes 1007620
  34.2 0.7 copy-start.1
  41.8 0.9 %copy-start = (bf16[16,88,256]{2,1,0:T(8,128)(2,1)}, bf16[16,88,256]{2,1,0:T(8,128)(2,1)S(1)}, u32[]{:S(2)}) copy-start(bf16[16,88,256]{2,1,0:T(8,128)(2,1)S(1)} %all-to-all-done.got_ref) | copy-start | bytes 2162692
  47.6 12.9 %collective-permute-start.2 = (bf16[576,256]{1,0:T(8,128)(2,1)}, bf16[576,256]{1,0:T(8,128)(2,1)S(1)}, u32[]{:S(2)}, u32[]{:S(2)}) collective-permute-start(bf16[576,256]{1,0:T(8,128)(2,1)} %get-tuple-element.16.own_e_ref), channel_id=1, source_target_pairs={{0,1},{1,2},{2,3},{3,4},{4,5},{5,6},{6,7},{7,8},{8,9},{9,10},{10,1... | collective-permute-start | bytes 884744 | tf_op jit(solution)/shard_map/ppermute | solution.py:516
  47.6 12.9 %collective-permute-start.3 = (bf16[576,256]{1,0:T(8,128)(2,1)}, bf16[576,256]{1,0:T(8,128)(2,1)S(1)}, u32[]{:S(2)}, u32[]{:S(2)}) collective-permute-start(bf16[576,256]{1,0:T(8,128)(2,1)} %get-tuple-element.17.own_w_ref), channel_id=1, source_target_pairs={{1,0},{2,1},{3,2},{4,3},{5,4},{6,5},{7,6},{8,7},{9,8},{10,9},{11,1... | collective-permute-start | bytes 884744 | tf_op jit(solution)/shard_map/ppermute | solution.py:517
  60.5 0.7 copy-start.3
  61.2 0.7 copy-start.4

commit v4 on v3

--- a/solution.py
+++ b/solution.py
@@ -106,14 +106,17 @@
     field_ref, east_ref, north_ref, level_mix_ref, fwd_ref, bwd_ref, mix_ref, *, lon, levels
 ):
     step = pl.program_id(0)
-    rows = field_ref.shape[0] // lon
-    total = rows * pl.num_programs(0)
-    for c in range(HALO):
-        for block in range(levels // 8):
-            spot = c * total + step * rows + block * 8 * GROUP
-            at = pl.ds(pl.multiple_of(spot, 16), 8 * GROUP)
-            fwd_ref[at, :] = both(field_ref, block, lon - HALO + c, lon, levels)
-            bwd_ref[at, :] = both(field_ref, block, c, lon, levels)
+    rows = GROUP * levels
+    groups = field_ref.shape[0] // (rows * lon)
+    total = rows * groups * pl.num_programs(0)
+    for group in range(groups):
+        view = field_ref.at[group * rows * lon : (group + 1) * rows * lon, :]
+        for c in range(HALO):
+            for block in range(levels // 8):
+                spot = c * total + (step * groups + group) * rows + block * 8 * GROUP
+                at = pl.ds(pl.multiple_of(spot, 16), 8 * GROUP)
+                fwd_ref[at, :] = both(view, block, lon - HALO + c, lon, levels)
+                bwd_ref[at, :] = both(view, block, c, lon, levels)
 
     @pl.when(step == 0)
     def _():
@@ -243,70 +246,117 @@
 
 
 def rim_kernel(
-    mix_ref, east_ref, north_ref, fwd_ref, bwd_ref, near_ref, out_ref, coef_ref, field_ref,
-    mixed_ref, *, lon, levels, total,
+    mix_ref, east_ref, north_ref, fwd_ref, bwd_ref, near_ref, got_ref, west_out_ref, east_out_ref,
+    coef_ref, field_ref, mixed_ref, weighted_ref, place_ref, range_ref, total_ref,
+    *, lon, levels, tracers,
 ):
-    step = pl.program_id(0)
+    total = near_ref.shape[0]
     lat = fwd_ref.shape[1]
-    rows = near_ref.shape[0]
+    rows = GROUP * levels
     wide = 3 * HALO
-
-    @pl.when(step == 0)
-    def _():
-        columns = list(range(1 - HALO, HALO + 1)) + list(range(lon - HALO - 1, lon + HALO - 1))
-        fill_coefs(
-            east_ref, north_ref, (fwd_ref, bwd_ref), coef_ref, columns, lon, levels, total
+    columns = list(range(1 - HALO, HALO + 1)) + list(range(lon - HALO - 1, lon + HALO - 1))
+    fill_coefs(east_ref, north_ref, (fwd_ref, bwd_ref), coef_ref, columns, lon, levels, total)
+
+    def group_of(group, carry):
+        for c in range(HALO):
+            at = pl.ds(pl.multiple_of(c * total + group * rows, 16), rows)
+            field_ref[:, c * lat : (c + 1) * lat] = fwd_ref[at, :]
+            e = wide + 2 * HALO + c
+            field_ref[:, e * lat : (e + 1) * lat] = bwd_ref[at, :]
+        side = 2 * HALO * lat
+        mine = pl.ds(pl.multiple_of(group * rows, 16), rows)
+        field_ref[:, HALO * lat : HALO * lat + side] = near_ref[mine, :side]
+        field_ref[:, wide * lat : wide * lat + side] = near_ref[mine, side:]
+        for half in range(2):
+            start = half * wide
+
+            def put(block, e, values):
+                spot = (e - start - HALO + half * HALO) * lat
+                for t, value in enumerate(values):
+                    row = pl.multiple_of(group * rows + block * 8 * GROUP + 8 * t, 8)
+                    total_ref[pl.ds(row, 8), spot : spot + lat] = value
+
+            two_steps(
+                mix_ref, field_ref, mixed_ref, coef_ref, start, wide, half * 2 * HALO, lat,
+                levels, put,
+            )
+        return carry
+
+    lax.fori_loop(0, total // rows, group_of, 0)
+    weigh(got_ref, weighted_ref, place_ref, range_ref, lat, levels, tracers)
+    cells = HALO * lat
+    for side, out_ref in ((0, west_out_ref), (1, east_out_ref)):
+        at = slice(side * cells, (side + 1) * cells)
+        pair = side * (lon // HALO - 1)
+        add_forcing(weighted_ref, place_ref, range_ref, total_ref, at, float(pair * cells))
+        out_ref[...] = total_ref[:, at].astype(BF16)
+
+
+def second_half_kernel(
+    mix_ref, east_hbm, north_hbm, fwd_hbm, bwd_hbm, far_w_hbm, own_w_hbm, inner_hbm, own_e_hbm,
+    far_e_hbm, out_hbm, east_ref, north_ref, fwd_ref, bwd_ref, coef_ref, field_ref, mixed_ref,
+    result_ref, side_sems, field_sems, out_sems, *, lon, levels, total,
+):
+    lat = out_hbm.shape[1]
+    rows = GROUP * levels
+    groups = total // rows
+    sides = [
+        pltpu.make_async_copy(source, target, side_sems.at[i])
+        for i, (source, target) in enumerate(
+            (
+                (east_hbm, east_ref),
+                (north_hbm, north_ref),
+                (fwd_hbm, fwd_ref),
+                (bwd_hbm, bwd_ref),
+            )
         )
-
-    for c in range(HALO):
-        at = pl.ds(pl.multiple_of(c * total + step * rows, 16), rows)
-        field_ref[:, c * lat : (c + 1) * lat] = fwd_ref[at, :]
-        e = wide + 2 * HALO + c
-        field_ref[:, e * lat : (e + 1) * lat] = bwd_ref[at, :]
-    side = 2 * HALO * lat
-    field_ref[:, HALO * lat : HALO * lat + side] = near_ref[:, :side]
-    field_ref[:, wide * lat : wide * lat + side] = near_ref[:, side:]
-    for half in range(2):
-        start = half * wide
+    ]
+
+    def pieces(group):
+        at = pl.ds(pl.multiple_of(group * rows, 16), rows)
+        copies, spot = [], 0
+        for i, ref in enumerate((far_w_hbm, own_w_hbm, inner_hbm, own_e_hbm, far_e_hbm)):
+            width = ref.shape[1]
+            target = field_ref.at[at, pl.ds(spot, width)]
+            copies.append(pltpu.make_async_copy(ref.at[at, :], target, field_sems.at[group, i]))
+            spot = spot + width
+        return copies
+
+    def leave(group):
+        at = pl.ds(pl.multiple_of(group * rows * lon, 16), rows * lon)
+        return pltpu.make_async_copy(result_ref.at[at, :], out_hbm.at[at, :], out_sems.at[group])
+
+    for copy in sides:
+        copy.start()
+    for group in range(groups):
+        for copy in pieces(group):
+            copy.start()
+    for copy in sides:
+        copy.wait()
+    columns = range(1 - HALO, lon + HALO - 1)
+    fill_coefs(east_ref, north_ref, (fwd_ref, bwd_ref), coef_ref, columns, lon, levels, total)
+
+    def group_of(group, carry):
+        for copy in pieces(group):
+            copy.wait()
+        view = field_ref.at[pl.ds(pl.multiple_of(group * rows, 16), rows), :]
+        base = pl.multiple_of(group * rows * lon, 16)
+        result = result_ref.at[pl.ds(base, rows * lon), :]
 
         def put(block, e, values):
-            spot = (e - start - HALO + half * HALO) * lat
             for t, value in enumerate(values):
-                row = block * 8 * GROUP + 8 * t
-                out_ref[row : row + 8, spot : spot + lat] = value
+                first = (t * levels + block * 8) * lon + e - HALO
+                result[pl.ds(first, 8, stride=lon), :] = value
 
         two_steps(
-            mix_ref, field_ref, mixed_ref, coef_ref, start, wide, half * 2 * HALO, lat, levels, put
+            mix_ref, view, mixed_ref, coef_ref, 0, lon + 2 * HALO, 0, lat, levels, put
         )
-
-
-def second_half_kernel(
-    mix_ref, east_ref, north_ref, fwd_ref, bwd_ref, far_w_ref, own_w_ref, inner_ref, own_e_ref,
-    far_e_ref, out_ref, coef_ref, field_ref, mixed_ref, *, lon, levels, total,
-):
-    lat = out_ref.shape[1]
-
-    @pl.when(pl.program_id(0) == 0)
-    def _():
-        columns = range(1 - HALO, lon + HALO - 1)
-        fill_coefs(
-            east_ref, north_ref, (fwd_ref, bwd_ref), coef_ref, columns, lon, levels, total
-        )
-
-    spot = 0
-    for ref in (far_w_ref, own_w_ref, inner_ref, own_e_ref, far_e_ref):
-        width = ref.shape[-1]
-        field_ref[:, spot : spot + width] = ref[...]
-        spot = spot + width
-
-    def put(block, e, values):
-        for t, value in enumerate(values):
-            first = (t * levels + block * 8) * lon + e - HALO
-            out_ref[pl.ds(first, 8, stride=lon), :] = value
-
-    two_steps(
-        mix_ref, field_ref, mixed_ref, coef_ref, 0, lon + 2 * HALO, 0, lat, levels, put
-    )
+        leave(group).start()
+        return carry
+
+    lax.fori_loop(0, groups, group_of, 0)
+    for group in range(groups):
+        leave(group).wait()
 
 
 def regions_of(capacity):
@@ -329,42 +379,38 @@
             store(spot + tiles * 64, jnp.where(low, pltpu.roll(one, 64, 1), two))
 
 
-def forcing(
-    got_ref, field_ref, weighted_ref, place_ref, range_ref, total_ref, step, pair,
-    *, lat, levels, tracers,
-):
+def weigh(got_ref, weighted_ref, place_ref, range_ref, lat, levels, tracers):
     tiles, _, capacity = got_ref.shape
-    cells = HALO * lat
     parts = regions_of(capacity)
     wide = tiles * capacity // parts
 
-    @pl.when(step == 0)
-    def _():
-        def store(spot, got):
-            at = slice(spot, spot + got.shape[1])
-            row = 0
-            for t in range(0, tracers, GROUP):
-                for block in range(0, levels, 8):
-                    kernel = got[block : block + 8]
-                    pieces = [
-                        kernel * got[levels + j : levels + j + 1, :] for j in range(t, t + GROUP)
-                    ]
-                    value = jnp.concatenate(pieces, axis=0).astype(BF16)
-                    weighted_ref[row : row + 8 * GROUP, at] = value
-                    row = row + 8 * GROUP
-            first = levels + tracers
-            column = (got[first : first + 1, :] - 1.0) * lat + got[first + 1 : first + 2, :]
-            place_ref[:, at] = jnp.broadcast_to(column, (8, got.shape[1]))
-
-        regroup(got_ref, store)
-        for part in range(parts):
-            place = place_ref[:, part * wide : (part + 1) * wide]
-            far = 1e6
-            range_ref[2 * part] = jnp.min(jnp.where(place < 0.0, far, place))
-            range_ref[2 * part + 1] = jnp.max(place)
-
-    total_ref[...] = field_ref[...]
-    offset = (pair * cells).astype(F32)
+    def store(spot, got):
+        at = slice(spot, spot + got.shape[1])
+        row = 0
+        for t in range(0, tracers, GROUP):
+            for block in range(0, levels, 8):
+                kernel = got[block : block + 8]
+                pieces = [
+                    kernel * got[levels + j : levels + j + 1, :] for j in range(t, t + GROUP)
+                ]
+                value = jnp.concatenate(pieces, axis=0).astype(BF16)
+                weighted_ref[row : row + 8 * GROUP, at] = value
+                row = row + 8 * GROUP
+        first = levels + tracers
+        column = (got[first : first + 1, :] - 1.0) * lat + got[first + 1 : first + 2, :]
+        place_ref[:, at] = jnp.broadcast_to(column, (8, got.shape[1]))
+
+    regroup(got_ref, store)
+    for part in range(parts):
+        place = place_ref[:, part * wide : (part + 1) * wide]
+        range_ref[2 * part] = jnp.min(jnp.where(place < 0.0, 1e6, place))
+        range_ref[2 * part + 1] = jnp.max(place)
+
+
+def add_forcing(weighted_ref, place_ref, range_ref, total_ref, columns, offset):
+    cells = total_ref[:, columns].shape[1]
+    parts = range_ref.shape[0] // 2
+    wide = weighted_ref.shape[1] // parts
     for part in range(parts):
         held = (range_ref[2 * part] < offset + cells) & (range_ref[2 * part + 1] >= offset)
 
@@ -375,27 +421,44 @@
             cell = lax.broadcasted_iota(jnp.int32, (cells, wide), 0).astype(F32).astype(BF16)
             hit = cell == stacked(key, cells // 16)
             one_hot = jnp.where(hit, jnp.ones_like(cell), jnp.zeros_like(cell))
-            total_ref[...] += nt_dot(weighted_ref[:, at], one_hot)
-
-    return total_ref[...].astype(BF16)
-
-
-def forcing_inner_kernel(got_ref, field_ref, out_ref, *scratch, **sizes):
-    step = pl.program_id(0)
-    out_ref[...] = forcing(got_ref, field_ref, *scratch, step, step + 1, **sizes)
-
-
-def forcing_rim_kernel(got_ref, field_ref, west_ref, east_ref, *scratch, pairs, **sizes):
-    step = pl.program_id(0)
-    value = forcing(got_ref, field_ref, *scratch, step, step * (pairs - 1), **sizes)
-
-    @pl.when(step == 0)
-    def _():
-        west_ref[...] = value
-
-    @pl.when(step == 1)
-    def _():
-        east_ref[...] = value
+            total_ref[:, columns] += nt_dot(weighted_ref[:, at], one_hot)
+
+
+def forcing_inner_kernel(
+    got_ref, field_hbm, out_hbm, weighted_ref, place_ref, range_ref, total_ref, rounded_ref,
+    in_sems, out_sems, *, lat, levels, tracers,
+):
+    cells = HALO * lat
+    count = field_hbm.shape[1] // cells
+
+    def at(i):
+        return pl.ds(pl.multiple_of(i * cells, cells), cells)
+
+    def enter(i):
+        return pltpu.make_async_copy(
+            field_hbm.at[:, at(i)], total_ref.at[:, at(i)], in_sems.at[i]
+        )
+
+    def leave(i):
+        return pltpu.make_async_copy(
+            rounded_ref.at[:, at(i)], out_hbm.at[:, at(i)], out_sems.at[i]
+        )
+
+    for i in range(count):
+        enter(i).start()
+    weigh(got_ref, weighted_ref, place_ref, range_ref, lat, levels, tracers)
+
+    def pair_of(i, carry):
+        enter(i).wait()
+        offset = ((i + 1) * cells).astype(F32)
+        add_forcing(weighted_ref, place_ref, range_ref, total_ref, at(i), offset)
+        rounded_ref[:, at(i)] = total_ref[:, at(i)].astype(BF16)
+        leave(i).start()
+        return carry
+
+    lax.fori_loop(0, count, pair_of, 0)
+    for i in range(count):
+        leave(i).wait()
 
 
 def per_device(
@@ -437,9 +500,9 @@
     whole = lambda *shape: pl.BlockSpec(shape, lambda i: (0,) * len(shape))
     fwd, bwd, mix = pl.pallas_call(
         functools.partial(edge_kernel, lon=lon, levels=levels),
-        grid=(steps,),
+        grid=(2,),
         in_specs=[
-            pl.BlockSpec((rows * lon, lat), lambda i: (i, 0)),
+            pl.BlockSpec((total * lon // 2, lat), lambda i: (i, 0)),
             whole(levels * lon, lat),
             whole(levels * lon, lat),
             whole(levels, levels),
@@ -466,7 +529,6 @@
     strip = lambda width: pl.BlockSpec((rows, width), lambda i: (i, 0))
     cells = HALO * lat
     fixed_specs = [whole(rows, rows), whole(levels * lon, lat), whole(levels * lon, lat)]
-    edge_specs = [whole(fwd_rows, lat), whole(bwd_rows, lat)]
     inner_width = (lon - 2 * HALO) * lat
     middle, near = pl.pallas_call(
         functools.partial(inner_kernel, lon=lon, levels=levels),
@@ -481,60 +543,69 @@
         compiler_params=params(),
         name="first_half_inner",
     )(mix, east, north, field)
-    rim = pl.pallas_call(
-        functools.partial(rim_kernel, lon=lon, levels=levels, total=total),
-        grid=(steps,),
-        in_specs=fixed_specs + edge_specs + [strip(4 * cells)],
-        out_specs=strip(2 * cells),
-        out_shape=jax.ShapeDtypeStruct((total, 2 * cells), F32),
-        scratch_shapes=scratch(6 * HALO, 4 * HALO),
-        compiler_params=params(),
-        name="first_half_rim",
-    )(mix, east, north, fwd, bwd, near)
-
-    sizes = dict(lat=lat, levels=levels, tracers=tracers)
-    forcing_specs = [
-        whole(tiles, height, capacity),
-        pl.BlockSpec((total, cells), lambda i: (0, i)),
-    ]
+    whole1 = lambda *shape: pl.BlockSpec(shape, lambda: (0,) * len(shape))
+    far = pl.BlockSpec(memory_space=pltpu.MemorySpace.HBM)
     forcing_scratch = [
         pltpu.VMEM((total, slots), BF16),
         pltpu.VMEM((8, slots), F32),
         pltpu.SMEM((2 * regions_of(capacity),), F32),
-        pltpu.VMEM((total, cells), F32),
     ]
     own_w, own_e = pl.pallas_call(
-        functools.partial(forcing_rim_kernel, pairs=pairs, **sizes),
-        grid=(2,),
-        in_specs=forcing_specs,
-        out_specs=[whole(total, cells), whole(total, cells)],
+        functools.partial(rim_kernel, lon=lon, levels=levels, tracers=tracers),
+        in_specs=[
+            whole1(rows, rows),
+            whole1(levels * lon, lat),
+            whole1(levels * lon, lat),
+            whole1(fwd_rows, lat),
+            whole1(bwd_rows, lat),
+            whole1(total, 4 * cells),
+            whole1(tiles, height, capacity),
+        ],
+        out_specs=[whole1(total, cells), whole1(total, cells)],
         out_shape=[jax.ShapeDtypeStruct((total, cells), BF16)] * 2,
-        scratch_shapes=forcing_scratch,
+        scratch_shapes=scratch(6 * HALO, 4 * HALO)
+        + forcing_scratch
+        + [pltpu.VMEM((total, 2 * cells), F32)],
         compiler_params=params(),
-        name="forcing_rim",
-    )(got, rim)
+        name="rim",
+    )(mix, east, north, fwd, bwd, near, got)
     far_w = lax.ppermute(own_e, "tile", ring)
     far_e = lax.ppermute(own_w, "tile", back)
     inner = pl.pallas_call(
-        functools.partial(forcing_inner_kernel, **sizes),
-        grid=(pairs - 2,),
-        in_specs=forcing_specs,
-        out_specs=pl.BlockSpec((total, cells), lambda i: (0, i)),
+        functools.partial(forcing_inner_kernel, lat=lat, levels=levels, tracers=tracers),
+        in_specs=[whole1(tiles, height, capacity), far],
+        out_specs=far,
         out_shape=jax.ShapeDtypeStruct((total, inner_width), BF16),
-        scratch_shapes=forcing_scratch,
+        scratch_shapes=forcing_scratch
+        + [
+            pltpu.VMEM((total, inner_width), F32),
+            pltpu.VMEM((total, inner_width), BF16),
+            pltpu.SemaphoreType.DMA((pairs - 2,)),
+            pltpu.SemaphoreType.DMA((pairs - 2,)),
+        ],
         compiler_params=params(),
         name="forcing_inner",
     )(got, middle)
 
+    coefs, fields, mixed = scratch(lon + 2 * HALO, lon + 2 * HALO - 2)
     out = pl.pallas_call(
         functools.partial(second_half_kernel, lon=lon, levels=levels, total=total),
-        grid=(steps,),
-        in_specs=fixed_specs
-        + edge_specs
-        + [strip(cells), strip(cells), strip(inner_width), strip(cells), strip(cells)],
-        out_specs=pl.BlockSpec((rows * lon, lat), lambda i: (i, 0)),
+        in_specs=[whole1(rows, rows)] + [far] * 9,
+        out_specs=far,
         out_shape=jax.ShapeDtypeStruct((total * lon, lat), F32),
-        scratch_shapes=scratch(lon + 2 * HALO, lon + 2 * HALO - 2),
+        scratch_shapes=[
+            pltpu.VMEM((levels * lon, lat), F32),
+            pltpu.VMEM((levels * lon, lat), F32),
+            pltpu.VMEM((fwd_rows, lat), BF16),
+            pltpu.VMEM((bwd_rows, lat), BF16),
+            coefs,
+            pltpu.VMEM((total, (lon + 2 * HALO) * lat), BF16),
+            mixed,
+            pltpu.VMEM((total * lon, lat), F32),
+            pltpu.SemaphoreType.DMA((4,)),
+            pltpu.SemaphoreType.DMA((steps, 5)),
+            pltpu.SemaphoreType.DMA((steps,)),
+        ],
         compiler_params=params(),
         name="second_half",
     )(mix, east, north, fwd, bwd, far_w, own_w, inner, own_e, far_e)

time: 73.4 us -> 71.2 us (0.970)
  Pallas kernels: 51.6 us -> 49 us
  waiting for transfers between devices: 2.02 us -> 2.93 us
    pallas_call x3 -> x2, Pallas kernels: 20.3 us -> 17.1 us  [the longest x1 10.1 us: per_device(): pl.pallas_call(functools.partial(rim_kernel, lon=lon, levels=levels, trac...]
    pallas_call x1, Pallas kernels: 11 us -> 12.5 us  [per_device(): pl.pallas_call(functools.partial(second_half_kernel, lon=lon, levels=leve...]
    pallas_call x1, Pallas kernels: 4.76 us -> 3.84 us  [per_device(): pl.pallas_call(functools.partial(edge_kernel, lon=lon, levels=levels), gr...]
    ppermute x1, waiting for transfers between devices: 2.01 us -> 2.92 us  [per_device(): fwd = lax.ppermute(fwd, 'tile', ring)]
  transfers between devices with their start and end apart: 5 -> 5, of which waited for: 1 -> 1; matrix products, arithmetic and copies ran while one was open for 0% -> 0% of each run, Pallas kernels for 42% -> 30%
where the time goes in v4:
time: 71.2 us; the launch traced here: 70.8 us
  Pallas kernels  49 us (69%)
  starting transfers between devices  16.3 us (23%)
  waiting for transfers between devices  2.93 us (4%)
  local copies, waits for them, and re-layouts  2.37 us (3%)
    pallas_call x1, Pallas kernels, per_device(): pl.pallas_call(functools.partial(second_half_kernel, lon=lon, levels=leve...  12.5 us
    pallas_call x1, Pallas kernels, per_device(): pl.pallas_call(functools.partial(inner_kernel, lon=lon, levels=levels), g...  10.3 us
    pallas_call x1, Pallas kernels, per_device(): pl.pallas_call(functools.partial(rim_kernel, lon=lon, levels=levels, trac...  10.1 us
    all_to_all x1, starting transfers between devices, per_device(): lax.all_to_all(payload, 'tile', split_axis=0, concat_axis=0, tiled=True)  7.39 us
    pallas_call x1, Pallas kernels, per_device(): pl.pallas_call(functools.partial(forcing_inner_kernel, lat=lat, levels=le...  7 us
    pallas_call x1, Pallas kernels, per_device(): pl.pallas_call(functools.partial(pack_kernel, tiles=tiles, capacity=capac...  5.33 us
    ppermute x1, starting transfers between devices, per_device(): far_e = lax.ppermute(own_w, 'tile', back)  4.39 us
    ppermute x1, starting transfers between devices, per_device(): bwd = lax.ppermute(bwd, 'tile', back)  4.04 us
  transfers between devices with their start and end apart: 5, of which 1 were waited for; matrix products, arithmetic and copies ran while one was open for 0% of the time, Pallas kernels for 30%

profile of v4, /device:TPU:0, one launch (start us, length us, event | category | flops | bytes accessed | tf_op | source)
XLA Modules:
  0.0 70.8 jit_solution(15775564981653026243)
XLA Ops:
  0.0 5.3 %pack.1 = bf16[16,88,256]{2,1,0:T(8,128)(2,1)} custom-call(bf16[72,1024]{1,0:T(8,128)(2,1)} %kernel_ref.1, bf16[8,1024]{1,0:T(8,128)(2,1)} %weight_ref.1, s32[1,1024]{1,0:T(1,128)} %bitcast.15, s32[1,1024]{1,0:T(1,128)} %column_ref.1), custom_call_target="tpu_custom_call" | custom-call | tf_op jit(solution)/shard_map/pack/pallas_call | solution.py:490
  5.3 7.4 %all-to-all-start = ((bf16[16,88,256]{2,1,0:T(8,128)(2,1)}), bf16[16,88,256]{2,1,0:T(8,128)(2,1)S(1)}, u32[]{:S(2)}, u32[]{:S(2)}) async-start(bf16[16,88,256]{2,1,0:T(8,128)(2,1)} %pack.1), calls=%async_computation | async-start | bytes 1441792 | tf_op jit(solution)/shard_map/all_to_all | solution.py:496
  12.7 3.8 %edges.1 = (bf16[1392,128]{1,0:T(8,128)(2,1)}, bf16[1312,128]{1,0:T(8,128)(2,1)}, bf16[144,144]{1,0:T(8,128)(2,1)}) custom-call(f32[9216,128]{1,0:T(8,128)} %bitcast.5, f32[1152,128]{1,0:T(8,128)} %bitcast.7, f32[1152,128]{1,0:T(8,128)} %bitcast.11, bf16[72,72]{1,0:T(8,128)(2,1)} %level_mix_ref.1), custom_call_target="tpu_custom_call" | custom-call | tf_op jit(solution)/shard_map/edges/pallas_call | solution.py:501
  16.6 0.4 collective-permute-start
  17.0 4.0 %collective-permute-start.1 = (bf16[1312,128]{1,0:T(8,128)(2,1)}, bf16[1312,128]{1,0:T(8,128)(2,1)S(1)}, u32[]{:S(2)}, u32[]{:S(2)}) collective-permute-start(bf16[1312,128]{1,0:T(8,128)(2,1)} %get-tuple-element.14), channel_id=1, source_target_pairs={{1,0},{2,1},{3,2},{4,3},{5,4},{6,5},{7,6},{8,7},{9,8},{10,9},{11,1... | collective-permute-start | bytes 1007624 | tf_op jit(solution)/shard_map/ppermute | solution.py:520
  21.0 10.3 %first_half_inner.1 = (f32[576,1536]{1,0:T(8,128)}, bf16[576,1024]{1,0:T(8,128)(2,1)}) custom-call(bf16[144,144]{1,0:T(8,128)(2,1)} %get-tuple-element.12.mix_ref, f32[1152,128]{1,0:T(8,128)} %bitcast.8, f32[1152,128]{1,0:T(8,128)} %bitcast.12, f32[9216,128]{1,0:T(8,128)} %bitcast.6), custom_call_target="tpu_custom_call" | custom-call | tf_op jit(solution)/shard_map/first_half_inner/pallas_call | solution.py:533
  31.3 0.0 collective-permute-done.1.bwd_ref.bwd_hbm
  31.3 0.0 copy-start.2
  31.3 2.9 %collective-permute-done.fwd_ref.fwd_hbm = bf16[1392,128]{1,0:T(8,128)(2,1)S(1)} collective-permute-done((bf16[1392,128]{1,0:T(8,128)(2,1)}, bf16[1392,128]{1,0:T(8,128)(2,1)S(1)}, u32[]{:S(2)}, u32[]{:S(2)}) %collective-permute-start) | collective-permute-done | bytes 356384 | tf_op jit(solution)/shard_map/ppermute | solution.py:519
  34.2 0.0 copy-start.1
  34.2 0.0 all-to-all-done.got_ref
  34.2 0.0 copy-start
  34.2 0.0 copy-done.2
  34.2 0.7 %copy-done.1 = bf16[1392,128]{1,0:T(8,128)(2,1)} copy-done((bf16[1392,128]{1,0:T(8,128)(2,1)}, bf16[1392,128]{1,0:T(8,128)(2,1)S(1)}, u32[]{:S(2)}) %copy-start.1) | copy-done | bytes 356376
  34.9 0.2 copy-done
  35.2 10.1 %rim.1 = (bf16[576,256]{1,0:T(8,128)(2,1)}, bf16[576,256]{1,0:T(8,128)(2,1)}) custom-call(bf16[144,144]{1,0:T(8,128)(2,1)} %get-tuple-element.12.mix_ref, f32[1152,128]{1,0:T(8,128)} %bitcast.9, f32[1152,128]{1,0:T(8,128)} %bitcast.13, bf16[1392,128]{1,0:T(8,128)(2,1)} %copy-done.1, bf16[1312,128]{1,0:T(8,128)(2,1)} %copy-done.2, ...), custom_call_target="tpu_custom_call" | custom-call | tf_op jit(solution)/shard_map/rim/pallas_call | solution.py:553
  45.3 0.1 collective-permute-start.2
  45.3 4.4 %collective-permute-start.3 = (bf16[576,256]{1,0:T(8,128)(2,1)}, bf16[576,256]{1,0:T(8,128)(2,1)S(1)}, u32[]{:S(2)}, u32[]{:S(2)}) collective-permute-start(bf16[576,256]{1,0:T(8,128)(2,1)} %get-tuple-element.17.own_w_hbm), channel_id=1, source_target_pairs={{1,0},{2,1},{3,2},{4,3},{5,4},{6,5},{7,6},{8,7},{9,8},{10,9},{11,1... | collective-permute-start | bytes 884744 | tf_op jit(solution)/shard_map/ppermute | solution.py:573
  49.7 7.0 %forcing_inner.1.inner_hbm = bf16[576,1536]{1,0:T(8,128)(2,1)} custom-call(bf16[16,88,256]{2,1,0:T(8,128)(2,1)} %copy-done, f32[576,1536]{1,0:T(8,128)} %get-tuple-element.18.field_hbm), custom_call_target="tpu_custom_call" | custom-call | tf_op jit(solution)/shard_map/forcing_inner/pallas_call | solution.py:574
  56.7 0.0 collective-permute-done.2.far_w_hbm
  56.7 0.0 copy-start.3
  56.7 0.0 collective-permute-done.3.far_e_hbm
  56.7 0.7 copy-done.3
  57.5 0.0 copy-start.4
  57.5 0.7 copy-done.4
  58.2 12.5 %second_half.1 = f32[9216,128]{1,0:T(8,128)} custom-call(bf16[144,144]{1,0:T(8,128)(2,1)} %get-tuple-element.12.mix_ref, f32[1152,128]{1,0:T(8,128)} %bitcast.10, f32[1152,128]{1,0:T(8,128)} %bitcast.14, bf16[1392,128]{1,0:T(8,128)(2,1)} %copy-done.1, bf16[1312,128]{1,0:T(8,128)(2,1)} %copy-done.2, bf16[576,256]{1,0:T(8,128)(2,1)} %copy-done.3, ...), custom_call_target="tpu_custom_call" | custom-call | tf_op jit(solution)/shard_map/second_half/pallas_call | solution.py:591
Async XLA Ops:
  5.3 28.9 %all-to-all-start = ((bf16[16,88,256]{2,1,0:T(8,128)(2,1)}), bf16[16,88,256]{2,1,0:T(8,128)(2,1)S(1)}, u32[]{:S(2)}, u32[]{:S(2)}) async-start(bf16[16,88,256]{2,1,0:T(8,128)(2,1)} %pack.1), calls=%async_computation | async-start | bytes 1441792 | tf_op jit(solution)/shard_map/all_to_all | solution.py:496
  16.6 17.6 %collective-permute-start = (bf16[1392,128]{1,0:T(8,128)(2,1)}, bf16[1392,128]{1,0:T(8,128)(2,1)S(1)}, u32[]{:S(2)}, u32[]{:S(2)}) collective-permute-start(bf16[1392,128]{1,0:T(8,128)(2,1)} %get-tuple-element.13), channel_id=1, source_target_pairs={{0,1},{1,2},{2,3},{3,4},{4,5},{5,6},{6,7},{7,8},{8,9},{9,10},{10,1... | collective-permute-start | bytes 1069064 | tf_op jit(solution)/shard_map/ppermute | solution.py:519
  17.0 14.3 %collective-permute-start.1 = (bf16[1312,128]{1,0:T(8,128)(2,1)}, bf16[1312,128]{1,0:T(8,128)(2,1)S(1)}, u32[]{:S(2)}, u32[]{:S(2)}) collective-permute-start(bf16[1312,128]{1,0:T(8,128)(2,1)} %get-tuple-element.14), channel_id=1, source_target_pairs={{1,0},{2,1},{3,2},{4,3},{5,4},{6,5},{7,6},{8,7},{9,8},{10,9},{11,1... | collective-permute-start | bytes 1007624 | tf_op jit(solution)/shard_map/ppermute | solution.py:520
  31.3 2.9 %copy-start.2 = (bf16[1312,128]{1,0:T(8,128)(2,1)}, bf16[1312,128]{1,0:T(8,128)(2,1)S(1)}, u32[]{:S(2)}) copy-start(bf16[1312,128]{1,0:T(8,128)(2,1)S(1)} %collective-permute-done.1.bwd_ref.bwd_hbm) | copy-start | bytes 1007620
  34.2 0.8 %copy-start.1 = (bf16[1392,128]{1,0:T(8,128)(2,1)}, bf16[1392,128]{1,0:T(8,128)(2,1)S(1)}, u32[]{:S(2)}) copy-start(bf16[1392,128]{1,0:T(8,128)(2,1)S(1)} %collective-permute-done.fwd_ref.fwd_hbm) | copy-start | bytes 1069060
  34.2 1.0 %copy-start = (bf16[16,88,256]{2,1,0:T(8,128)(2,1)}, bf16[16,88,256]{2,1,0:T(8,128)(2,1)S(1)}, u32[]{:S(2)}) copy-start(bf16[16,88,256]{2,1,0:T(8,128)(2,1)S(1)} %all-to-all-done.got_ref) | copy-start | bytes 2162692
  45.3 11.5 %collective-permute-start.2 = (bf16[576,256]{1,0:T(8,128)(2,1)}, bf16[576,256]{1,0:T(8,128)(2,1)S(1)}, u32[]{:S(2)}, u32[]{:S(2)}) collective-permute-start(bf16[576,256]{1,0:T(8,128)(2,1)} %get-tuple-element.16.own_e_hbm), channel_id=1, source_target_pairs={{0,1},{1,2},{2,3},{3,4},{4,5},{5,6},{6,7},{7,8},{8,9},{9,10},{10,1... | collective-permute-start | bytes 884744 | tf_op jit(solution)/shard_map/ppermute | solution.py:572
  45.3 11.4 %collective-permute-start.3 = (bf16[576,256]{1,0:T(8,128)(2,1)}, bf16[576,256]{1,0:T(8,128)(2,1)S(1)}, u32[]{:S(2)}, u32[]{:S(2)}) collective-permute-start(bf16[576,256]{1,0:T(8,128)(2,1)} %get-tuple-element.17.own_w_hbm), channel_id=1, source_target_pairs={{1,0},{2,1},{3,2},{4,3},{5,4},{6,5},{7,6},{8,7},{9,8},{10,9},{11,1... | collective-permute-start | bytes 884744 | tf_op jit(solution)/shard_map/ppermute | solution.py:573
  56.7 0.7 %copy-start.3 = (bf16[576,256]{1,0:T(8,128)(2,1)}, bf16[576,256]{1,0:T(8,128)(2,1)S(1)}, u32[]{:S(2)}) copy-start(bf16[576,256]{1,0:T(8,128)(2,1)S(1)} %collective-permute-done.2.far_w_hbm) | copy-start | bytes 884740
  57.5 0.7 copy-start.4

commit v5 on v4

--- a/solution.py
+++ b/solution.py
@@ -11,11 +11,20 @@
 BF16 = jnp.bfloat16
 GROUP = 2
 HALO = 2
-VMEM = 56 * 1024 * 1024
+VMEM_BYTES = 20 * 1024 * 1024
+VMEM = pltpu.MemorySpace.VMEM
 
 
 def params(**more):
-    return pltpu.CompilerParams(vmem_limit_bytes=VMEM, **more)
+    return pltpu.CompilerParams(vmem_limit_bytes=VMEM_BYTES, **more)
+
+
+def near_by(*arrays):
+    return [pltpu.with_memory_space_constraint(array, VMEM) for array in arrays]
+
+
+def away(array):
+    return pltpu.with_memory_space_constraint(array, pltpu.MemorySpace.HBM)
 
 
 def nt_dot(a, b):
@@ -105,41 +114,36 @@
 def edge_kernel(
     field_ref, east_ref, north_ref, level_mix_ref, fwd_ref, bwd_ref, mix_ref, *, lon, levels
 ):
-    step = pl.program_id(0)
     rows = GROUP * levels
-    groups = field_ref.shape[0] // (rows * lon)
-    total = rows * groups * pl.num_programs(0)
-    for group in range(groups):
+    total = field_ref.shape[0] // lon
+    for group in range(total // rows):
         view = field_ref.at[group * rows * lon : (group + 1) * rows * lon, :]
         for c in range(HALO):
             for block in range(levels // 8):
-                spot = c * total + (step * groups + group) * rows + block * 8 * GROUP
-                at = pl.ds(pl.multiple_of(spot, 16), 8 * GROUP)
+                spot = c * total + group * rows + block * 8 * GROUP
+                at = slice(spot, spot + 8 * GROUP)
                 fwd_ref[at, :] = both(view, block, lon - HALO + c, lon, levels)
                 bwd_ref[at, :] = both(view, block, c, lon, levels)
 
-    @pl.when(step == 0)
-    def _():
-        def put(out, place, ref, x):
-            spot = HALO * total + place * (levels + 8)
-            value = ref[pl.ds(x, levels, stride=lon), :]
-            value = jnp.concatenate([value, jnp.zeros((8, value.shape[1]), F32)], axis=0)
-            out[spot : spot + levels + 8, :] = value.astype(BF16)
-
-        put(fwd_ref, 0, east_ref, lon - 2)
-        put(fwd_ref, 1, east_ref, lon - 1)
-        put(fwd_ref, 2, north_ref, lon - 1)
-        put(bwd_ref, 0, east_ref, 0)
-        put(bwd_ref, 1, north_ref, 0)
-        rows = GROUP * levels
-        row = lax.broadcasted_iota(jnp.int32, (rows, levels), 0)
-        level = row // (8 * GROUP) * 8 + row % 8
-        mine = level == lax.broadcasted_iota(jnp.int32, (rows, levels), 1)
-        mix = jnp.zeros((rows, rows), F32)
-        for t in range(GROUP):
-            pick = (mine & (row // 8 % GROUP == t)).astype(F32).astype(BF16)
-            mix = mix + nt_dot(nt_dot(pick, level_mix_ref[...]).astype(BF16), pick)
-        mix_ref[...] = mix.astype(BF16)
+    def put(out, place, ref, x):
+        spot = HALO * total + place * (levels + 8)
+        value = ref[pl.ds(x, levels, stride=lon), :]
+        value = jnp.concatenate([value, jnp.zeros((8, value.shape[1]), F32)], axis=0)
+        out[spot : spot + levels + 8, :] = value.astype(BF16)
+
+    put(fwd_ref, 0, east_ref, lon - 2)
+    put(fwd_ref, 1, east_ref, lon - 1)
+    put(fwd_ref, 2, north_ref, lon - 1)
+    put(bwd_ref, 0, east_ref, 0)
+    put(bwd_ref, 1, north_ref, 0)
+    row = lax.broadcasted_iota(jnp.int32, (rows, levels), 0)
+    level = row // (8 * GROUP) * 8 + row % 8
+    mine = level == lax.broadcasted_iota(jnp.int32, (rows, levels), 1)
+    mix = jnp.zeros((rows, rows), F32)
+    for t in range(GROUP):
+        pick = (mine & (row // 8 % GROUP == t)).astype(F32).astype(BF16)
+        mix = mix + nt_dot(nt_dot(pick, level_mix_ref[...]).astype(BF16), pick)
+    mix_ref[...] = mix.astype(BF16)
 
 
 def fill_coefs(east_ref, north_ref, edges, coef_ref, columns, lon, levels, total):
@@ -178,7 +182,7 @@
         coef_ref[4, :, at] = -to_south
 
 
-def stencil(mixed_ref, coef_ref, start, count, coef_start, lat, levels, emit):
+def stencil(mixed_ref, coef, start, count, lat, levels, emit):
     def column(e):
         return slice(e * lat, (e + 1) * lat)
 
@@ -190,8 +194,7 @@
         left = [mixed_ref[r, column(start - 1)] for r in tracer_rows]
         centre = [mixed_ref[r, column(start)] for r in tracer_rows]
         for e in range(start, start + count):
-            at = column(coef_start + e - start)
-            factor = [coef_ref[j, lines, at] for j in range(5)]
+            factor = [coef(j, lines, e) for j in range(5)]
             values = []
             for t, r in enumerate(tracer_rows):
                 right = mixed_ref[r, column(e + 1)]
@@ -203,7 +206,7 @@
             emit(block, e, values)
 
 
-def two_steps(mix_ref, field_ref, mixed_ref, coef_ref, start, count, coef_start, lat, levels, put):
+def two_steps(mix_ref, field_ref, mixed_ref, coef, start, count, lat, levels, put):
     def mix(lo, hi):
         for e in range(lo, hi, 2):
             at = slice(e * lat, (e + 2) * lat)
@@ -214,40 +217,59 @@
         field_ref[at, e * lat : (e + 1) * lat] = jnp.concatenate(values, axis=0).astype(BF16)
 
     mix(start, start + count)
-    stencil(mixed_ref, coef_ref, start + 1, count - 2, coef_start, lat, levels, keep)
+    stencil(mixed_ref, coef, start + 1, count - 2, lat, levels, keep)
     mix(start + 1, start + count - 1)
-    stencil(mixed_ref, coef_ref, start + 2, count - 4, coef_start + 1, lat, levels, put)
+    stencil(mixed_ref, coef, start + 2, count - 4, lat, levels, put)
+
+
+def factors(coef_ref, lat, place_of):
+    def coef(j, lines, e):
+        place = place_of(e)
+        return coef_ref[j, lines, place * lat : (place + 1) * lat]
+
+    return coef
 
 
 def inner_kernel(
-    mix_ref, east_ref, north_ref, in_ref, out_ref, near_ref, coef_ref, field_ref, mixed_ref,
-    *, lon, levels,
+    mix_ref, east_ref, north_ref, in_ref, out_ref, near_ref, coef_hbm, coef_ref, field_ref,
+    mixed_ref, coef_sem, *, lon, levels,
 ):
     lat = in_ref.shape[1]
-
-    @pl.when(pl.program_id(0) == 0)
+    rows = GROUP * levels
+    step = pl.program_id(0)
+    base = pl.multiple_of(step * rows * lon, 16)
+    source = in_ref.at[pl.ds(base, rows * lon), :]
+
+    @pl.when(step == 0)
     def _():
         fill_coefs(east_ref, north_ref, None, coef_ref, range(1, lon - 1), lon, levels, 0)
+        pltpu.make_async_copy(coef_ref, coef_hbm, coef_sem).start()
 
     for x in range(lon):
         for block in range(levels // 8):
             at = slice(block * 8 * GROUP, (block + 1) * 8 * GROUP)
-            field_ref[at, x * lat : (x + 1) * lat] = both(in_ref, block, x, lon, levels)
+            field_ref[at, x * lat : (x + 1) * lat] = both(source, block, x, lon, levels)
     side = 2 * HALO * lat
-    near_ref[:, :side] = field_ref[:, :side]
-    near_ref[:, side:] = field_ref[:, lon * lat - side :]
+    mine = pl.ds(pl.multiple_of(step * rows, 16), rows)
+    near_ref[mine, :side] = field_ref[:, :side]
+    near_ref[mine, side:] = field_ref[:, lon * lat - side :]
 
     def put(block, e, values):
         for t, value in enumerate(values):
             row = block * 8 * GROUP + 8 * t
             out_ref[row : row + 8, (e - HALO) * lat : (e - HALO + 1) * lat] = value
 
-    two_steps(mix_ref, field_ref, mixed_ref, coef_ref, 0, lon, 0, lat, levels, put)
+    coef = factors(coef_ref, lat, lambda e: e - 1)
+    two_steps(mix_ref, field_ref, mixed_ref, coef, 0, lon, lat, levels, put)
+
+    @pl.when(step == pl.num_programs(0) - 1)
+    def _():
+        pltpu.make_async_copy(coef_ref, coef_hbm, coef_sem).wait()
 
 
 def rim_kernel(
     mix_ref, east_ref, north_ref, fwd_ref, bwd_ref, near_ref, got_ref, west_out_ref, east_out_ref,
-    coef_ref, field_ref, mixed_ref, weighted_ref, place_ref, range_ref, total_ref,
+    coef_ref, weighted_ref, place_ref, field_ref, mixed_ref, range_ref, total_ref,
     *, lon, levels, tracers,
 ):
     total = near_ref.shape[0]
@@ -276,10 +298,8 @@
                     row = pl.multiple_of(group * rows + block * 8 * GROUP + 8 * t, 8)
                     total_ref[pl.ds(row, 8), spot : spot + lat] = value
 
-            two_steps(
-                mix_ref, field_ref, mixed_ref, coef_ref, start, wide, half * 2 * HALO, lat,
-                levels, put,
-            )
+            coef = factors(coef_ref, lat, lambda e: e - start - 1 + half * 2 * HALO)
+            two_steps(mix_ref, field_ref, mixed_ref, coef, start, wide, lat, levels, put)
         return carry
 
     lax.fori_loop(0, total // rows, group_of, 0)
@@ -293,53 +313,34 @@
 
 
 def second_half_kernel(
-    mix_ref, east_hbm, north_hbm, fwd_hbm, bwd_hbm, far_w_hbm, own_w_hbm, inner_hbm, own_e_hbm,
-    far_e_hbm, out_hbm, east_ref, north_ref, fwd_ref, bwd_ref, coef_ref, field_ref, mixed_ref,
-    result_ref, side_sems, field_sems, out_sems, *, lon, levels, total,
+    mix_ref, inner_coef_ref, rim_coef_ref, far_w_ref, own_w_ref, inner_ref, own_e_ref, far_e_ref,
+    out_hbm, field_ref, mixed_ref, result_ref, out_sems, *, lon, levels,
 ):
     lat = out_hbm.shape[1]
     rows = GROUP * levels
-    groups = total // rows
-    sides = [
-        pltpu.make_async_copy(source, target, side_sems.at[i])
-        for i, (source, target) in enumerate(
-            (
-                (east_hbm, east_ref),
-                (north_hbm, north_ref),
-                (fwd_hbm, fwd_ref),
-                (bwd_hbm, bwd_ref),
-            )
-        )
-    ]
-
-    def pieces(group):
-        at = pl.ds(pl.multiple_of(group * rows, 16), rows)
-        copies, spot = [], 0
-        for i, ref in enumerate((far_w_hbm, own_w_hbm, inner_hbm, own_e_hbm, far_e_hbm)):
-            width = ref.shape[1]
-            target = field_ref.at[at, pl.ds(spot, width)]
-            copies.append(pltpu.make_async_copy(ref.at[at, :], target, field_sems.at[group, i]))
-            spot = spot + width
-        return copies
+    groups = far_w_ref.shape[0] // rows
+
+    def coef(j, lines, e):
+        x = e - HALO
+        if x < 1:
+            ref, place = rim_coef_ref, x + HALO - 1
+        elif x < lon - 1:
+            ref, place = inner_coef_ref, x - 1
+        else:
+            ref, place = rim_coef_ref, x - (lon - HALO - 1) + 2 * HALO
+        return ref[j, lines, place * lat : (place + 1) * lat]
 
     def leave(group):
         at = pl.ds(pl.multiple_of(group * rows * lon, 16), rows * lon)
         return pltpu.make_async_copy(result_ref.at[at, :], out_hbm.at[at, :], out_sems.at[group])
 
-    for copy in sides:
-        copy.start()
-    for group in range(groups):
-        for copy in pieces(group):
-            copy.start()
-    for copy in sides:
-        copy.wait()
-    columns = range(1 - HALO, lon + HALO - 1)
-    fill_coefs(east_ref, north_ref, (fwd_ref, bwd_ref), coef_ref, columns, lon, levels, total)
-
     def group_of(group, carry):
-        for copy in pieces(group):
-            copy.wait()
-        view = field_ref.at[pl.ds(pl.multiple_of(group * rows, 16), rows), :]
+        mine = pl.ds(pl.multiple_of(group * rows, 16), rows)
+        spot = 0
+        for ref in (far_w_ref, own_w_ref, inner_ref, own_e_ref, far_e_ref):
+            width = ref.shape[1]
+            field_ref[:, spot : spot + width] = ref[mine, :]
+            spot = spot + width
         base = pl.multiple_of(group * rows * lon, 16)
         result = result_ref.at[pl.ds(base, rows * lon), :]
 
@@ -348,9 +349,7 @@
                 first = (t * levels + block * 8) * lon + e - HALO
                 result[pl.ds(first, 8, stride=lon), :] = value
 
-        two_steps(
-            mix_ref, view, mixed_ref, coef_ref, 0, lon + 2 * HALO, 0, lat, levels, put
-        )
+        two_steps(mix_ref, field_ref, mixed_ref, coef, 0, lon + 2 * HALO, lat, levels, put)
         leave(group).start()
         return carry
 
@@ -380,10 +379,6 @@
 
 
 def weigh(got_ref, weighted_ref, place_ref, range_ref, lat, levels, tracers):
-    tiles, _, capacity = got_ref.shape
-    parts = regions_of(capacity)
-    wide = tiles * capacity // parts
-
     def store(spot, got):
         at = slice(spot, spot + got.shape[1])
         row = 0
@@ -401,6 +396,12 @@
         place_ref[:, at] = jnp.broadcast_to(column, (8, got.shape[1]))
 
     regroup(got_ref, store)
+    span(place_ref, range_ref)
+
+
+def span(place_ref, range_ref):
+    parts = range_ref.shape[0] // 2
+    wide = place_ref.shape[1] // parts
     for part in range(parts):
         place = place_ref[:, part * wide : (part + 1) * wide]
         range_ref[2 * part] = jnp.min(jnp.where(place < 0.0, 1e6, place))
@@ -425,40 +426,20 @@
 
 
 def forcing_inner_kernel(
-    got_ref, field_hbm, out_hbm, weighted_ref, place_ref, range_ref, total_ref, rounded_ref,
-    in_sems, out_sems, *, lat, levels, tracers,
+    weighted_ref, place_ref, field_ref, out_ref, range_ref, total_ref, *, lat
 ):
     cells = HALO * lat
-    count = field_hbm.shape[1] // cells
-
-    def at(i):
-        return pl.ds(pl.multiple_of(i * cells, cells), cells)
-
-    def enter(i):
-        return pltpu.make_async_copy(
-            field_hbm.at[:, at(i)], total_ref.at[:, at(i)], in_sems.at[i]
-        )
-
-    def leave(i):
-        return pltpu.make_async_copy(
-            rounded_ref.at[:, at(i)], out_hbm.at[:, at(i)], out_sems.at[i]
-        )
-
-    for i in range(count):
-        enter(i).start()
-    weigh(got_ref, weighted_ref, place_ref, range_ref, lat, levels, tracers)
+    span(place_ref, range_ref)
 
     def pair_of(i, carry):
-        enter(i).wait()
+        at = pl.ds(pl.multiple_of(i * cells, cells), cells)
+        total_ref[...] = field_ref[:, at]
         offset = ((i + 1) * cells).astype(F32)
-        add_forcing(weighted_ref, place_ref, range_ref, total_ref, at(i), offset)
-        rounded_ref[:, at(i)] = total_ref[:, at(i)].astype(BF16)
-        leave(i).start()
+        add_forcing(weighted_ref, place_ref, range_ref, total_ref, slice(0, cells), offset)
+        out_ref[:, at] = total_ref[...].astype(BF16)
         return carry
 
-    lax.fori_loop(0, count, pair_of, 0)
-    for i in range(count):
-        leave(i).wait()
+    lax.fori_loop(0, field_ref.shape[1] // cells, pair_of, 0)
 
 
 def per_device(
@@ -485,130 +466,104 @@
     field = adjoint_in.reshape(total * lon, lat)
     east = east_courant.reshape(levels * lon, lat)
     north = north_courant.reshape(levels * lon, lat)
+    here = pl.BlockSpec(memory_space=VMEM)
+    far = pl.BlockSpec(memory_space=pltpu.MemorySpace.HBM)
     pairs = lon // HALO
     height = levels + tracers + 8
     payload = pl.pallas_call(
         functools.partial(pack_kernel, tiles=tiles, capacity=capacity, lat=lat, pairs=pairs),
-        out_shape=jax.ShapeDtypeStruct((tiles, height, capacity), BF16),
+        out_specs=here,
+        out_shape=pltpu.VMEM((tiles, height, capacity), BF16),
         compiler_params=params(),
         name="pack",
-    )(avg_kernel, pixel_weight, pixel_owner.reshape(1, pixels), pixel_column)
+    )(
+        away(avg_kernel),
+        away(pixel_weight),
+        away(pixel_owner.reshape(1, pixels)),
+        away(pixel_column),
+    )
     got = lax.all_to_all(payload, "tile", split_axis=0, concat_axis=0, tiled=True)
 
     fwd_rows = HALO * total + 3 * (levels + 8)
     bwd_rows = HALO * total + 2 * (levels + 8)
-    whole = lambda *shape: pl.BlockSpec(shape, lambda i: (0,) * len(shape))
     fwd, bwd, mix = pl.pallas_call(
         functools.partial(edge_kernel, lon=lon, levels=levels),
-        grid=(2,),
-        in_specs=[
-            pl.BlockSpec((total * lon // 2, lat), lambda i: (i, 0)),
-            whole(levels * lon, lat),
-            whole(levels * lon, lat),
-            whole(levels, levels),
-        ],
-        out_specs=[whole(fwd_rows, lat), whole(bwd_rows, lat), whole(rows, rows)],
+        in_specs=[here, here, here, pl.BlockSpec((levels, levels), lambda: (0, 0))],
+        out_specs=[here] * 3,
         out_shape=[
-            jax.ShapeDtypeStruct((fwd_rows, lat), BF16),
-            jax.ShapeDtypeStruct((bwd_rows, lat), BF16),
-            jax.ShapeDtypeStruct((rows, rows), BF16),
+            pltpu.VMEM((fwd_rows, lat), BF16),
+            pltpu.VMEM((bwd_rows, lat), BF16),
+            pltpu.VMEM((rows, rows), BF16),
         ],
         compiler_params=params(),
         name="edges",
-    )(field, east, north, level_mix)
+    )(*near_by(field, east, north), away(level_mix))
     fwd = lax.ppermute(fwd, "tile", ring)
     bwd = lax.ppermute(bwd, "tile", back)
 
-    def scratch(columns, coefs):
+    def scratch(columns):
         return [
-            pltpu.VMEM((5, levels, coefs * lat), F32),
             pltpu.VMEM((rows, columns * lat), BF16),
             pltpu.VMEM((rows, columns * lat), F32),
         ]
 
-    strip = lambda width: pl.BlockSpec((rows, width), lambda i: (i, 0))
     cells = HALO * lat
-    fixed_specs = [whole(rows, rows), whole(levels * lon, lat), whole(levels * lon, lat)]
     inner_width = (lon - 2 * HALO) * lat
-    middle, near = pl.pallas_call(
+    middle, near, inner_coef = pl.pallas_call(
         functools.partial(inner_kernel, lon=lon, levels=levels),
         grid=(steps,),
-        in_specs=fixed_specs + [pl.BlockSpec((rows * lon, lat), lambda i: (i, 0))],
-        out_specs=[strip(inner_width), strip(4 * cells)],
+        in_specs=[here] * 4,
+        out_specs=[pl.BlockSpec((rows, inner_width), lambda i: (i, 0)), here, far],
         out_shape=[
-            jax.ShapeDtypeStruct((total, inner_width), F32),
-            jax.ShapeDtypeStruct((total, 4 * cells), BF16),
+            pltpu.HBM((total, inner_width), F32),
+            pltpu.VMEM((total, 4 * cells), BF16),
+            pltpu.HBM((5, levels, (lon - 2) * lat), F32),
         ],
-        scratch_shapes=scratch(lon, lon - 2),
+        scratch_shapes=[pltpu.VMEM((5, levels, (lon - 2) * lat), F32)]
+        + scratch(lon)
+        + [pltpu.SemaphoreType.DMA],
         compiler_params=params(),
         name="first_half_inner",
-    )(mix, east, north, field)
-    whole1 = lambda *shape: pl.BlockSpec(shape, lambda: (0,) * len(shape))
-    far = pl.BlockSpec(memory_space=pltpu.MemorySpace.HBM)
-    forcing_scratch = [
-        pltpu.VMEM((total, slots), BF16),
-        pltpu.VMEM((8, slots), F32),
-        pltpu.SMEM((2 * regions_of(capacity),), F32),
-    ]
-    own_w, own_e = pl.pallas_call(
+    )(*near_by(mix, east, north, field))
+
+    ranges = pltpu.SMEM((2 * regions_of(capacity),), F32)
+    own_w, own_e, rim_coef, weighted, place = pl.pallas_call(
         functools.partial(rim_kernel, lon=lon, levels=levels, tracers=tracers),
-        in_specs=[
-            whole1(rows, rows),
-            whole1(levels * lon, lat),
-            whole1(levels * lon, lat),
-            whole1(fwd_rows, lat),
-            whole1(bwd_rows, lat),
-            whole1(total, 4 * cells),
-            whole1(tiles, height, capacity),
+        in_specs=[here] * 7,
+        out_specs=[here] * 5,
+        out_shape=[
+            pltpu.VMEM((total, cells), BF16),
+            pltpu.VMEM((total, cells), BF16),
+            pltpu.VMEM((5, levels, 4 * HALO * lat), F32),
+            pltpu.VMEM((total, slots), BF16),
+            pltpu.VMEM((8, slots), F32),
         ],
-        out_specs=[whole1(total, cells), whole1(total, cells)],
-        out_shape=[jax.ShapeDtypeStruct((total, cells), BF16)] * 2,
-        scratch_shapes=scratch(6 * HALO, 4 * HALO)
-        + forcing_scratch
-        + [pltpu.VMEM((total, 2 * cells), F32)],
+        scratch_shapes=scratch(6 * HALO) + [ranges, pltpu.VMEM((total, 2 * cells), F32)],
         compiler_params=params(),
         name="rim",
-    )(mix, east, north, fwd, bwd, near, got)
+    )(*near_by(mix, east, north, fwd, bwd, near, got))
     far_w = lax.ppermute(own_e, "tile", ring)
     far_e = lax.ppermute(own_w, "tile", back)
     inner = pl.pallas_call(
-        functools.partial(forcing_inner_kernel, lat=lat, levels=levels, tracers=tracers),
-        in_specs=[whole1(tiles, height, capacity), far],
-        out_specs=far,
-        out_shape=jax.ShapeDtypeStruct((total, inner_width), BF16),
-        scratch_shapes=forcing_scratch
-        + [
-            pltpu.VMEM((total, inner_width), F32),
-            pltpu.VMEM((total, inner_width), BF16),
-            pltpu.SemaphoreType.DMA((pairs - 2,)),
-            pltpu.SemaphoreType.DMA((pairs - 2,)),
-        ],
+        functools.partial(forcing_inner_kernel, lat=lat),
+        in_specs=[here] * 3,
+        out_specs=here,
+        out_shape=pltpu.VMEM((total, inner_width), BF16),
+        scratch_shapes=[ranges, pltpu.VMEM((total, cells), F32)],
         compiler_params=params(),
         name="forcing_inner",
-    )(got, middle)
-
-    coefs, fields, mixed = scratch(lon + 2 * HALO, lon + 2 * HALO - 2)
+    )(*near_by(weighted, place, middle))
+
     out = pl.pallas_call(
-        functools.partial(second_half_kernel, lon=lon, levels=levels, total=total),
-        in_specs=[whole1(rows, rows)] + [far] * 9,
+        functools.partial(second_half_kernel, lon=lon, levels=levels),
+        in_specs=[here] * 8,
         out_specs=far,
         out_shape=jax.ShapeDtypeStruct((total * lon, lat), F32),
-        scratch_shapes=[
-            pltpu.VMEM((levels * lon, lat), F32),
-            pltpu.VMEM((levels * lon, lat), F32),
-            pltpu.VMEM((fwd_rows, lat), BF16),
-            pltpu.VMEM((bwd_rows, lat), BF16),
-            coefs,
-            pltpu.VMEM((total, (lon + 2 * HALO) * lat), BF16),
-            mixed,
-            pltpu.VMEM((total * lon, lat), F32),
-            pltpu.SemaphoreType.DMA((4,)),
-            pltpu.SemaphoreType.DMA((steps, 5)),
-            pltpu.SemaphoreType.DMA((steps,)),
-        ],
+        scratch_shapes=scratch(lon + 2 * HALO)
+        + [pltpu.VMEM((total * lon, lat), F32), pltpu.SemaphoreType.DMA((steps,))],
         compiler_params=params(),
         name="second_half",
-    )(mix, east, north, fwd, bwd, far_w, own_w, inner, own_e, far_e)
+    )(*near_by(mix, inner_coef, rim_coef, far_w, own_w, inner, own_e, far_e))
     return out.reshape(tracers, levels, lon, lat)
 
 

time: 71.2 us -> 62.3 us (0.87)
  the two profiles are of different devices: /device:TPU:0 before, /device:TPU:1 now
where the time goes in v5:
time: 62.3 us; the launch traced here: 61.9 us
  Pallas kernels  38.5 us (62%)
  starting transfers between devices  9.97 us (16%)
  waiting for transfers between devices  6.86 us (11%)
  local copies, waits for them, and re-layouts  6.31 us (10%)
    pallas_call x1, Pallas kernels, per_device(): pl.pallas_call(functools.partial(second_half_kernel, lon=lon, levels=leve...  9.12 us
    pallas_call x1, Pallas kernels, per_device(): pl.pallas_call(functools.partial(inner_kernel, lon=lon, levels=levels), g...  8.56 us
    pallas_call x1, Pallas kernels, per_device(): pl.pallas_call(functools.partial(rim_kernel, lon=lon, levels=levels, trac...  7.36 us
    all_to_all x1, starting transfers between devices, per_device(): lax.all_to_all(payload, 'tile', split_axis=0, concat_axis=0, tiled=True)  7.35 us
    pallas_call x1, Pallas kernels, per_device(): pl.pallas_call(functools.partial(forcing_inner_kernel, lat=lat), in_specs...  6.74 us
    unnamed x18, local copies, waits for them, and re-layouts  6.31 us
    pallas_call x1, Pallas kernels, per_device(): pl.pallas_call(functools.partial(pack_kernel, tiles=tiles, capacity=capac...  5.3 us
    all_to_all x1, waiting for transfers between devices, per_device(): lax.all_to_all(payload, 'tile', split_axis=0, concat_axis=0, tiled=True)  2.56 us
  transfers between devices with their start and end apart: 5, of which 3 were waited for; matrix products, arithmetic and copies ran while one was open for 0% of the time, Pallas kernels for 27%

profile of v5, /device:TPU:1, one launch (start us, length us, event | category | flops | bytes accessed | tf_op | source)
XLA Modules:
  0.0 61.9 jit_solution(11234508856823503520)
XLA Ops:
  0.0 5.3 %pack.1 = bf16[16,88,256]{2,1,0:T(8,128)(2,1)} custom-call(bf16[72,1024]{1,0:T(8,128)(2,1)} %kernel_ref.1, bf16[8,1024]{1,0:T(8,128)(2,1)} %weight_ref.1, s32[1,1024]{1,0:T(1,128)} %bitcast.13, s32[1,1024]{1,0:T(1,128)} %column_ref.1), custom_call_target="tpu_custom_call" | custom-call | tf_op jit(solution)/shard_map/pack/pallas_call | solution.py:473
  5.3 7.3 %all-to-all-start = ((bf16[16,88,256]{2,1,0:T(8,128)(2,1)}), bf16[16,88,256]{2,1,0:T(8,128)(2,1)S(1)}, u32[]{:S(2)}, u32[]{:S(2)}) async-start(bf16[16,88,256]{2,1,0:T(8,128)(2,1)} %pack.1), calls=%async_computation | async-start | bytes 1441792 | tf_op jit(solution)/shard_map/all_to_all | solution.py:485
  12.7 0.0 copy-start
  12.7 2.3 %copy-done = f32[8,72,16,128]{3,2,1,0:T(8,128)S(1)} copy-done((f32[8,72,16,128]{3,2,1,0:T(8,128)S(1)}, f32[8,72,16,128]{3,2,1,0:T(8,128)}, u32[]{:S(2)}) %copy-start) | copy-done | bytes 4718616
  15.0 0.0 copy-start.1
  15.0 1.1 %copy-done.1 = f32[72,16,128]{2,1,0:T(8,128)S(1)} copy-done((f32[72,16,128]{2,1,0:T(8,128)S(1)}, f32[72,16,128]{2,1,0:T(8,128)}, u32[]{:S(2)}) %copy-start.1) | copy-done | bytes 589848
  16.1 0.0 copy-start.3
  16.1 1.1 %copy-done.3 = f32[72,16,128]{2,1,0:T(8,128)S(1)} copy-done((f32[72,16,128]{2,1,0:T(8,128)S(1)}, f32[72,16,128]{2,1,0:T(8,128)}, u32[]{:S(2)}) %copy-start.3) | copy-done | bytes 589848
  17.1 1.4 %edges.1 = (bf16[1392,128]{1,0:T(8,128)(2,1)S(1)}, bf16[1312,128]{1,0:T(8,128)(2,1)S(1)}, bf16[144,144]{1,0:T(8,128)(2,1)S(1)}) custom-call(f32[9216,128]{1,0:T(8,128)S(1)} %bitcast.5, f32[1152,128]{1,0:T(8,128)S(1)} %bitcast.7, f32[1152,128]{1,0:T(8,128)S(1)} %bitcast.10, bf16[72,72]{1,0:T(8,128)(2,1)} %level_mix_ref.1), custom_call_target="tpu_custom_call" | custom-call | tf_op jit(solution)/shard_map/edges/pallas_call | solution.py:489
  18.5 0.0 copy-start.2
  18.6 0.0 copy-start.4
  18.6 1.7 %collective-permute-start = (bf16[1392,128]{1,0:T(8,128)(2,1)S(1)}, bf16[1392,128]{1,0:T(8,128)(2,1)S(1)}, u32[]{:S(2)}, u32[]{:S(2)}) collective-permute-start(bf16[1392,128]{1,0:T(8,128)(2,1)S(1)} %get-tuple-element.18), channel_id=1, source_target_pairs={{0,1},{1,2},{2,3},{3,4},{4,5},{5,6},{6,7},{7,8},{8,9},{9,10},{10,1... | collective-permute-start | bytes 1069064 | tf_op jit(solution)/shard_map/ppermute | solution.py:501
  20.3 0.0 collective-permute-start.1
  20.3 8.6 %first_half_inner.1 = (f32[576,1536]{1,0:T(8,128)}, bf16[576,1024]{1,0:T(8,128)(2,1)S(1)}, f32[5,72,1792]{2,1,0:T(8,128)}) custom-call(bf16[144,144]{1,0:T(8,128)(2,1)S(1)} %get-tuple-element.16.mix_ref, f32[1152,128]{1,0:T(8,128)S(1)} %bitcast.8, f32[1152,128]{1,0:T(8,128)S(1)} %bitcast.11, f32[9216,128]{1,0:T(8,128)S(1)} %bitcast.6), custom_call_target="tpu_custom_call" | custom-call | tf_op jit(solution)/shard_map/first_half_inner/pallas_call | solution.py:512
  28.8 0.0 collective-permute-done.1.bwd_ref
  28.8 0.0 copy-start.7
  28.9 0.7 %copy-done.7 = bf16[1312,128]{1,0:T(8,128)(2,1)} copy-done((bf16[1312,128]{1,0:T(8,128)(2,1)}, bf16[1312,128]{1,0:T(8,128)(2,1)S(1)}, u32[]{:S(2)}) %copy-start.7) | copy-done | bytes 335896
  29.6 1.8 %collective-permute-done.fwd_ref = bf16[1392,128]{1,0:T(8,128)(2,1)S(1)} collective-permute-done((bf16[1392,128]{1,0:T(8,128)(2,1)S(1)}, bf16[1392,128]{1,0:T(8,128)(2,1)S(1)}, u32[]{:S(2)}, u32[]{:S(2)}) %collective-permute-start) | collective-permute-done | bytes 356384 | tf_op jit(solution)/shard_map/ppermute | solution.py:501
  31.3 2.6 %all-to-all-done.got_ref = bf16[16,88,256]{2,1,0:T(8,128)(2,1)S(1)} async-done(((bf16[16,88,256]{2,1,0:T(8,128)(2,1)}), bf16[16,88,256]{2,1,0:T(8,128)(2,1)S(1)}, u32[]{:S(2)}, u32[]{:S(2)}) %all-to-all-start) | async-done | bytes 720928 | tf_op jit(solution)/shard_map/all_to_all | solution.py:485
  33.9 0.0 copy-start.5
  33.9 0.0 copy-done.2
  33.9 0.0 copy-done.4
  33.9 0.0 copy-start.8
  33.9 1.1 %copy-done.8 = bf16[1312,128]{1,0:T(8,128)(2,1)S(1)} copy-done((bf16[1312,128]{1,0:T(8,128)(2,1)S(1)}, bf16[1312,128]{1,0:T(8,128)(2,1)}, u32[]{:S(2)}) %copy-start.8) | copy-done | bytes 335896
  35.0 7.4 %rim.1 = (bf16[576,256]{1,0:T(8,128)(2,1)S(1)}, bf16[576,256]{1,0:T(8,128)(2,1)S(1)}, f32[5,72,1024]{2,1,0:T(8,128)S(1)}, bf16[576,4096]{1,0:T(8,128)(2,1)S(1)}, f32[8,4096]{1,0:T(8,128)S(1)}) custom-call(bf16[144,144]{1,0:T(8,128)(2,1)S(1)} %get-tuple-element.16.mix_ref, f32[1152,128]{1,0:T(8,128)S(1)} %bitcast.9, f32[1152,128]{1,0:T(8,128)S(1)} %bitcast.12, ...), custom_call_target="tpu_custom_call" | custom-call | tf_op jit(solution)/shard_map/rim/pallas_call | solution.py:530
  42.4 0.9 %collective-permute-start.2 = (bf16[576,256]{1,0:T(8,128)(2,1)S(1)}, bf16[576,256]{1,0:T(8,128)(2,1)S(1)}, u32[]{:S(2)}, u32[]{:S(2)}) collective-permute-start(bf16[576,256]{1,0:T(8,128)(2,1)S(1)} %get-tuple-element.22.own_e_ref), channel_id=1, source_target_pairs={{0,1},{1,2},{2,3},{3,4},{4,5},{5,6},{6,7},{7,8},{8,9},{9,10},{10,1... | collective-permute-start | bytes 884744 | tf_op jit(solution)/shard_map/ppermute | solution.py:545
  43.3 0.0 collective-permute-start.3
  43.3 0.0 copy-done.5
  43.3 0.0 copy-start.6
  43.3 6.7 %forcing_inner.1.inner_ref = bf16[576,1536]{1,0:T(8,128)(2,1)S(1)} custom-call(bf16[576,4096]{1,0:T(8,128)(2,1)S(1)} %get-tuple-element.24.weighted_ref, f32[8,4096]{1,0:T(8,128)S(1)} %get-tuple-element.25.place_ref, f32[576,1536]{1,0:T(8,128)S(1)} %copy-done.5), custom_call_target="tpu_custom_call" | custom-call | tf_op jit(solution)/shard_map/forcing_inner/pallas_call | solution.py:547
  50.1 0.0 collective-permute-done.2.far_w_ref
  50.1 2.5 %collective-permute-done.3.far_e_ref = bf16[576,256]{1,0:T(8,128)(2,1)S(1)} collective-permute-done((bf16[576,256]{1,0:T(8,128)(2,1)S(1)}, bf16[576,256]{1,0:T(8,128)(2,1)S(1)}, u32[]{:S(2)}, u32[]{:S(2)}) %collective-permute-start.3) | collective-permute-done | bytes 294944 | tf_op jit(solution)/shard_map/ppermute | solution.py:546
  52.6 0.0 copy-done.6
  52.6 9.1 %second_half.1 = f32[9216,128]{1,0:T(8,128)} custom-call(bf16[144,144]{1,0:T(8,128)(2,1)S(1)} %get-tuple-element.16.mix_ref, f32[5,72,1792]{2,1,0:T(8,128)S(1)} %copy-done.6, f32[5,72,1024]{2,1,0:T(8,128)S(1)} %get-tuple-element.21.rim_coef_ref, bf16[576,256]{1,0:T(8,128)(2,1)S(1)} %collective-permute-done.2.far_w_ref, ...), custom_call_target="tpu_custom_call" | custom-call | tf_op jit(solution)/shard_map/second_half/pallas_call | solution.py:557
Async XLA Ops:
  5.3 28.6 %all-to-all-start = ((bf16[16,88,256]{2,1,0:T(8,128)(2,1)}), bf16[16,88,256]{2,1,0:T(8,128)(2,1)S(1)}, u32[]{:S(2)}, u32[]{:S(2)}) async-start(bf16[16,88,256]{2,1,0:T(8,128)(2,1)} %pack.1), calls=%async_computation | async-start | bytes 1441792 | tf_op jit(solution)/shard_map/all_to_all | solution.py:485
  12.7 2.3 %copy-start = (f32[8,72,16,128]{3,2,1,0:T(8,128)S(1)}, f32[8,72,16,128]{3,2,1,0:T(8,128)}, u32[]{:S(2)}) copy-start(f32[8,72,16,128]{3,2,1,0:T(8,128)} %param.8) | copy-start | bytes 14155780
  15.0 1.1 %copy-start.1 = (f32[72,16,128]{2,1,0:T(8,128)S(1)}, f32[72,16,128]{2,1,0:T(8,128)}, u32[]{:S(2)}) copy-start(f32[72,16,128]{2,1,0:T(8,128)} %param.9) | copy-start | bytes 1769476
  16.1 1.1 %copy-start.3 = (f32[72,16,128]{2,1,0:T(8,128)S(1)}, f32[72,16,128]{2,1,0:T(8,128)}, u32[]{:S(2)}) copy-start(f32[72,16,128]{2,1,0:T(8,128)} %param.10) | copy-start | bytes 1769476
  18.5 15.3 %copy-start.2 = (f32[72,16,128]{2,1,0:T(8,128)S(1)}, f32[72,16,128]{2,1,0:T(8,128)}, u32[]{:S(2)}) copy-start(f32[72,16,128]{2,1,0:T(8,128)} %param.9) | copy-start | bytes 1769476
  18.6 15.3 %copy-start.4 = (f32[72,16,128]{2,1,0:T(8,128)S(1)}, f32[72,16,128]{2,1,0:T(8,128)}, u32[]{:S(2)}) copy-start(f32[72,16,128]{2,1,0:T(8,128)} %param.10) | copy-start | bytes 1769476
  18.6 12.7 %collective-permute-start = (bf16[1392,128]{1,0:T(8,128)(2,1)S(1)}, bf16[1392,128]{1,0:T(8,128)(2,1)S(1)}, u32[]{:S(2)}, u32[]{:S(2)}) collective-permute-start(bf16[1392,128]{1,0:T(8,128)(2,1)S(1)} %get-tuple-element.18), channel_id=1, source_target_pairs={{0,1},{1,2},{2,3},{3,4},{4,5},{5,6},{6,7},{7,8},{8,9},{9,10},{10,1... | collective-permute-start | bytes 1069064 | tf_op jit(solution)/shard_map/ppermute | solution.py:501
  20.3 8.6 %collective-permute-start.1 = (bf16[1312,128]{1,0:T(8,128)(2,1)S(1)}, bf16[1312,128]{1,0:T(8,128)(2,1)S(1)}, u32[]{:S(2)}, u32[]{:S(2)}) collective-permute-start(bf16[1312,128]{1,0:T(8,128)(2,1)S(1)} %get-tuple-element.19), channel_id=1, source_target_pairs={{1,0},{2,1},{3,2},{4,3},{5,4},{6,5},{7,6},{8,7},{9,8},{10,9},{11,1... | collective-permute-start | bytes 1007624 | tf_op jit(solution)/shard_map/ppermute | solution.py:502
  28.8 0.7 %copy-start.7 = (bf16[1312,128]{1,0:T(8,128)(2,1)}, bf16[1312,128]{1,0:T(8,128)(2,1)S(1)}, u32[]{:S(2)}) copy-start(bf16[1312,128]{1,0:T(8,128)(2,1)S(1)} %collective-permute-done.1.bwd_ref) | copy-start | bytes 1007620
  33.9 9.4 %copy-start.5 = (f32[576,1536]{1,0:T(8,128)S(1)}, f32[576,1536]{1,0:T(8,128)}, u32[]{:S(2)}) copy-start(f32[576,1536]{1,0:T(8,128)} %get-tuple-element.26.field_ref) | copy-start | bytes 10616836
  33.9 1.1 %copy-start.8 = (bf16[1312,128]{1,0:T(8,128)(2,1)S(1)}, bf16[1312,128]{1,0:T(8,128)(2,1)}, u32[]{:S(2)}) copy-start(bf16[1312,128]{1,0:T(8,128)(2,1)} %copy-done.7) | copy-start | bytes 1007620
  42.4 7.7 %collective-permute-start.2 = (bf16[576,256]{1,0:T(8,128)(2,1)S(1)}, bf16[576,256]{1,0:T(8,128)(2,1)S(1)}, u32[]{:S(2)}, u32[]{:S(2)}) collective-permute-start(bf16[576,256]{1,0:T(8,128)(2,1)S(1)} %get-tuple-element.22.own_e_ref), channel_id=1, source_target_pairs={{0,1},{1,2},{2,3},{3,4},{4,5},{5,6},{6,7},{7,8},{8,9},{9,10},{10,1... | collective-permute-start | bytes 884744 | tf_op jit(solution)/shard_map/ppermute | solution.py:545
  43.3 9.3 %collective-permute-start.3 = (bf16[576,256]{1,0:T(8,128)(2,1)S(1)}, bf16[576,256]{1,0:T(8,128)(2,1)S(1)}, u32[]{:S(2)}, u32[]{:S(2)}) collective-permute-start(bf16[576,256]{1,0:T(8,128)(2,1)S(1)} %get-tuple-element.23.own_w_ref), channel_id=1, source_target_pairs={{1,0},{2,1},{3,2},{4,3},{5,4},{6,5},{7,6},{8,7},{9,8},{10,9},{11,1... | collective-permute-start | bytes 884744 | tf_op jit(solution)/shard_map/ppermute | solution.py:546
  43.3 9.3 %copy-start.6 = (f32[5,72,1792]{2,1,0:T(8,128)S(1)}, f32[5,72,1792]{2,1,0:T(8,128)}, u32[]{:S(2)}) copy-start(f32[5,72,1792]{2,1,0:T(8,128)} %get-tuple-element.17.inner_coef_ref) | copy-start | bytes 7741444

commit v6 on v5

--- a/solution.py
+++ b/solution.py
@@ -10,6 +10,8 @@
 F32 = jnp.float32
 BF16 = jnp.bfloat16
 GROUP = 2
+RIM_TOGETHER = 2
+TOGETHER = 2
 HALO = 2
 VMEM_BYTES = 20 * 1024 * 1024
 VMEM = pltpu.MemorySpace.VMEM
@@ -206,20 +208,25 @@
             emit(block, e, values)
 
 
-def two_steps(mix_ref, field_ref, mixed_ref, coef, start, count, lat, levels, put):
-    def mix(lo, hi):
+def two_steps(mix_ref, levels, lat, segments):
+    def mix(field_ref, mixed_ref, lo, hi):
         for e in range(lo, hi, 2):
             at = slice(e * lat, (e + 2) * lat)
             mixed_ref[:, at] = jnp.dot(mix_ref[...], field_ref[:, at], preferred_element_type=F32)
 
-    def keep(block, e, values):
-        at = slice(block * 8 * GROUP, (block + 1) * 8 * GROUP)
-        field_ref[at, e * lat : (e + 1) * lat] = jnp.concatenate(values, axis=0).astype(BF16)
-
-    mix(start, start + count)
-    stencil(mixed_ref, coef, start + 1, count - 2, lat, levels, keep)
-    mix(start + 1, start + count - 1)
-    stencil(mixed_ref, coef, start + 2, count - 4, lat, levels, put)
+    for field_ref, mixed_ref, _, start, count, _ in segments:
+        mix(field_ref, mixed_ref, start, start + count)
+    for field_ref, mixed_ref, coef, start, count, _ in segments:
+
+        def keep(block, e, values):
+            at = slice(block * 8 * GROUP, (block + 1) * 8 * GROUP)
+            field_ref[at, e * lat : (e + 1) * lat] = jnp.concatenate(values, axis=0).astype(BF16)
+
+        stencil(mixed_ref, coef, start + 1, count - 2, lat, levels, keep)
+    for field_ref, mixed_ref, _, start, count, _ in segments:
+        mix(field_ref, mixed_ref, start + 1, start + count - 1)
+    for field_ref, mixed_ref, coef, start, count, put in segments:
+        stencil(mixed_ref, coef, start + 2, count - 4, lat, levels, put)
 
 
 def factors(coef_ref, lat, place_of):
@@ -260,7 +267,7 @@
             out_ref[row : row + 8, (e - HALO) * lat : (e - HALO + 1) * lat] = value
 
     coef = factors(coef_ref, lat, lambda e: e - 1)
-    two_steps(mix_ref, field_ref, mixed_ref, coef, 0, lon, lat, levels, put)
+    two_steps(mix_ref, levels, lat, [(field_ref, mixed_ref, coef, 0, lon, put)])
 
     @pl.when(step == pl.num_programs(0) - 1)
     def _():
@@ -268,42 +275,53 @@
 
 
 def rim_kernel(
-    mix_ref, east_ref, north_ref, fwd_ref, bwd_ref, near_ref, got_ref, west_out_ref, east_out_ref,
-    coef_ref, weighted_ref, place_ref, field_ref, mixed_ref, range_ref, total_ref,
+    mix_ref, east_ref, north_ref, fwd_ref, near_ref, got_ref, bwd_hbm, west_out_ref, east_out_ref,
+    coef_ref, weighted_ref, place_ref, field_ref, mixed_ref, range_ref, total_ref, bwd_ref, bwd_sem,
     *, lon, levels, tracers,
 ):
+    copy = pltpu.make_async_copy(bwd_hbm, bwd_ref, bwd_sem)
+    copy.start()
     total = near_ref.shape[0]
     lat = fwd_ref.shape[1]
     rows = GROUP * levels
     wide = 3 * HALO
+    weigh(got_ref, weighted_ref, place_ref, range_ref, lat, levels, tracers)
+    copy.wait()
     columns = list(range(1 - HALO, HALO + 1)) + list(range(lon - HALO - 1, lon + HALO - 1))
     fill_coefs(east_ref, north_ref, (fwd_ref, bwd_ref), coef_ref, columns, lon, levels, total)
-
-    def group_of(group, carry):
-        for c in range(HALO):
-            at = pl.ds(pl.multiple_of(c * total + group * rows, 16), rows)
-            field_ref[:, c * lat : (c + 1) * lat] = fwd_ref[at, :]
-            e = wide + 2 * HALO + c
-            field_ref[:, e * lat : (e + 1) * lat] = bwd_ref[at, :]
-        side = 2 * HALO * lat
-        mine = pl.ds(pl.multiple_of(group * rows, 16), rows)
-        field_ref[:, HALO * lat : HALO * lat + side] = near_ref[mine, :side]
-        field_ref[:, wide * lat : wide * lat + side] = near_ref[mine, side:]
-        for half in range(2):
-            start = half * wide
-
-            def put(block, e, values):
-                spot = (e - start - HALO + half * HALO) * lat
-                for t, value in enumerate(values):
-                    row = pl.multiple_of(group * rows + block * 8 * GROUP + 8 * t, 8)
-                    total_ref[pl.ds(row, 8), spot : spot + lat] = value
-
-            coef = factors(coef_ref, lat, lambda e: e - start - 1 + half * 2 * HALO)
-            two_steps(mix_ref, field_ref, mixed_ref, coef, start, wide, lat, levels, put)
+    together = field_ref.shape[0]
+
+    def segment(group, slot, half):
+        field, mixed = field_ref.at[slot], mixed_ref.at[slot]
+        start = half * wide
+
+        def put(block, e, values):
+            spot = (e - start - HALO + half * HALO) * lat
+            for t, value in enumerate(values):
+                row = pl.multiple_of(group * rows + block * 8 * GROUP + 8 * t, 8)
+                total_ref[pl.ds(row, 8), spot : spot + lat] = value
+
+        coef = factors(coef_ref, lat, lambda e: e - start - 1 + half * 2 * HALO)
+        return field, mixed, coef, start, wide, put
+
+    def groups_of(i, carry):
+        segments = []
+        for slot in range(together):
+            group = i * together + slot
+            for c in range(HALO):
+                at = pl.ds(pl.multiple_of(c * total + group * rows, 16), rows)
+                field_ref[slot, :, c * lat : (c + 1) * lat] = fwd_ref[at, :]
+                e = wide + 2 * HALO + c
+                field_ref[slot, :, e * lat : (e + 1) * lat] = bwd_ref[at, :]
+            side = 2 * HALO * lat
+            mine = pl.ds(pl.multiple_of(group * rows, 16), rows)
+            field_ref[slot, :, HALO * lat : HALO * lat + side] = near_ref[mine, :side]
+            field_ref[slot, :, wide * lat : wide * lat + side] = near_ref[mine, side:]
+            segments = segments + [segment(group, slot, half) for half in range(2)]
+        two_steps(mix_ref, levels, lat, segments)
         return carry
 
-    lax.fori_loop(0, total // rows, group_of, 0)
-    weigh(got_ref, weighted_ref, place_ref, range_ref, lat, levels, tracers)
+    lax.fori_loop(0, total // rows // together, groups_of, 0)
     cells = HALO * lat
     for side, out_ref in ((0, west_out_ref), (1, east_out_ref)):
         at = slice(side * cells, (side + 1) * cells)
@@ -334,12 +352,15 @@
         at = pl.ds(pl.multiple_of(group * rows * lon, 16), rows * lon)
         return pltpu.make_async_copy(result_ref.at[at, :], out_hbm.at[at, :], out_sems.at[group])
 
-    def group_of(group, carry):
+    together = field_ref.shape[0]
+
+    def segment(group, slot):
+        field = field_ref.at[slot]
         mine = pl.ds(pl.multiple_of(group * rows, 16), rows)
         spot = 0
         for ref in (far_w_ref, own_w_ref, inner_ref, own_e_ref, far_e_ref):
             width = ref.shape[1]
-            field_ref[:, spot : spot + width] = ref[mine, :]
+            field[:, spot : spot + width] = ref[mine, :]
             spot = spot + width
         base = pl.multiple_of(group * rows * lon, 16)
         result = result_ref.at[pl.ds(base, rows * lon), :]
@@ -349,11 +370,16 @@
                 first = (t * levels + block * 8) * lon + e - HALO
                 result[pl.ds(first, 8, stride=lon), :] = value
 
-        two_steps(mix_ref, field_ref, mixed_ref, coef, 0, lon + 2 * HALO, lat, levels, put)
-        leave(group).start()
+        return field, mixed_ref.at[slot], coef, 0, lon + 2 * HALO, put
+
+    def groups_of(i, carry):
+        mine = [i * together + slot for slot in range(together)]
+        two_steps(mix_ref, levels, lat, [segment(group, slot) for slot, group in enumerate(mine)])
+        for group in mine:
+            leave(group).start()
         return carry
 
-    lax.fori_loop(0, groups, group_of, 0)
+    lax.fori_loop(0, groups // together, groups_of, 0)
     for group in range(groups):
         leave(group).wait()
 
@@ -501,10 +527,10 @@
     fwd = lax.ppermute(fwd, "tile", ring)
     bwd = lax.ppermute(bwd, "tile", back)
 
-    def scratch(columns):
+    def scratch(columns, *together):
         return [
-            pltpu.VMEM((rows, columns * lat), BF16),
-            pltpu.VMEM((rows, columns * lat), F32),
+            pltpu.VMEM((*together, rows, columns * lat), BF16),
+            pltpu.VMEM((*together, rows, columns * lat), F32),
         ]
 
     cells = HALO * lat
@@ -529,7 +555,7 @@
     ranges = pltpu.SMEM((2 * regions_of(capacity),), F32)
     own_w, own_e, rim_coef, weighted, place = pl.pallas_call(
         functools.partial(rim_kernel, lon=lon, levels=levels, tracers=tracers),
-        in_specs=[here] * 7,
+        in_specs=[here] * 6 + [far],
         out_specs=[here] * 5,
         out_shape=[
             pltpu.VMEM((total, cells), BF16),
@@ -538,10 +564,16 @@
             pltpu.VMEM((total, slots), BF16),
             pltpu.VMEM((8, slots), F32),
         ],
-        scratch_shapes=scratch(6 * HALO) + [ranges, pltpu.VMEM((total, 2 * cells), F32)],
+        scratch_shapes=scratch(6 * HALO, RIM_TOGETHER)
+        + [
+            ranges,
+            pltpu.VMEM((total, 2 * cells), F32),
+            pltpu.VMEM((bwd_rows, lat), BF16),
+            pltpu.SemaphoreType.DMA,
+        ],
         compiler_params=params(),
         name="rim",
-    )(*near_by(mix, east, north, fwd, bwd, near, got))
+    )(*near_by(mix, east, north, fwd, near, got), away(bwd))
     far_w = lax.ppermute(own_e, "tile", ring)
     far_e = lax.ppermute(own_w, "tile", back)
     inner = pl.pallas_call(
@@ -559,7 +591,7 @@
         in_specs=[here] * 8,
         out_specs=far,
         out_shape=jax.ShapeDtypeStruct((total * lon, lat), F32),
-        scratch_shapes=scratch(lon + 2 * HALO)
+        scratch_shapes=scratch(lon + 2 * HALO, TOGETHER)
         + [pltpu.VMEM((total * lon, lat), F32), pltpu.SemaphoreType.DMA((steps,))],
         compiler_params=params(),
         name="second_half",

time: 62.3 us -> 59.2 us (0.950)
  Pallas kernels: 38.5 us -> 34.1 us
  waiting for transfers between devices: 6.86 us -> 9.3 us
  local copies, waits for them, and re-layouts: 6.31 us -> 5.2 us
    ppermute x1, waiting for transfers between devices: 2.53 us -> 4.98 us  [per_device(): far_e = lax.ppermute(own_w, 'tile', back)]
    pallas_call x1, Pallas kernels: 6.74 us -> 4.3 us  [per_device(): pl.pallas_call(functools.partial(forcing_inner_kernel, lat=lat), in_specs...]
    pallas_call x1, Pallas kernels: 7.36 us -> 5.85 us  [per_device(): pl.pallas_call(functools.partial(rim_kernel, lon=lon, levels=levels, trac...]
    unnamed x18 -> x16, local copies, waits for them, and re-layouts: 6.31 us -> 5.2 us
  transfers between devices with their start and end apart: 5 -> 5, of which waited for: 3 -> 3; matrix products, arithmetic and copies ran while one was open for 0% -> 0% of each run, Pallas kernels for 27% -> 24%
where the time goes in v6:
time: 59.2 us; the launch traced here: 58.8 us
  Pallas kernels  34.1 us (58%)
  starting transfers between devices  9.96 us (17%)
  waiting for transfers between devices  9.3 us (16%)
  local copies, waits for them, and re-layouts  5.2 us (9%)
    pallas_call x1, Pallas kernels, per_device(): pl.pallas_call(functools.partial(second_half_kernel, lon=lon, levels=leve...  8.61 us
    pallas_call x1, Pallas kernels, per_device(): pl.pallas_call(functools.partial(inner_kernel, lon=lon, levels=levels), g...  8.56 us
    all_to_all x1, starting transfers between devices, per_device(): lax.all_to_all(payload, 'tile', split_axis=0, concat_axis=0, tiled=True)  7.35 us
    pallas_call x1, Pallas kernels, per_device(): pl.pallas_call(functools.partial(rim_kernel, lon=lon, levels=levels, trac...  5.85 us
    pallas_call x1, Pallas kernels, per_device(): pl.pallas_call(functools.partial(pack_kernel, tiles=tiles, capacity=capac...  5.31 us
    unnamed x16, local copies, waits for them, and re-layouts  5.2 us
    ppermute x1, waiting for transfers between devices, per_device(): far_e = lax.ppermute(own_w, 'tile', back)  4.98 us
    pallas_call x1, Pallas kernels, per_device(): pl.pallas_call(functools.partial(forcing_inner_kernel, lat=lat), in_specs...  4.3 us
  transfers between devices with their start and end apart: 5, of which 3 were waited for; matrix products, arithmetic and copies ran while one was open for 0% of the time, Pallas kernels for 24%

profile of v6, /device:TPU:1, one launch (start us, length us, event | category | flops | bytes accessed | tf_op | source)
XLA Modules:
  0.0 58.8 jit_solution(12965139945987203886)
XLA Ops:
  0.0 5.3 %pack.1 = bf16[16,88,256]{2,1,0:T(8,128)(2,1)} custom-call(bf16[72,1024]{1,0:T(8,128)(2,1)} %kernel_ref.1, bf16[8,1024]{1,0:T(8,128)(2,1)} %weight_ref.1, s32[1,1024]{1,0:T(1,128)} %bitcast.13, s32[1,1024]{1,0:T(1,128)} %column_ref.1), custom_call_target="tpu_custom_call" | custom-call | tf_op jit(solution)/shard_map/pack/pallas_call | solution.py:499
  5.3 7.3 %all-to-all-start = ((bf16[16,88,256]{2,1,0:T(8,128)(2,1)}), bf16[16,88,256]{2,1,0:T(8,128)(2,1)S(1)}, u32[]{:S(2)}, u32[]{:S(2)}) async-start(bf16[16,88,256]{2,1,0:T(8,128)(2,1)} %pack.1), calls=%async_computation | async-start | bytes 1441792 | tf_op jit(solution)/shard_map/all_to_all | solution.py:511
  12.7 0.0 copy-start
  12.7 2.3 %copy-done = f32[8,72,16,128]{3,2,1,0:T(8,128)S(1)} copy-done((f32[8,72,16,128]{3,2,1,0:T(8,128)S(1)}, f32[8,72,16,128]{3,2,1,0:T(8,128)}, u32[]{:S(2)}) %copy-start) | copy-done | bytes 4718616
  15.0 0.0 copy-start.1
  15.0 1.1 %copy-done.1 = f32[72,16,128]{2,1,0:T(8,128)S(1)} copy-done((f32[72,16,128]{2,1,0:T(8,128)S(1)}, f32[72,16,128]{2,1,0:T(8,128)}, u32[]{:S(2)}) %copy-start.1) | copy-done | bytes 589848
  16.1 0.0 copy-start.3
  16.1 1.1 %copy-done.3 = f32[72,16,128]{2,1,0:T(8,128)S(1)} copy-done((f32[72,16,128]{2,1,0:T(8,128)S(1)}, f32[72,16,128]{2,1,0:T(8,128)}, u32[]{:S(2)}) %copy-start.3) | copy-done | bytes 589848
  17.1 1.4 %edges.1 = (bf16[1392,128]{1,0:T(8,128)(2,1)S(1)}, bf16[1312,128]{1,0:T(8,128)(2,1)S(1)}, bf16[144,144]{1,0:T(8,128)(2,1)S(1)}) custom-call(f32[9216,128]{1,0:T(8,128)S(1)} %bitcast.5, f32[1152,128]{1,0:T(8,128)S(1)} %bitcast.7, f32[1152,128]{1,0:T(8,128)S(1)} %bitcast.10, bf16[72,72]{1,0:T(8,128)(2,1)} %level_mix_ref.1), custom_call_target="tpu_custom_call" | custom-call | tf_op jit(solution)/shard_map/edges/pallas_call | solution.py:515
  18.6 0.0 copy-start.2
  18.6 0.0 copy-start.4
  18.6 1.7 %collective-permute-start = (bf16[1392,128]{1,0:T(8,128)(2,1)S(1)}, bf16[1392,128]{1,0:T(8,128)(2,1)S(1)}, u32[]{:S(2)}, u32[]{:S(2)}) collective-permute-start(bf16[1392,128]{1,0:T(8,128)(2,1)S(1)} %get-tuple-element.18), channel_id=1, source_target_pairs={{0,1},{1,2},{2,3},{3,4},{4,5},{5,6},{6,7},{7,8},{8,9},{9,10},{10,1... | collective-permute-start | bytes 1069064 | tf_op jit(solution)/shard_map/ppermute | solution.py:527
  20.3 0.0 collective-permute-start.1
  20.3 8.6 %first_half_inner.1 = (f32[576,1536]{1,0:T(8,128)}, bf16[576,1024]{1,0:T(8,128)(2,1)S(1)}, f32[5,72,1792]{2,1,0:T(8,128)}) custom-call(bf16[144,144]{1,0:T(8,128)(2,1)S(1)} %get-tuple-element.16.mix_ref, f32[1152,128]{1,0:T(8,128)S(1)} %bitcast.8, f32[1152,128]{1,0:T(8,128)S(1)} %bitcast.11, f32[9216,128]{1,0:T(8,128)S(1)} %bitcast.6), custom_call_target="tpu_custom_call" | custom-call | tf_op jit(solution)/shard_map/first_half_inner/pallas_call | solution.py:538
  28.8 0.0 collective-permute-done.1.bwd_hbm
  28.8 0.0 copy-start.7
  28.9 0.7 %copy-done.7 = bf16[1312,128]{1,0:T(8,128)(2,1)} copy-done((bf16[1312,128]{1,0:T(8,128)(2,1)}, bf16[1312,128]{1,0:T(8,128)(2,1)S(1)}, u32[]{:S(2)}) %copy-start.7) | copy-done | bytes 335896
  29.6 1.8 %collective-permute-done.fwd_ref = bf16[1392,128]{1,0:T(8,128)(2,1)S(1)} collective-permute-done((bf16[1392,128]{1,0:T(8,128)(2,1)S(1)}, bf16[1392,128]{1,0:T(8,128)(2,1)S(1)}, u32[]{:S(2)}, u32[]{:S(2)}) %collective-permute-start) | collective-permute-done | bytes 356384 | tf_op jit(solution)/shard_map/ppermute | solution.py:527
  31.3 2.6 %all-to-all-done.got_ref = bf16[16,88,256]{2,1,0:T(8,128)(2,1)S(1)} async-done(((bf16[16,88,256]{2,1,0:T(8,128)(2,1)}), bf16[16,88,256]{2,1,0:T(8,128)(2,1)S(1)}, u32[]{:S(2)}, u32[]{:S(2)}) %all-to-all-start) | async-done | bytes 720928 | tf_op jit(solution)/shard_map/all_to_all | solution.py:511
  33.9 0.0 copy-start.5
  33.9 0.0 copy-done.2
  33.9 0.0 copy-done.4
  33.9 5.8 %rim.1 = (bf16[576,256]{1,0:T(8,128)(2,1)S(1)}, bf16[576,256]{1,0:T(8,128)(2,1)S(1)}, f32[5,72,1024]{2,1,0:T(8,128)S(1)}, bf16[576,4096]{1,0:T(8,128)(2,1)S(1)}, f32[8,4096]{1,0:T(8,128)S(1)}) custom-call(bf16[144,144]{1,0:T(8,128)(2,1)S(1)} %get-tuple-element.16.mix_ref, f32[1152,128]{1,0:T(8,128)S(1)} %bitcast.9, f32[1152,128]{1,0:T(8,128)S(1)} %bitcast.12, ...), custom_call_target="tpu_custom_call" | custom-call | tf_op jit(solution)/shard_map/rim/pallas_call | solution.py:556
  39.8 0.9 %collective-permute-start.2 = (bf16[576,256]{1,0:T(8,128)(2,1)S(1)}, bf16[576,256]{1,0:T(8,128)(2,1)S(1)}, u32[]{:S(2)}, u32[]{:S(2)}) collective-permute-start(bf16[576,256]{1,0:T(8,128)(2,1)S(1)} %get-tuple-element.22.own_e_ref), channel_id=1, source_target_pairs={{0,1},{1,2},{2,3},{3,4},{4,5},{5,6},{6,7},{7,8},{8,9},{9,10},{10,1... | collective-permute-start | bytes 884744 | tf_op jit(solution)/shard_map/ppermute | solution.py:577
  40.7 0.0 collective-permute-start.3
  40.7 0.0 copy-done.5
  40.7 0.0 copy-start.6
  40.7 4.3 %forcing_inner.1.inner_ref = bf16[576,1536]{1,0:T(8,128)(2,1)S(1)} custom-call(bf16[576,4096]{1,0:T(8,128)(2,1)S(1)} %get-tuple-element.24.weighted_ref, f32[8,4096]{1,0:T(8,128)S(1)} %get-tuple-element.25.place_ref, f32[576,1536]{1,0:T(8,128)S(1)} %copy-done.5), custom_call_target="tpu_custom_call" | custom-call | tf_op jit(solution)/shard_map/forcing_inner/pallas_call | solution.py:579
  45.0 0.0 collective-permute-done.2.far_w_ref
  45.0 5.0 %collective-permute-done.3.far_e_ref = bf16[576,256]{1,0:T(8,128)(2,1)S(1)} collective-permute-done((bf16[576,256]{1,0:T(8,128)(2,1)S(1)}, bf16[576,256]{1,0:T(8,128)(2,1)S(1)}, u32[]{:S(2)}, u32[]{:S(2)}) %collective-permute-start.3) | collective-permute-done | bytes 294944 | tf_op jit(solution)/shard_map/ppermute | solution.py:578
  50.0 0.0 copy-done.6
  50.0 8.6 %second_half.1 = f32[9216,128]{1,0:T(8,128)} custom-call(bf16[144,144]{1,0:T(8,128)(2,1)S(1)} %get-tuple-element.16.mix_ref, f32[5,72,1792]{2,1,0:T(8,128)S(1)} %copy-done.6, f32[5,72,1024]{2,1,0:T(8,128)S(1)} %get-tuple-element.21.rim_coef_ref, bf16[576,256]{1,0:T(8,128)(2,1)S(1)} %collective-permute-done.2.far_w_ref, ...), custom_call_target="tpu_custom_call" | custom-call | tf_op jit(solution)/shard_map/second_half/pallas_call | solution.py:589
Async XLA Ops:
  5.3 28.6 %all-to-all-start = ((bf16[16,88,256]{2,1,0:T(8,128)(2,1)}), bf16[16,88,256]{2,1,0:T(8,128)(2,1)S(1)}, u32[]{:S(2)}, u32[]{:S(2)}) async-start(bf16[16,88,256]{2,1,0:T(8,128)(2,1)} %pack.1), calls=%async_computation | async-start | bytes 1441792 | tf_op jit(solution)/shard_map/all_to_all | solution.py:511
  12.7 2.3 %copy-start = (f32[8,72,16,128]{3,2,1,0:T(8,128)S(1)}, f32[8,72,16,128]{3,2,1,0:T(8,128)}, u32[]{:S(2)}) copy-start(f32[8,72,16,128]{3,2,1,0:T(8,128)} %param.8) | copy-start | bytes 14155780
  15.0 1.1 %copy-start.1 = (f32[72,16,128]{2,1,0:T(8,128)S(1)}, f32[72,16,128]{2,1,0:T(8,128)}, u32[]{:S(2)}) copy-start(f32[72,16,128]{2,1,0:T(8,128)} %param.9) | copy-start | bytes 1769476
  16.1 1.1 %copy-start.3 = (f32[72,16,128]{2,1,0:T(8,128)S(1)}, f32[72,16,128]{2,1,0:T(8,128)}, u32[]{:S(2)}) copy-start(f32[72,16,128]{2,1,0:T(8,128)} %param.10) | copy-start | bytes 1769476
  18.6 15.3 %copy-start.2 = (f32[72,16,128]{2,1,0:T(8,128)S(1)}, f32[72,16,128]{2,1,0:T(8,128)}, u32[]{:S(2)}) copy-start(f32[72,16,128]{2,1,0:T(8,128)} %param.9) | copy-start | bytes 1769476
  18.6 15.3 %copy-start.4 = (f32[72,16,128]{2,1,0:T(8,128)S(1)}, f32[72,16,128]{2,1,0:T(8,128)}, u32[]{:S(2)}) copy-start(f32[72,16,128]{2,1,0:T(8,128)} %param.10) | copy-start | bytes 1769476
  18.6 12.7 %collective-permute-start = (bf16[1392,128]{1,0:T(8,128)(2,1)S(1)}, bf16[1392,128]{1,0:T(8,128)(2,1)S(1)}, u32[]{:S(2)}, u32[]{:S(2)}) collective-permute-start(bf16[1392,128]{1,0:T(8,128)(2,1)S(1)} %get-tuple-element.18), channel_id=1, source_target_pairs={{0,1},{1,2},{2,3},{3,4},{4,5},{5,6},{6,7},{7,8},{8,9},{9,10},{10,1... | collective-permute-start | bytes 1069064 | tf_op jit(solution)/shard_map/ppermute | solution.py:527
  20.3 8.6 %collective-permute-start.1 = (bf16[1312,128]{1,0:T(8,128)(2,1)S(1)}, bf16[1312,128]{1,0:T(8,128)(2,1)S(1)}, u32[]{:S(2)}, u32[]{:S(2)}) collective-permute-start(bf16[1312,128]{1,0:T(8,128)(2,1)S(1)} %get-tuple-element.20), channel_id=1, source_target_pairs={{1,0},{2,1},{3,2},{4,3},{5,4},{6,5},{7,6},{8,7},{9,8},{10,9},{11,1... | collective-permute-start | bytes 1007624 | tf_op jit(solution)/shard_map/ppermute | solution.py:528
  28.8 0.7 %copy-start.7 = (bf16[1312,128]{1,0:T(8,128)(2,1)}, bf16[1312,128]{1,0:T(8,128)(2,1)S(1)}, u32[]{:S(2)}) copy-start(bf16[1312,128]{1,0:T(8,128)(2,1)S(1)} %collective-permute-done.1.bwd_hbm) | copy-start | bytes 1007620
  33.9 6.8 %copy-start.5 = (f32[576,1536]{1,0:T(8,128)S(1)}, f32[576,1536]{1,0:T(8,128)}, u32[]{:S(2)}) copy-start(f32[576,1536]{1,0:T(8,128)} %get-tuple-element.26.field_ref) | copy-start | bytes 10616836
  39.8 5.2 %collective-permute-start.2 = (bf16[576,256]{1,0:T(8,128)(2,1)S(1)}, bf16[576,256]{1,0:T(8,128)(2,1)S(1)}, u32[]{:S(2)}, u32[]{:S(2)}) collective-permute-start(bf16[576,256]{1,0:T(8,128)(2,1)S(1)} %get-tuple-element.22.own_e_ref), channel_id=1, source_target_pairs={{0,1},{1,2},{2,3},{3,4},{4,5},{5,6},{6,7},{7,8},{8,9},{9,10},{10,1... | collective-permute-start | bytes 884744 | tf_op jit(solution)/shard_map/ppermute | solution.py:577
  40.7 9.3 %collective-permute-start.3 = (bf16[576,256]{1,0:T(8,128)(2,1)S(1)}, bf16[576,256]{1,0:T(8,128)(2,1)S(1)}, u32[]{:S(2)}, u32[]{:S(2)}) collective-permute-start(bf16[576,256]{1,0:T(8,128)(2,1)S(1)} %get-tuple-element.23.own_w_ref), channel_id=1, source_target_pairs={{1,0},{2,1},{3,2},{4,3},{5,4},{6,5},{7,6},{8,7},{9,8},{10,9},{11,1... | collective-permute-start | bytes 884744 | tf_op jit(solution)/shard_map/ppermute | solution.py:578
  40.7 9.3 %copy-start.6 = (f32[5,72,1792]{2,1,0:T(8,128)S(1)}, f32[5,72,1792]{2,1,0:T(8,128)}, u32[]{:S(2)}) copy-start(f32[5,72,1792]{2,1,0:T(8,128)} %get-tuple-element.17.inner_coef_ref) | copy-start | bytes 7741444

commit v7 on v6

--- a/solution.py
+++ b/solution.py
@@ -10,7 +10,7 @@
 F32 = jnp.float32
 BF16 = jnp.bfloat16
 GROUP = 2
-RIM_TOGETHER = 2
+RIM_TOGETHER = 4
 TOGETHER = 2
 HALO = 2
 VMEM_BYTES = 20 * 1024 * 1024
@@ -42,9 +42,16 @@
 
 
 def pack_kernel(
-    kernel_ref, weight_ref, owner_ref, column_ref, out_ref, *, tiles, capacity, lat, pairs
+    owner_ref, column_ref, kernel_hbm, weight_hbm, out_hbm, kernel_ref, weight_ref, out_ref,
+    in_sems, out_sems, *, tiles, capacity, lat, pairs,
 ):
     levels, pixels = kernel_ref.shape
+    entering = [
+        pltpu.make_async_copy(kernel_hbm, kernel_ref, in_sems.at[0]),
+        pltpu.make_async_copy(weight_hbm, weight_ref, in_sems.at[1]),
+    ]
+    for copy in entering:
+        copy.start()
     column = column_ref[...]
     longitude = column // lat
     line = lax.broadcasted_iota(jnp.int32, (8, pixels), 0)
@@ -53,9 +60,6 @@
         (longitude + 1).astype(F32),
         jnp.where(line == 1, (column % lat).astype(F32), 0.0),
     )
-    payload = jnp.concatenate(
-        [kernel_ref[...].astype(F32), weight_ref[...].astype(F32), place], axis=0
-    ).astype(BF16)
     classes = tiles * pairs
     named = owner_ref[...] * pairs + longitude // HALO
     block = min(256, pixels)
@@ -100,10 +104,21 @@
     ]
     ranks = jnp.concatenate(ranks, axis=1)
     slot = iota((capacity, pixels), 0).astype(F32).astype(BF16)
+    for copy in entering:
+        copy.wait()
+    payload = jnp.concatenate(
+        [kernel_ref[...].astype(F32), weight_ref[...].astype(F32), place], axis=0
+    ).astype(BF16)
+    leaving = []
     for tile in range(tiles):
         rank = stacked(rows16(ranks[tile : tile + 1, :]), capacity // 16)
         chosen = jnp.where(slot == rank, jnp.ones_like(slot), jnp.zeros_like(slot))
         out_ref[tile] = nt_dot(payload, chosen).astype(BF16)
+        copy = pltpu.make_async_copy(out_ref.at[tile], out_hbm.at[tile], out_sems.at[tile])
+        copy.start()
+        leaving.append(copy)
+    for copy in leaving:
+        copy.wait()
 
 
 def both(ref, block, x, lon, levels):
@@ -498,15 +513,23 @@
     height = levels + tracers + 8
     payload = pl.pallas_call(
         functools.partial(pack_kernel, tiles=tiles, capacity=capacity, lat=lat, pairs=pairs),
-        out_specs=here,
-        out_shape=pltpu.VMEM((tiles, height, capacity), BF16),
+        in_specs=[pl.BlockSpec((1, pixels), lambda: (0, 0))] * 2 + [far] * 2,
+        out_specs=far,
+        out_shape=pltpu.HBM((tiles, height, capacity), BF16),
+        scratch_shapes=[
+            pltpu.VMEM((levels, pixels), BF16),
+            pltpu.VMEM((tracers, pixels), BF16),
+            pltpu.VMEM((tiles, height, capacity), BF16),
+            pltpu.SemaphoreType.DMA((2,)),
+            pltpu.SemaphoreType.DMA((tiles,)),
+        ],
         compiler_params=params(),
         name="pack",
     )(
+        away(pixel_owner.reshape(1, pixels)),
+        away(pixel_column),
         away(avg_kernel),
         away(pixel_weight),
-        away(pixel_owner.reshape(1, pixels)),
-        away(pixel_column),
     )
     got = lax.all_to_all(payload, "tile", split_axis=0, concat_axis=0, tiled=True)
 

time: 59.2 us -> 58.6 us (0.990)
  the two profiles are of different devices: /device:TPU:1 before, /device:TPU:0 now
where the time goes in v7:
time: 58.6 us; the launch traced here: 58.9 us
  Pallas kernels  35.4 us (60%)
  starting transfers between devices  16.4 us (28%)
  local copies, waits for them, and re-layouts  5.2 us (9%)
  waiting for transfers between devices  1.55 us (3%)
    pallas_call x1, Pallas kernels, per_device(): pl.pallas_call(functools.partial(inner_kernel, lon=lon, levels=levels), g...  8.77 us
    pallas_call x1, Pallas kernels, per_device(): pl.pallas_call(functools.partial(second_half_kernel, lon=lon, levels=leve...  7.94 us
    all_to_all x1, starting transfers between devices, per_device(): lax.all_to_all(payload, 'tile', split_axis=0, concat_axis=0, tiled=True)  7.4 us
    pallas_call x1, Pallas kernels, per_device(): pl.pallas_call(functools.partial(forcing_inner_kernel, lat=lat), in_specs...  6.77 us
    pallas_call x1, Pallas kernels, per_device(): pl.pallas_call(functools.partial(rim_kernel, lon=lon, levels=levels, trac...  5.46 us
    unnamed x16, local copies, waits for them, and re-layouts  5.2 us
    pallas_call x1, Pallas kernels, per_device(): pl.pallas_call(functools.partial(pack_kernel, tiles=tiles, capacity=capac...  5.06 us
    ppermute x1, starting transfers between devices, per_device(): far_e = lax.ppermute(own_w, 'tile', back)  4.3 us
  transfers between devices with their start and end apart: 5, of which 1 were waited for; matrix products, arithmetic and copies ran while one was open for 0% of the time, Pallas kernels for 29%

profile of v7, /device:TPU:0, one launch (start us, length us, event | category | flops | bytes accessed | tf_op | source)
XLA Modules:
  0.0 58.9 jit_solution(16536939310664143362)
XLA Ops:
  0.0 5.1 %pack.1 = bf16[16,88,256]{2,1,0:T(8,128)(2,1)} custom-call(s32[1,1024]{1,0:T(1,128)} %bitcast.13, s32[1,1024]{1,0:T(1,128)} %column_ref.1, bf16[72,1024]{1,0:T(8,128)(2,1)} %kernel_hbm.1, bf16[8,1024]{1,0:T(8,128)(2,1)} %weight_hbm.1), custom_call_target="tpu_custom_call" | custom-call | tf_op jit(solution)/shard_map/pack/pallas_call | solution.py:514
  5.1 7.4 %all-to-all-start = ((bf16[16,88,256]{2,1,0:T(8,128)(2,1)}), bf16[16,88,256]{2,1,0:T(8,128)(2,1)S(1)}, u32[]{:S(2)}, u32[]{:S(2)}) async-start(bf16[16,88,256]{2,1,0:T(8,128)(2,1)} %pack.1), calls=%async_computation | async-start | bytes 1441792 | tf_op jit(solution)/shard_map/all_to_all | solution.py:534
  12.5 0.0 copy-start
  12.5 2.3 %copy-done = f32[8,72,16,128]{3,2,1,0:T(8,128)S(1)} copy-done((f32[8,72,16,128]{3,2,1,0:T(8,128)S(1)}, f32[8,72,16,128]{3,2,1,0:T(8,128)}, u32[]{:S(2)}) %copy-start) | copy-done | bytes 4718616
  14.8 0.0 copy-start.1
  14.8 1.1 %copy-done.1 = f32[72,16,128]{2,1,0:T(8,128)S(1)} copy-done((f32[72,16,128]{2,1,0:T(8,128)S(1)}, f32[72,16,128]{2,1,0:T(8,128)}, u32[]{:S(2)}) %copy-start.1) | copy-done | bytes 589848
  15.9 0.0 copy-start.3
  15.9 1.1 %copy-done.3 = f32[72,16,128]{2,1,0:T(8,128)S(1)} copy-done((f32[72,16,128]{2,1,0:T(8,128)S(1)}, f32[72,16,128]{2,1,0:T(8,128)}, u32[]{:S(2)}) %copy-start.3) | copy-done | bytes 589848
  16.9 1.4 %edges.1 = (bf16[1392,128]{1,0:T(8,128)(2,1)S(1)}, bf16[1312,128]{1,0:T(8,128)(2,1)S(1)}, bf16[144,144]{1,0:T(8,128)(2,1)S(1)}) custom-call(f32[9216,128]{1,0:T(8,128)S(1)} %bitcast.5, f32[1152,128]{1,0:T(8,128)S(1)} %bitcast.7, f32[1152,128]{1,0:T(8,128)S(1)} %bitcast.10, bf16[72,72]{1,0:T(8,128)(2,1)} %level_mix_ref.1), custom_call_target="tpu_custom_call" | custom-call | tf_op jit(solution)/shard_map/edges/pallas_call | solution.py:538
  18.4 0.0 copy-start.2
  18.4 0.0 copy-start.4
  18.4 0.5 collective-permute-start
  18.9 4.0 %collective-permute-start.1 = (bf16[1312,128]{1,0:T(8,128)(2,1)S(1)}, bf16[1312,128]{1,0:T(8,128)(2,1)S(1)}, u32[]{:S(2)}, u32[]{:S(2)}) collective-permute-start(bf16[1312,128]{1,0:T(8,128)(2,1)S(1)} %get-tuple-element.20), channel_id=1, source_target_pairs={{1,0},{2,1},{3,2},{4,3},{5,4},{6,5},{7,6},{8,7},{9,8},{10,9},{11,1... | collective-permute-start | bytes 1007624 | tf_op jit(solution)/shard_map/ppermute | solution.py:551
  22.9 8.8 %first_half_inner.1 = (f32[576,1536]{1,0:T(8,128)}, bf16[576,1024]{1,0:T(8,128)(2,1)S(1)}, f32[5,72,1792]{2,1,0:T(8,128)}) custom-call(bf16[144,144]{1,0:T(8,128)(2,1)S(1)} %get-tuple-element.16.mix_ref, f32[1152,128]{1,0:T(8,128)S(1)} %bitcast.8, f32[1152,128]{1,0:T(8,128)S(1)} %bitcast.11, f32[9216,128]{1,0:T(8,128)S(1)} %bitcast.6), custom_call_target="tpu_custom_call" | custom-call | tf_op jit(solution)/shard_map/first_half_inner/pallas_call | solution.py:561
  31.7 0.0 collective-permute-done.1.bwd_hbm
  31.7 0.0 copy-start.7
  31.7 0.7 %copy-done.7 = bf16[1312,128]{1,0:T(8,128)(2,1)} copy-done((bf16[1312,128]{1,0:T(8,128)(2,1)}, bf16[1312,128]{1,0:T(8,128)(2,1)S(1)}, u32[]{:S(2)}) %copy-start.7) | copy-done | bytes 335896
  32.4 1.5 %collective-permute-done.fwd_ref = bf16[1392,128]{1,0:T(8,128)(2,1)S(1)} collective-permute-done((bf16[1392,128]{1,0:T(8,128)(2,1)S(1)}, bf16[1392,128]{1,0:T(8,128)(2,1)S(1)}, u32[]{:S(2)}, u32[]{:S(2)}) %collective-permute-start) | collective-permute-done | bytes 356384 | tf_op jit(solution)/shard_map/ppermute | solution.py:550
  34.0 0.0 all-to-all-done.got_ref
  34.0 0.0 copy-start.5
  34.0 0.0 copy-done.2
  34.0 0.0 copy-done.4
  34.0 5.5 %rim.1 = (bf16[576,256]{1,0:T(8,128)(2,1)S(1)}, bf16[576,256]{1,0:T(8,128)(2,1)S(1)}, f32[5,72,1024]{2,1,0:T(8,128)S(1)}, bf16[576,4096]{1,0:T(8,128)(2,1)S(1)}, f32[8,4096]{1,0:T(8,128)S(1)}) custom-call(bf16[144,144]{1,0:T(8,128)(2,1)S(1)} %get-tuple-element.16.mix_ref, f32[1152,128]{1,0:T(8,128)S(1)} %bitcast.9, f32[1152,128]{1,0:T(8,128)S(1)} %bitcast.12, ...), custom_call_target="tpu_custom_call" | custom-call | tf_op jit(solution)/shard_map/rim/pallas_call | solution.py:579
  39.4 0.2 collective-permute-start.2
  39.6 4.3 %collective-permute-start.3 = (bf16[576,256]{1,0:T(8,128)(2,1)S(1)}, bf16[576,256]{1,0:T(8,128)(2,1)S(1)}, u32[]{:S(2)}, u32[]{:S(2)}) collective-permute-start(bf16[576,256]{1,0:T(8,128)(2,1)S(1)} %get-tuple-element.23.own_w_ref), channel_id=1, source_target_pairs={{1,0},{2,1},{3,2},{4,3},{5,4},{6,5},{7,6},{8,7},{9,8},{10,9},{11,1... | collective-permute-start | bytes 884744 | tf_op jit(solution)/shard_map/ppermute | solution.py:601
  43.9 0.0 copy-done.5
  43.9 0.0 copy-start.6
  43.9 6.8 %forcing_inner.1.inner_ref = bf16[576,1536]{1,0:T(8,128)(2,1)S(1)} custom-call(bf16[576,4096]{1,0:T(8,128)(2,1)S(1)} %get-tuple-element.24.weighted_ref, f32[8,4096]{1,0:T(8,128)S(1)} %get-tuple-element.25.place_ref, f32[576,1536]{1,0:T(8,128)S(1)} %copy-done.5), custom_call_target="tpu_custom_call" | custom-call | tf_op jit(solution)/shard_map/forcing_inner/pallas_call | solution.py:602
  50.7 0.0 collective-permute-done.2.far_w_ref
  50.7 0.0 collective-permute-done.3.far_e_ref
  50.7 0.0 copy-done.6
  50.8 7.9 %second_half.1 = f32[9216,128]{1,0:T(8,128)} custom-call(bf16[144,144]{1,0:T(8,128)(2,1)S(1)} %get-tuple-element.16.mix_ref, f32[5,72,1792]{2,1,0:T(8,128)S(1)} %copy-done.6, f32[5,72,1024]{2,1,0:T(8,128)S(1)} %get-tuple-element.21.rim_coef_ref, bf16[576,256]{1,0:T(8,128)(2,1)S(1)} %collective-permute-done.2.far_w_ref, ...), custom_call_target="tpu_custom_call" | custom-call | tf_op jit(solution)/shard_map/second_half/pallas_call | solution.py:612
Async XLA Ops:
  5.1 28.9 %all-to-all-start = ((bf16[16,88,256]{2,1,0:T(8,128)(2,1)}), bf16[16,88,256]{2,1,0:T(8,128)(2,1)S(1)}, u32[]{:S(2)}, u32[]{:S(2)}) async-start(bf16[16,88,256]{2,1,0:T(8,128)(2,1)} %pack.1), calls=%async_computation | async-start | bytes 1441792 | tf_op jit(solution)/shard_map/all_to_all | solution.py:534
  12.5 2.3 %copy-start = (f32[8,72,16,128]{3,2,1,0:T(8,128)S(1)}, f32[8,72,16,128]{3,2,1,0:T(8,128)}, u32[]{:S(2)}) copy-start(f32[8,72,16,128]{3,2,1,0:T(8,128)} %param.8) | copy-start | bytes 14155780
  14.8 1.1 %copy-start.1 = (f32[72,16,128]{2,1,0:T(8,128)S(1)}, f32[72,16,128]{2,1,0:T(8,128)}, u32[]{:S(2)}) copy-start(f32[72,16,128]{2,1,0:T(8,128)} %param.9) | copy-start | bytes 1769476
  15.9 1.1 %copy-start.3 = (f32[72,16,128]{2,1,0:T(8,128)S(1)}, f32[72,16,128]{2,1,0:T(8,128)}, u32[]{:S(2)}) copy-start(f32[72,16,128]{2,1,0:T(8,128)} %param.10) | copy-start | bytes 1769476
  18.4 15.6 %copy-start.2 = (f32[72,16,128]{2,1,0:T(8,128)S(1)}, f32[72,16,128]{2,1,0:T(8,128)}, u32[]{:S(2)}) copy-start(f32[72,16,128]{2,1,0:T(8,128)} %param.9) | copy-start | bytes 1769476
  18.4 15.6 %copy-start.4 = (f32[72,16,128]{2,1,0:T(8,128)S(1)}, f32[72,16,128]{2,1,0:T(8,128)}, u32[]{:S(2)}) copy-start(f32[72,16,128]{2,1,0:T(8,128)} %param.10) | copy-start | bytes 1769476
  18.4 15.5 %collective-permute-start = (bf16[1392,128]{1,0:T(8,128)(2,1)S(1)}, bf16[1392,128]{1,0:T(8,128)(2,1)S(1)}, u32[]{:S(2)}, u32[]{:S(2)}) collective-permute-start(bf16[1392,128]{1,0:T(8,128)(2,1)S(1)} %get-tuple-element.18), channel_id=1, source_target_pairs={{0,1},{1,2},{2,3},{3,4},{4,5},{5,6},{6,7},{7,8},{8,9},{9,10},{10,1... | collective-permute-start | bytes 1069064 | tf_op jit(solution)/shard_map/ppermute | solution.py:550
  18.9 12.8 %collective-permute-start.1 = (bf16[1312,128]{1,0:T(8,128)(2,1)S(1)}, bf16[1312,128]{1,0:T(8,128)(2,1)S(1)}, u32[]{:S(2)}, u32[]{:S(2)}) collective-permute-start(bf16[1312,128]{1,0:T(8,128)(2,1)S(1)} %get-tuple-element.20), channel_id=1, source_target_pairs={{1,0},{2,1},{3,2},{4,3},{5,4},{6,5},{7,6},{8,7},{9,8},{10,9},{11,1... | collective-permute-start | bytes 1007624 | tf_op jit(solution)/shard_map/ppermute | solution.py:551
  31.7 0.7 %copy-start.7 = (bf16[1312,128]{1,0:T(8,128)(2,1)}, bf16[1312,128]{1,0:T(8,128)(2,1)S(1)}, u32[]{:S(2)}) copy-start(bf16[1312,128]{1,0:T(8,128)(2,1)S(1)} %collective-permute-done.1.bwd_hbm) | copy-start | bytes 1007620
  34.0 10.0 %copy-start.5 = (f32[576,1536]{1,0:T(8,128)S(1)}, f32[576,1536]{1,0:T(8,128)}, u32[]{:S(2)}) copy-start(f32[576,1536]{1,0:T(8,128)} %get-tuple-element.26.field_ref) | copy-start | bytes 10616836
  39.4 11.3 %collective-permute-start.2 = (bf16[576,256]{1,0:T(8,128)(2,1)S(1)}, bf16[576,256]{1,0:T(8,128)(2,1)S(1)}, u32[]{:S(2)}, u32[]{:S(2)}) collective-permute-start(bf16[576,256]{1,0:T(8,128)(2,1)S(1)} %get-tuple-element.22.own_e_ref), channel_id=1, source_target_pairs={{0,1},{1,2},{2,3},{3,4},{4,5},{5,6},{6,7},{7,8},{8,9},{9,10},{10,1... | collective-permute-start | bytes 884744 | tf_op jit(solution)/shard_map/ppermute | solution.py:600
  39.6 11.1 %collective-permute-start.3 = (bf16[576,256]{1,0:T(8,128)(2,1)S(1)}, bf16[576,256]{1,0:T(8,128)(2,1)S(1)}, u32[]{:S(2)}, u32[]{:S(2)}) collective-permute-start(bf16[576,256]{1,0:T(8,128)(2,1)S(1)} %get-tuple-element.23.own_w_ref), channel_id=1, source_target_pairs={{1,0},{2,1},{3,2},{4,3},{5,4},{6,5},{7,6},{8,7},{9,8},{10,9},{11,1... | collective-permute-start | bytes 884744 | tf_op jit(solution)/shard_map/ppermute | solution.py:601
  43.9 6.8 %copy-start.6 = (f32[5,72,1792]{2,1,0:T(8,128)S(1)}, f32[5,72,1792]{2,1,0:T(8,128)}, u32[]{:S(2)}) copy-start(f32[5,72,1792]{2,1,0:T(8,128)} %get-tuple-element.17.inner_coef_ref) | copy-start | bytes 7741444

commit v8 on v7

--- a/solution.py
+++ b/solution.py
@@ -199,7 +199,7 @@
         coef_ref[4, :, at] = -to_south
 
 
-def stencil(mixed_ref, coef, start, count, lat, levels, emit):
+def stencil(mixed_ref, coef, start, count, lat, levels, emit, after=None):
     def column(e):
         return slice(e * lat, (e + 1) * lat)
 
@@ -221,9 +221,11 @@
                 values.append(value + factor[4] * pltpu.roll(centre[t], 1, 1))
                 left[t], centre[t] = centre[t], right
             emit(block, e, values)
-
-
-def two_steps(mix_ref, levels, lat, segments):
+        if after is not None:
+            after(block)
+
+
+def two_steps(mix_ref, levels, lat, segments, afters=None):
     def mix(field_ref, mixed_ref, lo, hi):
         for e in range(lo, hi, 2):
             at = slice(e * lat, (e + 2) * lat)
@@ -240,8 +242,9 @@
         stencil(mixed_ref, coef, start + 1, count - 2, lat, levels, keep)
     for field_ref, mixed_ref, _, start, count, _ in segments:
         mix(field_ref, mixed_ref, start + 1, start + count - 1)
-    for field_ref, mixed_ref, coef, start, count, put in segments:
-        stencil(mixed_ref, coef, start + 2, count - 4, lat, levels, put)
+    for i, (field_ref, mixed_ref, coef, start, count, put) in enumerate(segments):
+        after = afters[i] if afters else None
+        stencil(mixed_ref, coef, start + 2, count - 4, lat, levels, put, after)
 
 
 def factors(coef_ref, lat, place_of):
@@ -363,9 +366,21 @@
             ref, place = rim_coef_ref, x - (lon - HALO - 1) + 2 * HALO
         return ref[j, lines, place * lat : (place + 1) * lat]
 
-    def leave(group):
-        at = pl.ds(pl.multiple_of(group * rows * lon, 16), rows * lon)
-        return pltpu.make_async_copy(result_ref.at[at, :], out_hbm.at[at, :], out_sems.at[group])
+    blocks = levels // 8
+    chunk = 3 if blocks % 3 == 0 else blocks
+    size = chunk * 8 * lon
+
+    def leave(group, part):
+        copies = []
+        for t in range(GROUP):
+            first = group * rows * lon + t * levels * lon + part * size
+            at = pl.ds(pl.multiple_of(first, 16), size)
+            copies.append(
+                pltpu.make_async_copy(
+                    result_ref.at[at, :], out_hbm.at[at, :], out_sems.at[group, part, t]
+                )
+            )
+        return copies
 
     together = field_ref.shape[0]
 
@@ -389,14 +404,24 @@
 
     def groups_of(i, carry):
         mine = [i * together + slot for slot in range(together)]
-        two_steps(mix_ref, levels, lat, [segment(group, slot) for slot, group in enumerate(mine)])
-        for group in mine:
-            leave(group).start()
+
+        def leaver(group):
+            def after(block):
+                if (block + 1) % chunk == 0:
+                    for copy in leave(group, block // chunk):
+                        copy.start()
+
+            return after
+
+        segments = [segment(group, slot) for slot, group in enumerate(mine)]
+        two_steps(mix_ref, levels, lat, segments, [leaver(group) for group in mine])
         return carry
 
     lax.fori_loop(0, groups // together, groups_of, 0)
     for group in range(groups):
-        leave(group).wait()
+        for part in range(blocks // chunk):
+            for copy in leave(group, part):
+                copy.wait()
 
 
 def regions_of(capacity):
@@ -615,7 +640,7 @@
         out_specs=far,
         out_shape=jax.ShapeDtypeStruct((total * lon, lat), F32),
         scratch_shapes=scratch(lon + 2 * HALO, TOGETHER)
-        + [pltpu.VMEM((total * lon, lat), F32), pltpu.SemaphoreType.DMA((steps,))],
+        + [pltpu.VMEM((total * lon, lat), F32), pltpu.SemaphoreType.DMA((steps, levels // 8, GROUP))],
         compiler_params=params(),
         name="second_half",
     )(*near_by(mix, inner_coef, rim_coef, far_w, own_w, inner, own_e, far_e))

time: 58.6 us -> 57.8 us (0.986)
  the two profiles are of different devices: /device:TPU:0 before, /device:TPU:1 now
where the time goes in v8:
time: 57.8 us; the launch traced here: 57.4 us
  Pallas kernels  32.3 us (56%)
  starting transfers between devices  9.97 us (17%)
  waiting for transfers between devices  9.63 us (17%)
  local copies, waits for them, and re-layouts  5.2 us (9%)
    pallas_call x1, Pallas kernels, per_device(): pl.pallas_call(functools.partial(inner_kernel, lon=lon, levels=levels), g...  8.77 us
    pallas_call x1, Pallas kernels, per_device(): pl.pallas_call(functools.partial(second_half_kernel, lon=lon, levels=leve...  7.85 us
    all_to_all x1, starting transfers between devices, per_device(): lax.all_to_all(payload, 'tile', split_axis=0, concat_axis=0, tiled=True)  7.36 us
    ppermute x1, waiting for transfers between devices, per_device(): far_e = lax.ppermute(own_w, 'tile', back)  5.52 us
    pallas_call x1, Pallas kernels, per_device(): pl.pallas_call(functools.partial(rim_kernel, lon=lon, levels=levels, trac...  5.46 us
    unnamed x16, local copies, waits for them, and re-layouts  5.2 us
    pallas_call x1, Pallas kernels, per_device(): pl.pallas_call(functools.partial(pack_kernel, tiles=tiles, capacity=capac...  5.07 us
    pallas_call x1, Pallas kernels, per_device(): pl.pallas_call(functools.partial(forcing_inner_kernel, lat=lat), in_specs...  3.76 us
  transfers between devices with their start and end apart: 5, of which 3 were waited for; matrix products, arithmetic and copies ran while one was open for 0% of the time, Pallas kernels for 24%

profile of v8, /device:TPU:1, one launch (start us, length us, event | category | flops | bytes accessed | tf_op | source)
XLA Modules:
  0.0 57.4 jit_solution(326036746629876068)
XLA Ops:
  0.0 5.1 %pack.1 = bf16[16,88,256]{2,1,0:T(8,128)(2,1)} custom-call(s32[1,1024]{1,0:T(1,128)} %bitcast.13, s32[1,1024]{1,0:T(1,128)} %column_ref.1, bf16[72,1024]{1,0:T(8,128)(2,1)} %kernel_hbm.1, bf16[8,1024]{1,0:T(8,128)(2,1)} %weight_hbm.1), custom_call_target="tpu_custom_call" | custom-call | tf_op jit(solution)/shard_map/pack/pallas_call | solution.py:539
  5.1 7.4 %all-to-all-start = ((bf16[16,88,256]{2,1,0:T(8,128)(2,1)}), bf16[16,88,256]{2,1,0:T(8,128)(2,1)S(1)}, u32[]{:S(2)}, u32[]{:S(2)}) async-start(bf16[16,88,256]{2,1,0:T(8,128)(2,1)} %pack.1), calls=%async_computation | async-start | bytes 1441792 | tf_op jit(solution)/shard_map/all_to_all | solution.py:559
  12.4 0.0 copy-start
  12.4 2.3 %copy-done = f32[8,72,16,128]{3,2,1,0:T(8,128)S(1)} copy-done((f32[8,72,16,128]{3,2,1,0:T(8,128)S(1)}, f32[8,72,16,128]{3,2,1,0:T(8,128)}, u32[]{:S(2)}) %copy-start) | copy-done | bytes 4718616
  14.8 0.0 copy-start.1
  14.8 1.1 %copy-done.1 = f32[72,16,128]{2,1,0:T(8,128)S(1)} copy-done((f32[72,16,128]{2,1,0:T(8,128)S(1)}, f32[72,16,128]{2,1,0:T(8,128)}, u32[]{:S(2)}) %copy-start.1) | copy-done | bytes 589848
  15.8 0.0 copy-start.3
  15.8 1.1 %copy-done.3 = f32[72,16,128]{2,1,0:T(8,128)S(1)} copy-done((f32[72,16,128]{2,1,0:T(8,128)S(1)}, f32[72,16,128]{2,1,0:T(8,128)}, u32[]{:S(2)}) %copy-start.3) | copy-done | bytes 589848
  16.9 1.4 %edges.1 = (bf16[1392,128]{1,0:T(8,128)(2,1)S(1)}, bf16[1312,128]{1,0:T(8,128)(2,1)S(1)}, bf16[144,144]{1,0:T(8,128)(2,1)S(1)}) custom-call(f32[9216,128]{1,0:T(8,128)S(1)} %bitcast.5, f32[1152,128]{1,0:T(8,128)S(1)} %bitcast.7, f32[1152,128]{1,0:T(8,128)S(1)} %bitcast.10, bf16[72,72]{1,0:T(8,128)(2,1)} %level_mix_ref.1), custom_call_target="tpu_custom_call" | custom-call | tf_op jit(solution)/shard_map/edges/pallas_call | solution.py:563
  18.3 0.0 copy-start.2
  18.3 0.0 copy-start.4
  18.4 1.7 %collective-permute-start = (bf16[1392,128]{1,0:T(8,128)(2,1)S(1)}, bf16[1392,128]{1,0:T(8,128)(2,1)S(1)}, u32[]{:S(2)}, u32[]{:S(2)}) collective-permute-start(bf16[1392,128]{1,0:T(8,128)(2,1)S(1)} %get-tuple-element.18), channel_id=1, source_target_pairs={{0,1},{1,2},{2,3},{3,4},{4,5},{5,6},{6,7},{7,8},{8,9},{9,10},{10,1... | collective-permute-start | bytes 1069064 | tf_op jit(solution)/shard_map/ppermute | solution.py:575
  20.0 0.0 collective-permute-start.1
  20.0 8.8 %first_half_inner.1 = (f32[576,1536]{1,0:T(8,128)}, bf16[576,1024]{1,0:T(8,128)(2,1)S(1)}, f32[5,72,1792]{2,1,0:T(8,128)}) custom-call(bf16[144,144]{1,0:T(8,128)(2,1)S(1)} %get-tuple-element.16.mix_ref, f32[1152,128]{1,0:T(8,128)S(1)} %bitcast.8, f32[1152,128]{1,0:T(8,128)S(1)} %bitcast.11, f32[9216,128]{1,0:T(8,128)S(1)} %bitcast.6), custom_call_target="tpu_custom_call" | custom-call | tf_op jit(solution)/shard_map/first_half_inner/pallas_call | solution.py:586
  28.8 0.0 collective-permute-done.1.bwd_hbm
  28.8 0.0 copy-start.7
  28.8 0.7 %copy-done.7 = bf16[1312,128]{1,0:T(8,128)(2,1)} copy-done((bf16[1312,128]{1,0:T(8,128)(2,1)}, bf16[1312,128]{1,0:T(8,128)(2,1)S(1)}, u32[]{:S(2)}) %copy-start.7) | copy-done | bytes 335896
  29.6 1.5 %collective-permute-done.fwd_ref = bf16[1392,128]{1,0:T(8,128)(2,1)S(1)} collective-permute-done((bf16[1392,128]{1,0:T(8,128)(2,1)S(1)}, bf16[1392,128]{1,0:T(8,128)(2,1)S(1)}, u32[]{:S(2)}, u32[]{:S(2)}) %collective-permute-start) | collective-permute-done | bytes 356384 | tf_op jit(solution)/shard_map/ppermute | solution.py:575
  31.1 2.6 %all-to-all-done.got_ref = bf16[16,88,256]{2,1,0:T(8,128)(2,1)S(1)} async-done(((bf16[16,88,256]{2,1,0:T(8,128)(2,1)}), bf16[16,88,256]{2,1,0:T(8,128)(2,1)S(1)}, u32[]{:S(2)}, u32[]{:S(2)}) %all-to-all-start) | async-done | bytes 720928 | tf_op jit(solution)/shard_map/all_to_all | solution.py:559
  33.7 0.0 copy-start.5
  33.7 0.0 copy-done.2
  33.7 0.0 copy-done.4
  33.7 5.5 %rim.1 = (bf16[576,256]{1,0:T(8,128)(2,1)S(1)}, bf16[576,256]{1,0:T(8,128)(2,1)S(1)}, f32[5,72,1024]{2,1,0:T(8,128)S(1)}, bf16[576,4096]{1,0:T(8,128)(2,1)S(1)}, f32[8,4096]{1,0:T(8,128)S(1)}) custom-call(bf16[144,144]{1,0:T(8,128)(2,1)S(1)} %get-tuple-element.16.mix_ref, f32[1152,128]{1,0:T(8,128)S(1)} %bitcast.9, f32[1152,128]{1,0:T(8,128)S(1)} %bitcast.12, ...), custom_call_target="tpu_custom_call" | custom-call | tf_op jit(solution)/shard_map/rim/pallas_call | solution.py:604
  39.1 0.9 %collective-permute-start.2 = (bf16[576,256]{1,0:T(8,128)(2,1)S(1)}, bf16[576,256]{1,0:T(8,128)(2,1)S(1)}, u32[]{:S(2)}, u32[]{:S(2)}) collective-permute-start(bf16[576,256]{1,0:T(8,128)(2,1)S(1)} %get-tuple-element.22.own_e_ref), channel_id=1, source_target_pairs={{0,1},{1,2},{2,3},{3,4},{4,5},{5,6},{6,7},{7,8},{8,9},{9,10},{10,1... | collective-permute-start | bytes 884744 | tf_op jit(solution)/shard_map/ppermute | solution.py:625
  40.1 0.0 collective-permute-start.3
  40.1 0.0 copy-done.5
  40.1 0.0 copy-start.6
  40.1 3.8 %forcing_inner.1.inner_ref = bf16[576,1536]{1,0:T(8,128)(2,1)S(1)} custom-call(bf16[576,4096]{1,0:T(8,128)(2,1)S(1)} %get-tuple-element.24.weighted_ref, f32[8,4096]{1,0:T(8,128)S(1)} %get-tuple-element.25.place_ref, f32[576,1536]{1,0:T(8,128)S(1)} %copy-done.5), custom_call_target="tpu_custom_call" | custom-call | tf_op jit(solution)/shard_map/forcing_inner/pallas_call | solution.py:627
  43.8 0.0 collective-permute-done.2.far_w_ref
  43.9 5.5 %collective-permute-done.3.far_e_ref = bf16[576,256]{1,0:T(8,128)(2,1)S(1)} collective-permute-done((bf16[576,256]{1,0:T(8,128)(2,1)S(1)}, bf16[576,256]{1,0:T(8,128)(2,1)S(1)}, u32[]{:S(2)}, u32[]{:S(2)}) %collective-permute-start.3) | collective-permute-done | bytes 294944 | tf_op jit(solution)/shard_map/ppermute | solution.py:626
  49.4 0.0 copy-done.6
  49.4 7.9 %second_half.1 = f32[9216,128]{1,0:T(8,128)} custom-call(bf16[144,144]{1,0:T(8,128)(2,1)S(1)} %get-tuple-element.16.mix_ref, f32[5,72,1792]{2,1,0:T(8,128)S(1)} %copy-done.6, f32[5,72,1024]{2,1,0:T(8,128)S(1)} %get-tuple-element.21.rim_coef_ref, bf16[576,256]{1,0:T(8,128)(2,1)S(1)} %collective-permute-done.2.far_w_ref, ...), custom_call_target="tpu_custom_call" | custom-call | tf_op jit(solution)/shard_map/second_half/pallas_call | solution.py:637
Async XLA Ops:
  5.1 28.6 %all-to-all-start = ((bf16[16,88,256]{2,1,0:T(8,128)(2,1)}), bf16[16,88,256]{2,1,0:T(8,128)(2,1)S(1)}, u32[]{:S(2)}, u32[]{:S(2)}) async-start(bf16[16,88,256]{2,1,0:T(8,128)(2,1)} %pack.1), calls=%async_computation | async-start | bytes 1441792 | tf_op jit(solution)/shard_map/all_to_all | solution.py:559
  12.4 2.3 %copy-start = (f32[8,72,16,128]{3,2,1,0:T(8,128)S(1)}, f32[8,72,16,128]{3,2,1,0:T(8,128)}, u32[]{:S(2)}) copy-start(f32[8,72,16,128]{3,2,1,0:T(8,128)} %param.8) | copy-start | bytes 14155780
  14.8 1.1 %copy-start.1 = (f32[72,16,128]{2,1,0:T(8,128)S(1)}, f32[72,16,128]{2,1,0:T(8,128)}, u32[]{:S(2)}) copy-start(f32[72,16,128]{2,1,0:T(8,128)} %param.9) | copy-start | bytes 1769476
  15.8 1.1 %copy-start.3 = (f32[72,16,128]{2,1,0:T(8,128)S(1)}, f32[72,16,128]{2,1,0:T(8,128)}, u32[]{:S(2)}) copy-start(f32[72,16,128]{2,1,0:T(8,128)} %param.10) | copy-start | bytes 1769476
  18.3 15.3 %copy-start.2 = (f32[72,16,128]{2,1,0:T(8,128)S(1)}, f32[72,16,128]{2,1,0:T(8,128)}, u32[]{:S(2)}) copy-start(f32[72,16,128]{2,1,0:T(8,128)} %param.9) | copy-start | bytes 1769476
  18.3 15.3 %copy-start.4 = (f32[72,16,128]{2,1,0:T(8,128)S(1)}, f32[72,16,128]{2,1,0:T(8,128)}, u32[]{:S(2)}) copy-start(f32[72,16,128]{2,1,0:T(8,128)} %param.10) | copy-start | bytes 1769476
  18.4 12.7 %collective-permute-start = (bf16[1392,128]{1,0:T(8,128)(2,1)S(1)}, bf16[1392,128]{1,0:T(8,128)(2,1)S(1)}, u32[]{:S(2)}, u32[]{:S(2)}) collective-permute-start(bf16[1392,128]{1,0:T(8,128)(2,1)S(1)} %get-tuple-element.18), channel_id=1, source_target_pairs={{0,1},{1,2},{2,3},{3,4},{4,5},{5,6},{6,7},{7,8},{8,9},{9,10},{10,1... | collective-permute-start | bytes 1069064 | tf_op jit(solution)/shard_map/ppermute | solution.py:575
  20.0 8.8 %collective-permute-start.1 = (bf16[1312,128]{1,0:T(8,128)(2,1)S(1)}, bf16[1312,128]{1,0:T(8,128)(2,1)S(1)}, u32[]{:S(2)}, u32[]{:S(2)}) collective-permute-start(bf16[1312,128]{1,0:T(8,128)(2,1)S(1)} %get-tuple-element.20), channel_id=1, source_target_pairs={{1,0},{2,1},{3,2},{4,3},{5,4},{6,5},{7,6},{8,7},{9,8},{10,9},{11,1... | collective-permute-start | bytes 1007624 | tf_op jit(solution)/shard_map/ppermute | solution.py:576
  28.8 0.7 %copy-start.7 = (bf16[1312,128]{1,0:T(8,128)(2,1)}, bf16[1312,128]{1,0:T(8,128)(2,1)S(1)}, u32[]{:S(2)}) copy-start(bf16[1312,128]{1,0:T(8,128)(2,1)S(1)} %collective-permute-done.1.bwd_hbm) | copy-start | bytes 1007620
  33.7 6.4 %copy-start.5 = (f32[576,1536]{1,0:T(8,128)S(1)}, f32[576,1536]{1,0:T(8,128)}, u32[]{:S(2)}) copy-start(f32[576,1536]{1,0:T(8,128)} %get-tuple-element.26.field_ref) | copy-start | bytes 10616836
  39.1 4.7 %collective-permute-start.2 = (bf16[576,256]{1,0:T(8,128)(2,1)S(1)}, bf16[576,256]{1,0:T(8,128)(2,1)S(1)}, u32[]{:S(2)}, u32[]{:S(2)}) collective-permute-start(bf16[576,256]{1,0:T(8,128)(2,1)S(1)} %get-tuple-element.22.own_e_ref), channel_id=1, source_target_pairs={{0,1},{1,2},{2,3},{3,4},{4,5},{5,6},{6,7},{7,8},{8,9},{9,10},{10,1... | collective-permute-start | bytes 884744 | tf_op jit(solution)/shard_map/ppermute | solution.py:625
  40.1 9.3 %collective-permute-start.3 = (bf16[576,256]{1,0:T(8,128)(2,1)S(1)}, bf16[576,256]{1,0:T(8,128)(2,1)S(1)}, u32[]{:S(2)}, u32[]{:S(2)}) collective-permute-start(bf16[576,256]{1,0:T(8,128)(2,1)S(1)} %get-tuple-element.23.own_w_ref), channel_id=1, source_target_pairs={{1,0},{2,1},{3,2},{4,3},{5,4},{6,5},{7,6},{8,7},{9,8},{10,9},{11,1... | collective-permute-start | bytes 884744 | tf_op jit(solution)/shard_map/ppermute | solution.py:626
  40.1 9.3 %copy-start.6 = (f32[5,72,1792]{2,1,0:T(8,128)S(1)}, f32[5,72,1792]{2,1,0:T(8,128)}, u32[]{:S(2)}) copy-start(f32[5,72,1792]{2,1,0:T(8,128)} %get-tuple-element.17.inner_coef_ref) | copy-start | bytes 7741444
